TPU v7x, 32 devices: a whole 2x2x4 slice. The times are simulated.
32 devices in a mesh: dp: 2 (over core), expert: 16 (over z, y, x).
Axes of the slice: x: 2, y: 2, z: 4, core: 2. Of those that a mesh axis runs over, the one named last changes fastest.
Arguments:
- tokens: bfloat16 [4096, 2048], P(('dp', 'expert')), may hold values from -6 to 6
- cotangent: bfloat16 [4096, 2048], P(('dp', 'expert')), may hold values from -3 to 3
- experts: int32 [4096, 4], P(('dp', 'expert')), may hold values from 0 to 15, as said below
- mixing: float32 [4096, 4], P(('dp', 'expert')), may hold values from 0.1 to 0.9
- gate_matrix: bfloat16 [16, 2048, 768], P('expert'), may hold values from -0.125 to 0.125
- up_matrix: bfloat16 [16, 2048, 768], P('expert'), may hold values from -0.125 to 0.125
- down_matrix: bfloat16 [16, 768, 2048], P('expert'), may hold values from -0.21875 to 0.21875
Outputs:
- input_grad: bfloat16 [4096, 2048], P(('dp', 'expert'))
- gate_grad: float32 [16, 2048, 768], P('expert', 'dp')
- up_grad: float32 [16, 2048, 768], P('expert', 'dp')
- down_grad: float32 [16, 768, 2048], P('expert', 'dp')
Inputs may be any that keep to these rules, and one draw needn't show every extreme that they name: A token names 4 different experts. Among the 128 tokens of one device, expert e and expert (e + 8) mod 16 are named together exactly 2 * 32 times, no expert more than 64 times, and one expert is named exactly 64 times by the tokens of every device.
All inputs are finite; a program needn't handle non-finite values.
Results may differ from a plain program's by a relative error of at most 0.0065.
Values may be sent and summed in bfloat16 or wider, within the bound.
No kernel may reach another device: no remote copies, remote signals or barrier semaphores. Data moves between devices by JAX's collectives and lax.ppermute only.
A program may use at most 128 MiB of HBM per device.

v0:
```python
import functools

import jax
import jax.numpy as jnp
from jax import lax
from jax.experimental import pallas as pl
from jax.experimental.pallas import tpu as pltpu
from jax.sharding import PartitionSpec as P

BF16 = jnp.bfloat16
F32 = jnp.float32
META = 16
PARAMS = pltpu.CompilerParams(vmem_limit_bytes=8 << 20)
LARGE = pltpu.CompilerParams(vmem_limit_bytes=15 << 20)
VMEM = pl.BlockSpec(memory_space=pltpu.VMEM)
SMEM = pl.BlockSpec(memory_space=pltpu.SMEM)
ANYWHERE = pl.BlockSpec(memory_space=pl.ANY)
HBM = pl.BlockSpec(memory_space=pltpu.HBM)


def estimate(flops):
    return pl.CostEstimate(flops=flops, transcendentals=0, bytes_accessed=1)


def dot(left, right, dims=((1,), (0,))):
    return lax.dot_general(left, right, (dims, ((), ())), preferred_element_type=F32)


def array(shape, dtype=BF16):
    return jax.ShapeDtypeStruct(shape, dtype)


def in_hbm(*values):
    return [pltpu.with_memory_space_constraint(value, pltpu.HBM) for value in values]


def in_vmem(*values):
    return [pltpu.with_memory_space_constraint(value, pltpu.VMEM) for value in values]


def resident(*shape, dtype=BF16):
    return pltpu.VMEM(shape, dtype)


def pack_kernel(in_ref, experts_ref, mixing_ref, out_ref, block_ref, sems):
    tokens, model = in_ref.shape
    rows = pltpu.make_async_copy(in_ref, out_ref.at[:tokens], sems.at[0])
    rows.start()
    mixing = mixing_ref[...]
    high = mixing.astype(BF16).astype(F32)
    middle = (mixing - high).astype(BF16).astype(F32)
    low = mixing - high - middle
    block = [experts_ref[...].astype(F32), high, middle, low]
    if META > 4 * mixing.shape[0]:
        block.append(jnp.zeros((META - 4 * mixing.shape[0], tokens), F32))
    block_ref[:, :tokens] = jnp.concatenate(block, axis=0).astype(BF16)
    block_ref[:, tokens:] = jnp.zeros((META, model - tokens), BF16)
    routing = pltpu.make_async_copy(block_ref, out_ref.at[tokens:], sems.at[1])
    routing.start()
    rows.wait()
    routing.wait()


def pack(tokens, experts, mixing, flops=1):
    rows, model = tokens.shape
    return pl.pallas_call(
        pack_kernel,
        out_shape=array((rows + META, model)),
        in_specs=[HBM, VMEM, VMEM],
        out_specs=HBM,
        scratch_shapes=[pltpu.VMEM((META, model), BF16), pltpu.SemaphoreType.DMA((2,))],
        compiler_params=PARAMS,
        cost_estimate=estimate(flops),
        name="pack",
    )(*in_hbm(tokens), experts.T, mixing.T)


def slot_masks(ids_ref, block, count, cap, top):
    block = block.astype(F32)
    chosen, high, middle, low = (block[top * part : top * (part + 1)] for part in range(4))
    mixing = (high + middle) + low
    tokens = chosen.shape[1]
    earlier = lax.broadcasted_iota(jnp.int32, (tokens, tokens), 0)
    later = lax.broadcasted_iota(jnp.int32, (tokens, tokens), 1)
    before = (earlier < later).astype(F32)
    slot = lax.broadcasted_iota(jnp.int32, (cap, tokens), 0).astype(F32)
    named, weights = [], []
    for which in range(count):
        hit = chosen == ids_ref[which].astype(F32)
        named.append(jnp.sum(jnp.where(hit, 1.0, 0.0), axis=0, keepdims=True))
        weights.append(jnp.sum(jnp.where(hit, mixing, 0.0), axis=0, keepdims=True))
    position = dot(jnp.concatenate(named, axis=0), before)
    onehot, slot_weight = [], []
    for which in range(count):
        here = (slot == position[which : which + 1]) & (named[which] > 0.5)
        onehot.append(jnp.where(here, 1.0, 0.0))
        slot_weight.append(jnp.sum(jnp.where(here, weights[which], 0.0), axis=1, keepdims=True))
    return jnp.concatenate(onehot, axis=0), jnp.concatenate(slot_weight, axis=0)


def select_kernel(count, cap, top, parts, copied, ids_ref, *refs):
    packed_ref, cots_ref = refs[:2]
    sources = refs[2 : 2 + copied]
    targets, sems = refs[-1 - copied : -1], refs[-1]
    outs = refs[-1 - copied - count : -1 - copied]
    copies = [
        pltpu.make_async_copy(source, target, sems.at[which])
        for which, (source, target) in enumerate(zip(sources, targets))
    ]
    for copy in copies:
        copy.start()
    model = packed_ref.shape[1]
    tokens = packed_ref.shape[0] - META
    masks, weight = slot_masks(ids_ref, packed_ref[tokens:, :tokens], count, cap, top)
    onehot = masks.astype(BF16)
    step = min(512, model)
    for start in range(0, model, step):
        columns = slice(start, start + step)
        for place, part in enumerate(parts):
            if part == "rows":
                value = dot(onehot, packed_ref[:tokens, columns])
            else:
                value = dot(onehot, cots_ref[:, columns]) * weight
            value = value.astype(BF16)
            for which in range(count):
                outs[which][place, :, columns] = value[which * cap : (which + 1) * cap]
    for copy in copies:
        copy.wait()


def select(ids, packed, cots, cap, top, parts, copied, flops, after):
    count = ids.shape[0] - 2
    model = packed.shape[1]
    result = pl.pallas_call(
        functools.partial(select_kernel, count, cap, top, parts, len(copied)),
        out_shape=[array((len(parts), cap, model))] * count
        + [array(value.shape) for value in copied],
        in_specs=[SMEM, VMEM, VMEM if "cots" in parts else ANYWHERE]
        + [ANYWHERE] * (len(copied) + len(after)),
        out_specs=[VMEM] * count + [HBM] * len(copied),
        scratch_shapes=[pltpu.SemaphoreType.DMA((max(1, len(copied)),))],
        compiler_params=PARAMS,
        cost_estimate=estimate(flops),
        name="select",
    )(ids, packed, cots, *copied, *after)
    return result[:count], result[count:]


def flip_kernel(gate_in, up_in, down_in, _, gate_ref, up_ref, both_ref, flipped_ref, down, sems):
    copies = [
        pltpu.make_async_copy(source, target, sems.at[which])
        for which, (source, target) in enumerate(
            ((gate_in, gate_ref), (up_in, up_ref), (down_in, down))
        )
    ]
    for copy in copies:
        copy.start()
    model, units = gate_ref.shape
    step = min(512, model)
    for which, source in enumerate((gate_ref, up_ref)):
        copies[which].wait()
        for start in range(0, model, step):
            both_ref[which * units : (which + 1) * units, start : start + step] = source[
                start : start + step, :
            ].T
    copies[2].wait()
    for start in range(0, model, step):
        flipped_ref[start : start + step, :] = down[:, start : start + step].T


def flip(weight_gate, weight_up, weight_down, flops, after):
    model, units = weight_gate.shape
    return pl.pallas_call(
        flip_kernel,
        in_specs=[HBM] * 3 + [ANYWHERE],
        out_specs=[VMEM] * 4,
        out_shape=[
            resident(model, units),
            resident(model, units),
            resident(2 * units, model),
            resident(model, units),
        ],
        scratch_shapes=[pltpu.VMEM((units, model), BF16), pltpu.SemaphoreType.DMA((3,))],
        compiler_params=PARAMS,
        cost_estimate=estimate(flops),
        name="flip",
    )(*in_hbm(weight_gate, weight_up, weight_down), after)


def begin_kernel(count, *refs):
    ins = refs[:count]
    gate_ref, up_ref = refs[count : count + 2]
    rows_ref, pre_gate_ref, pre_up_ref = refs[-3:]
    cap = ins[0].shape[1]
    for which in range(count):
        rows_ref[which * cap : (which + 1) * cap, :] = ins[which][0]
    pre_gate_ref[...] = dot(rows_ref[...], gate_ref[...])
    pre_up_ref[...] = dot(rows_ref[...], up_ref[...])


def begin(arrived, weights, flops, after):
    count = len(arrived)
    _, cap, model = arrived[0].shape
    units = weights[0].shape[1]
    rows = count * cap
    return pl.pallas_call(
        functools.partial(begin_kernel, count),
        in_specs=[VMEM] * (count + 2) + [ANYWHERE] * len(after),
        out_specs=[VMEM] * 3,
        out_shape=[resident(rows, model)] + [resident(rows, units, dtype=F32)] * 2,
        compiler_params=PARAMS,
        cost_estimate=estimate(flops),
        name="begin",
    )(*arrived, *in_vmem(*weights[:2]), *after)


def expert_kernel(count, begun, *refs):
    ins = refs[:count]
    gate_ref, up_ref, both_ref, flipped_ref = refs[count : count + 4]
    cap = ins[0].shape[1]
    model, units = gate_ref.shape
    if begun:
        pre_gate_ref, pre_up_ref = refs[count + 4 : count + 6]
        outs, (cots_ref, pair_units_ref, hidden_ref) = refs[-count - 3 : -3], refs[-3:]
    else:
        outs = refs[-count - 4 : -4]
        rows_ref, cots_ref, pair_units_ref, hidden_ref = refs[-4:]
    for which in range(count):
        part = slice(which * cap, (which + 1) * cap)
        if not begun:
            rows_ref[part, :] = ins[which][0]
        cots_ref[part, :] = ins[which][0 if begun else 1]
    block = min(256, units)
    for start in range(0, units, block):
        columns = slice(start, start + block)
        if begun:
            pre_gate, pre_up = pre_gate_ref[:, columns], pre_up_ref[:, columns]
        else:
            pre_gate = dot(rows_ref[...], gate_ref[:, columns])
            pre_up = dot(rows_ref[...], up_ref[:, columns])
        hidden_cot = dot(cots_ref[...], flipped_ref[:, columns])
        sigmoid_gate = jax.nn.sigmoid(pre_gate)
        activated = pre_gate * sigmoid_gate
        hidden_ref[:, columns] = (activated * pre_up).astype(BF16)
        pair_units_ref[:, columns] = (
            hidden_cot * pre_up * sigmoid_gate * (1.0 + pre_gate * (1.0 - sigmoid_gate))
        ).astype(BF16)
        pair_units_ref[:, units + start : units + start + block] = (
            hidden_cot * activated
        ).astype(BF16)
    block = min(512, model)
    for start in range(0, model, block):
        columns = slice(start, start + block)
        pair_cot = dot(pair_units_ref[...], both_ref[:, columns]).astype(BF16)
        for which in range(count):
            outs[which][:, columns] = pair_cot[which * cap : (which + 1) * cap]


def expert(arrived, weights, begun, flops, after):
    count = len(arrived)
    _, cap, model = arrived[0].shape
    units = weights[0].shape[1]
    rows = count * cap
    kept = [resident(rows, model)] * (1 if begun else 2)
    kept += [resident(rows, 2 * units), resident(rows, units)]
    result = pl.pallas_call(
        functools.partial(expert_kernel, count, bool(begun)),
        in_specs=[VMEM] * (count + 4 + len(begun[1:])) + [ANYWHERE] * len(after),
        out_specs=[VMEM] * (count + len(kept)),
        out_shape=[array((cap, model))] * count + kept,
        compiler_params=PARAMS,
        cost_estimate=estimate(flops),
        name="expert",
    )(*arrived, *in_vmem(*weights, *begun[1:]), *after)
    return result[:count], list(begun[:1]) + list(result[count:])


STEPS = 4


def grads_kernel(planes, add, ids_ref, *refs):
    saved = [refs[4 * which : 4 * which + 4] for which in range(planes)]
    refs = refs[4 * planes :]
    model, units = saved[0][0].shape[1], saved[0][3].shape[1]
    half = ids_ref[ids_ref.shape[0] - (2 if add else 1)]
    height, width = model // 2 // STEPS, model // STEPS
    rest = units // 2 - height
    fold = height // rest
    part = width // fold
    if add:
        other_in, _, gate_out, up_out, down_out, token, gate_ref, up_ref, down_ref, other_ref, sems, other_sems = refs
        token[...] = jnp.zeros(token.shape, F32)
    else:
        _, sent_out, sent_ref, sems = refs
    own_units = pl.ds(pl.multiple_of(half * (units // 2), 128), units // 2)
    flipped_hidden = [kept[3][:, own_units].T for kept in saved]

    def fetch(step):
        at = slice(step * height, (step + 1) * height)
        slot = step % 2
        return pltpu.make_async_copy(other_in.at[at], other_ref.at[slot], other_sems.at[slot])

    def moves(step):
        at = slice(step * height, (step + 1) * height)
        across = slice(step * width, (step + 1) * width)
        slot = step % 2
        if add:
            pairs = (
                (gate_ref.at[slot], gate_out.at[at]),
                (up_ref.at[slot], up_out.at[at]),
                (down_ref.at[slot], down_out.at[:, across]),
            )
        else:
            pairs = ((sent_ref.at[slot], sent_out.at[at]),)
        return [
            pltpu.make_async_copy(source, target, sems.at[slot, which])
            for which, (source, target) in enumerate(pairs)
        ]

    if add:
        fetch(0).start()
    for step in range(STEPS):
        slot = step % 2
        across = slice(step * width, (step + 1) * width)
        own_rows = pl.ds(pl.multiple_of(half * (model // 2) + step * height, 128), height)
        both, down = 0.0, 0.0
        for flipped, (rows_ref, cots_ref, pair_units_ref, _) in zip(flipped_hidden, saved):
            both = both + dot(rows_ref[:, own_rows].T, pair_units_ref[...])
            down = down + dot(flipped, cots_ref[:, across])
        if step >= 2:
            for copy in moves(step - 2):
                copy.wait()
        if add:
            fetch(step).wait()
            if step + 1 < STEPS:
                fetch(step + 1).start()
            gate_ref[slot] = both[:, :units] + other_ref[slot, :, :units].astype(F32)
            up_ref[slot] = both[:, units:] + other_ref[slot, :, units : 2 * units].astype(F32)
            down_ref[slot, :height, :] = down[:height] + other_ref[
                slot, :, 2 * units : 2 * units + width
            ].astype(F32)
            for which in range(fold):
                columns = slice(which * part, (which + 1) * part)
                lower = slice(which * rest, (which + 1) * rest)
                down_ref[slot, height:, columns] = down[height:, columns] + other_ref[
                    slot, lower, 2 * units + width :
                ].astype(F32)
        else:
            sent_ref[slot, :, : 2 * units] = both.astype(BF16)
            down = down.astype(BF16)
            sent_ref[slot, :, 2 * units : 2 * units + width] = down[:height]
            for which in range(fold):
                lower = slice(which * rest, (which + 1) * rest)
                sent_ref[slot, lower, 2 * units + width :] = down[
                    height:, which * part : (which + 1) * part
                ]
        for copy in moves(step):
            copy.start()
    for step in range(STEPS - 2, STEPS):
        for copy in moves(step):
            copy.wait()


def grads(ids, saved, received, flops, after):
    model, units = saved[0][0].shape[1], saved[0][3].shape[1]
    height = model // 2 // STEPS
    sent_width = 3 * units
    add = bool(received)
    if add:
        shapes = [(model // 2, units), (model // 2, units), (units // 2, model)]
        stages = [(2, height, units), (2, height, units), (2, units // 2, model // STEPS)]
        dtype = F32
    else:
        shapes, stages, dtype = [(model // 2, sent_width)], [(2, height, sent_width)], BF16
    scratch = [pltpu.VMEM(shape, dtype) for shape in stages]
    if add:
        scratch.append(pltpu.VMEM((2, height, sent_width), BF16))
    scratch.append(pltpu.SemaphoreType.DMA((2, len(shapes))))
    if add:
        scratch.append(pltpu.SemaphoreType.DMA((2,)))
    return pl.pallas_call(
        functools.partial(grads_kernel, len(saved), add),
        in_specs=[SMEM] + [VMEM] * (4 * len(saved)) + [ANYWHERE] * (1 + add),
        out_specs=[HBM] * len(shapes) + [VMEM] * add,
        out_shape=[array(shape, dtype) for shape in shapes] + [array((8, 128), F32)] * add,
        scratch_shapes=scratch,
        compiler_params=LARGE,
        cost_estimate=estimate(flops),
        name="grads",
    )(ids, *in_vmem(*(part for kept in saved for part in kept)), *received, after)


def expand_kernel(count, top, ids_ref, meta_ref, *refs):
    back, out = refs[:count], refs[-1]
    cap, model = back[0].shape
    onehot, _ = slot_masks(ids_ref, meta_ref[...], count, cap, top)
    spread = onehot.T.astype(BF16)
    step = min(512, model)
    for start in range(0, model, step):
        columns = slice(start, start + step)
        value = dot(spread, jnp.concatenate([ref[:, columns] for ref in back], axis=0))
        out[:, columns] = value.astype(out.dtype)


def expand(ids, packed, back, top, dtype, flops, after):
    count = len(back)
    cap, model = back[0].shape
    tokens = packed.shape[0] - META
    whole = lambda *shape: pl.BlockSpec(shape, lambda s: (0, 0))
    return pl.pallas_call(
        functools.partial(expand_kernel, count, top),
        grid=(1,),
        out_shape=array((tokens, model), dtype),
        in_specs=[SMEM, pl.BlockSpec((META, tokens), lambda s: (tokens // META, 0))]
        + [whole(cap, model)] * count
        + [ANYWHERE],
        out_specs=whole(tokens, model),
        compiler_params=PARAMS,
        cost_estimate=estimate(flops),
        name="expand",
    )(ids, packed, *back, after)


def total_kernel(count, own_ref, *refs):
    value = own_ref[...]
    for ref in refs[:count]:
        value = value + ref[...].astype(F32)
    refs[-1][...] = value.astype(refs[-1].dtype)


def total(own, others, dtype, flops, after):
    return pl.pallas_call(
        functools.partial(total_kernel, len(others)),
        out_shape=array(own.shape, dtype),
        in_specs=[VMEM] * (1 + len(others)) + [ANYWHERE],
        out_specs=VMEM,
        compiler_params=PARAMS,
        cost_estimate=estimate(flops),
        name="total",
    )(own, *others, after)


FOUR_PLANES = (
    ("both", 0, 0),
    ("flip", 0, 0),
    ("rows", 2, 0),
    ("expert", 0, 0),
    ("begin", 2, 34),
    ("own", 0, 0),
    ("cots", 2, 0),
    ("both", 3, 0),
    ("expert", 2, 29),
    ("expert", 3, 0),
    ("both", 1, 0),
    ("expand", 2, 0),
    ("expand", 3, 0),
    ("total", 1, 0),
    ("expert", 1, 0),
    ("lend", 0, 37),
    ("expand", 1, 37),
    ("finish", 0, 37),
)
LATE = ()


def many_planes(outer):
    order = list(range(2, outer)) + [1]
    chain = [("both", 0, 0), ("flip", 0, 0), ("expert", 0, 0), ("own", 0, 0)]
    for plane in order:
        chain += [("both", plane, 0), ("expert", plane, 0)]
        chain += [("expand", plane, 0)]
    return chain + [("lend", 0, 0), ("finish", 0, 0)]


def local(tokens, cotangent, experts, mixing, gate_matrix, up_matrix, down_matrix):
    expert_count = lax.axis_size("expert")
    inner = min(4, expert_count)
    outer = expert_count // inner
    tok_rows, top = experts.shape
    cap = 2 * tok_rows * top // expert_count
    weight_gate, weight_up, weight_down = gate_matrix[0], up_matrix[0], down_matrix[0]

    def swap(value, mask):
        pairs = [(device, device ^ mask) for device in range(expert_count)]
        return lax.ppermute(value, "expert", pairs)

    def swap_inner(values):
        return [values[0]] + [swap(values[which], which) for which in range(1, inner)]

    core = lax.axis_index("dp").astype(jnp.int32)
    plane_ids = jnp.bitwise_xor(lax.axis_index("expert").astype(jnp.int32), jnp.arange(inner, dtype=jnp.int32))
    ids = jnp.concatenate([plane_ids, jnp.stack([core, 1 - core])])
    chain = FOUR_PLANES if outer == 4 else many_planes(outer)
    planes = [plane for kind, plane, _ in chain if kind == "expert"]
    packed = {0: pack(tokens, experts, mixing)}
    cots = {0: cotangent}
    arrived, returned, partial, saved, begun = {}, {}, [], {}, {}
    late = LATE if outer == 4 else ()
    late_planes = [plane for plane, _, _ in late]
    split = [plane for kind, plane, _ in chain if kind == "rows"]
    for plane in planes[1:]:
        if plane == plane & -plane and plane not in late_planes:
            packed[plane] = swap(packed[0], plane * inner)
            if plane not in split:
                cots[plane] = swap(cotangent, plane * inner)

    def send(kind, plane, flops, last):
        parts = ("rows", "cots") if kind == "both" else (kind,)
        onward = [other for other in planes if other ^ (other & -other) == plane and plane]
        copied = []
        if onward and "rows" in parts:
            copied.append(packed[plane])
        if onward and "cots" in parts:
            copied.append(cots[plane])
        if kind == "rows":
            copied.append(cotangent)
        waiting = [other for other, what, where in late if (what, where) == (kind, plane)]
        if waiting:
            copied += [packed[0], cotangent]
        value = cots.get(plane, cotangent)
        sent, copies = select(ids, packed[plane], value, cap, top, parts, copied, flops, last)
        copies = list(copies)
        arrived[plane, kind] = swap_inner(sent)
        for part, held in (("rows", packed), ("cots", cots)):
            if onward and part in parts:
                copy = copies.pop(0)
                for other in onward:
                    held[other] = swap(copy, (other & -other) * inner)
        if kind == "rows":
            cots[plane] = swap(copies.pop(0), plane * inner)
        for other in waiting:
            packed[other] = swap(copies[0], other * inner)
            cots[other] = swap(copies[1], other * inner)
        return sent[0]

    last, weights, own, received, results = None, None, None, None, None
    for kind, plane, size in chain:
        after = [] if last is None else [last]
        flops = 1 << size
        if kind in ("both", "rows", "cots"):
            last = send(kind, plane, flops, after)
        elif kind == "flip":
            weights = flip(weight_gate, weight_up, weight_down, flops, last)
            last = weights[3]
        elif kind == "begin":
            begun[plane] = begin(arrived[plane, "rows"], weights, flops, after)
            last = begun[plane][1]
        elif kind == "expert":
            pieces = arrived[plane, "cots" if plane in begun else "both"]
            pair_cot, saved[plane] = expert(pieces, weights, begun.get(plane, []), flops, after)
            returned[plane] = swap_inner(pair_cot)
            last = pair_cot[0]
        elif kind == "own":
            own = last = expand(ids, packed[0], returned[0], top, F32, flops, last)
        elif kind == "expand":
            last = expand(ids, packed[plane], returned[plane], top, BF16, flops, last)
            partial.append(swap(last, plane * inner))
        elif kind == "total":
            own = last = total(own, partial[:plane], F32, flops, last)
            del partial[:plane]
        elif kind == "lend":
            (last,) = grads(ids, [saved[other] for other in planes], [], flops, last)
            received = lax.ppermute(last, "dp", [(0, 1), (1, 0)])
        elif kind == "finish":
            kept = [saved[other] for other in planes]
            *results, last = grads(ids, kept, [received], flops, last)
    input_grad = total(own, partial, BF16, 1, last)
    return (input_grad, *(value[None] for value in results))


def solution(mesh):
    return jax.shard_map(
        local,
        mesh=mesh,
        in_specs=(
            P(("dp", "expert"), None),
            P(("dp", "expert"), None),
            P(("dp", "expert"), None),
            P(("dp", "expert"), None),
            P("expert", None, None),
            P("expert", None, None),
            P("expert", None, None),
        ),
        out_specs=(
            P(("dp", "expert"), None),
            P("expert", "dp", None),
            P("expert", "dp", None),
            P("expert", "dp", None),
        ),
        check_vma=False,
    )
```

profile of v0, /device:TPU:0, one launch (start us, length us, event | category | flops | bytes accessed | tf_op | source)
XLA Modules:
  0.0 187.6 jit_solution(10927940976849008054)
XLA Ops:
  0.6 0.7 copy-done.4
  1.3 0.7 copy-done.5
  2.0 1.1 pack.1.refs_0_.meta_ref
  3.1 4.1 %collective-permute-start.3 = (bf16[144,2048]{1,0:T(8,128)(2,1)S(1)}, bf16[144,2048]{1,0:T(8,128)(2,1)S(1)}, u32[]{:S(2)}, u32[]{:S(2)}) collective-permute-start(bf16[144,2048]{1,0:T(8,128)(2,1)S(1)} %pack.1.refs_0_.meta_ref), channel_id=1, source_target_pairs={{0,8},{1,9},{2,10},{3,11},{4,12},{5,13},{6,14},{7,15},{8,0},{9,1},... | collective-permute-start | bytes 1769480 | tf_op jit(solution)/shard_map/ppermute | solution.py:485
  7.3 1.0 copy-done.2
  8.3 1.4 select.5
  9.7 1.6 collective-permute-start
  11.2 1.5 collective-permute-start.1
  12.8 0.5 collective-permute-start.2
  13.2 4.7 %flip.1 = (bf16[2048,768]{1,0:T(8,128)(2,1)S(1)}, bf16[2048,768]{1,0:T(8,128)(2,1)S(1)}, bf16[1536,2048]{1,0:T(8,128)(2,1)S(1)}, bf16[2048,768]{1,0:T(8,128)(2,1)S(1)}) custom-call(bf16[2048,768]{1,0:T(8,128)(2,1)} %bitcast.12, bf16[2048,768]{1,0:T(8,128)(2,1)} %bitcast.13, bf16[768,2048]{1,0:T(8,128)(2,1)} %bitcast.14, ...), custom_call_target="tpu_custom_call" | custom-call | flops 1 | bytes 1 | tf_op jit(solution)/shard_map/flip/pallas_call | solution.py:173
  17.9 15.2 %collective-permute-done.3.refs_0_.refs_2_.meta_ref = bf16[144,2048]{1,0:T(8,128)(2,1)S(1)} collective-permute-done((bf16[144,2048]{1,0:T(8,128)(2,1)S(1)}, bf16[144,2048]{1,0:T(8,128)(2,1)S(1)}, u32[]{:S(2)}, u32[]{:S(2)}) %collective-permute-start.3) | collective-permute-done | bytes 589856 | tf_op jit(solution)/shard_map/ppermute | solution.py:485
  33.1 1.3 select.6
  34.4 1.6 collective-permute-start.7
  36.0 1.5 collective-permute-start.8
  37.5 0.4 collective-permute-start.9
  38.0 4.1 %collective-permute-start.14 = (bf16[144,2048]{1,0:T(8,128)(2,1)S(1)}, bf16[144,2048]{1,0:T(8,128)(2,1)S(1)}, u32[]{:S(2)}, u32[]{:S(2)}) collective-permute-start(bf16[144,2048]{1,0:T(8,128)(2,1)S(1)} %get-tuple-element.92), channel_id=1, source_target_pairs={{0,4},{1,5},{2,6},{3,7},{4,0},{5,1},{6,2},{7,3},{8,12},{9,13},{10,... | collective-permute-start | bytes 1769480 | tf_op jit(solution)/shard_map/ppermute | solution.py:485
  42.1 5.2 %expert.4 = (bf16[64,2048]{1,0:T(8,128)(2,1)S(1)}, bf16[64,2048]{1,0:T(8,128)(2,1)S(1)}, bf16[64,2048]{1,0:T(8,128)(2,1)S(1)}, bf16[64,2048]{1,0:T(8,128)(2,1)S(...) custom-call(bf16[2,64,2048]{2,1,0:T(8,128)(2,1)S(1)} %get-tuple-elem, ...), custom_call_target="tpu_custom_call" | custom-call | flops 1 | bytes 1 | tf_op jit(solution)/shard_map/expert/pallas_call | solution.py:266
  47.3 1.6 collective-permute-start.4
  48.9 1.5 collective-permute-start.5
  50.4 0.5 collective-permute-start.6
  50.9 1.8 begin.1
  52.7 3.9 %collective-permute-done.4.refs_1_ = bf16[64,2048]{1,0:T(8,128)(2,1)S(1)} collective-permute-done((bf16[64,2048]{1,0:T(8,128)(2,1)S(1)}, bf16[64,2048]{1,0:T(8,128)(2,1)S(1)}, u32[]{:S(2)}, u32[]{:S(2)}) %collective-permute-start.4) | collective-permute-done | bytes 262176 | tf_op jit(solution)/shard_map/ppermute | solution.py:485
  56.6 4.4 %collective-permute-done.5.refs_2_ = bf16[64,2048]{1,0:T(8,128)(2,1)S(1)} collective-permute-done((bf16[64,2048]{1,0:T(8,128)(2,1)S(1)}, bf16[64,2048]{1,0:T(8,128)(2,1)S(1)}, u32[]{:S(2)}, u32[]{:S(2)}) %collective-permute-start.5) | collective-permute-done | bytes 262176 | tf_op jit(solution)/shard_map/ppermute | solution.py:485
  61.1 1.0 expand.4.refs_3_.own_ref
  62.1 0.4 collective-permute-done.10.refs_1_.refs_2_
  62.5 1.3 select.7
  63.8 0.8 collective-permute-start.15
  64.7 0.5 collective-permute-start.11
  65.2 1.5 collective-permute-start.12
  66.7 1.4 collective-permute-start.13
  68.1 7.8 %collective-permute-done.15.refs_1_ = bf16[128,2048]{1,0:T(8,128)(2,1)S(1)} collective-permute-done((bf16[128,2048]{1,0:T(8,128)(2,1)S(1)}, bf16[128,2048]{1,0:T(8,128)(2,1)S(1)}, u32[]{:S(2)}, u32[]{:S(2)}) %collective-permute-start.15) | collective-permute-done | bytes 524320 | tf_op jit(solution)/shard_map/ppermute | solution.py:485
  75.9 1.4 select.8
  77.3 1.1 collective-permute-start.21
  78.4 1.5 collective-permute-start.22
  79.9 1.0 collective-permute-start.23
  80.9 0.3 collective-permute-start.20
  81.2 1.7 collective-permute-start.19
  82.9 3.6 %expert.5 = (bf16[64,2048]{1,0:T(8,128)(2,1)S(1)}, bf16[64,2048]{1,0:T(8,128)(2,1)S(1)}, bf16[64,2048]{1,0:T(8,128)(2,1)S(1)}, bf16[64,2048]{1,0:T(8,128)(2,1)S(...) custom-call(bf16[1,64,2048]{2,1,0:T(8,128)(2,1)S(1)} %get-tuple-element.87.refs_2_.re, ...), custom_call_target="tpu_custom_call" | custom-call | flops 536870912 | bytes 1 | tf_op jit(solution)/shard_map/expert/pallas_call | solution.py:266
  86.5 5.8 %collective-permute-done.21.refs_1_ = bf16[2,64,2048]{2,1,0:T(8,128)(2,1)S(1)} collective-permute-done((bf16[2,64,2048]{2,1,0:T(8,128)(2,1)S(1)}, bf16[2,64,2048]{2,1,0:T(8,128)(2,1)S(1)}, u32[]{:S(2)}, u32[]{:S(2)}) %collective-permute-start.21) | collective-permute-done | bytes 524320 | tf_op jit(solution)/shard_map/ppermute | solution.py:485
  92.3 1.0 collective-permute-start.16
  93.3 10.8 %collective-permute-done.22.refs_2_ = bf16[2,64,2048]{2,1,0:T(8,128)(2,1)S(1)} collective-permute-done((bf16[2,64,2048]{2,1,0:T(8,128)(2,1)S(1)}, bf16[2,64,2048]{2,1,0:T(8,128)(2,1)S(1)}, u32[]{:S(2)}, u32[]{:S(2)}) %collective-permute-start.22) | collective-permute-done | bytes 524320 | tf_op jit(solution)/shard_map/ppermute | solution.py:485
  104.1 1.7 collective-permute-start.17
  105.8 5.3 %expert.6 = (bf16[64,2048]{1,0:T(8,128)(2,1)S(1)}, bf16[64,2048]{1,0:T(8,128)(2,1)S(1)}, bf16[64,2048]{1,0:T(8,128)(2,1)S(1)}, bf16[64,2048]{1,0:T(8,128)(2,1)S(...) custom-call(bf16[2,64,2048]{2,1,0:T(8,128)(2,1)S(1)} %get-tuple-elem, ...), custom_call_target="tpu_custom_call" | custom-call | flops 1 | bytes 1 | tf_op jit(solution)/shard_map/expert/pallas_call | solution.py:266
  111.0 1.9 %collective-permute-start.25 = (bf16[64,2048]{1,0:T(8,128)(2,1)S(1)}, bf16[64,2048]{1,0:T(8,128)(2,1)S(1)}, u32[]{:S(2)}, u32[]{:S(2)}) collective-permute-start(bf16[64,2048]{1,0:T(8,128)(2,1)S(1)} %get-tuple-element.104), channel_id=1, source_target_pairs={{0,1},{1,0},{2,3},{3,2},{4,5},{5,4},{6,7},{7,6},{8,9},{9,8},{10,11... | collective-permute-start | bytes 786440 | tf_op jit(solution)/shard_map/ppermute | solution.py:485
  112.9 1.7 collective-permute-start.26
  114.6 1.4 select.9
  116.0 0.6 collective-permute-start.29
  116.6 1.0 expand.5.refs_4_
  117.6 3.4 %collective-permute-start.24 = (bf16[128,2048]{1,0:T(8,128)(2,1)S(1)}, bf16[128,2048]{1,0:T(8,128)(2,1)S(1)}, u32[]{:S(2)}, u32[]{:S(2)}) collective-permute-start(bf16[128,2048]{1,0:T(8,128)(2,1)S(1)} %expand.5.refs_4_), channel_id=1, source_target_pairs={{0,8},{1,9},{2,10},{3,11},{4,12},{5,13},{6,14},{7,15},{8,0},{9,1},... | collective-permute-start | bytes 1572872 | tf_op jit(solution)/shard_map/ppermute | solution.py:485
  121.1 1.0 collective-permute-start.30
  122.1 1.2 collective-permute-start.31
  123.3 1.8 collective-permute-start.27
  125.0 20.1 %collective-permute-done.27.refs_3_ = bf16[64,2048]{1,0:T(8,128)(2,1)S(1)} collective-permute-done((bf16[64,2048]{1,0:T(8,128)(2,1)S(1)}, bf16[64,2048]{1,0:T(8,128)(2,1)S(1)}, u32[]{:S(2)}, u32[]{:S(2)}) %collective-permute-start.27) | collective-permute-done | bytes 262176 | tf_op jit(solution)/shard_map/ppermute | solution.py:485
  145.1 1.8 expand.6.refs_1_
  146.9 3.5 %collective-permute-start.28 = (bf16[128,2048]{1,0:T(8,128)(2,1)}, bf16[128,2048]{1,0:T(8,128)(2,1)}, u32[]{:S(2)}, u32[]{:S(2)}) collective-permute-start(bf16[128,2048]{1,0:T(8,128)(2,1)} %expand.6.refs_1_), channel_id=1, source_target_pairs={{0,12},{1,13},{2,14},{3,15},{4,8},{5,9},{6,10},{7,11},{8,4},{9,5},... | collective-permute-start | bytes 1572872 | tf_op jit(solution)/shard_map/ppermute | solution.py:485
  150.4 0.1 total.2.refs_8_.own_ref
  150.5 5.4 %expert.7 = (bf16[64,2048]{1,0:T(8,128)(2,1)S(1)}, bf16[64,2048]{1,0:T(8,128)(2,1)S(1)}, bf16[64,2048]{1,0:T(8,128)(2,1)S(1)}, bf16[64,2048]{1,0:T(8,128)(2,1)S(...) custom-call(bf16[2,64,2048]{2,1,0:T(8,128)(2,1)S(1)} %get-tuple-elem, ...), custom_call_target="tpu_custom_call" | custom-call | flops 1 | bytes 1 | tf_op jit(solution)/shard_map/expert/pallas_call | solution.py:266
  155.9 1.8 collective-permute-start.32
  157.7 1.9 %collective-permute-start.33 = (bf16[64,2048]{1,0:T(8,128)(2,1)S(1)}, bf16[64,2048]{1,0:T(8,128)(2,1)S(1)}, u32[]{:S(2)}, u32[]{:S(2)}) collective-permute-start(bf16[64,2048]{1,0:T(8,128)(2,1)S(1)} %get-tuple-element.112), channel_id=1, source_target_pairs={{0,2},{1,3},{2,0},{3,1},{4,6},{5,7},{6,4},{7,5},{8,10},{9,11},{10,... | collective-permute-start | bytes 786440 | tf_op jit(solution)/shard_map/ppermute | solution.py:485
  159.7 7.5 %grads.2.refs_4_ = bf16[1024,2304]{1,0:T(8,128)(2,1)S(1)} custom-call(s32[6]{0:T(128)S(1)} %pad_add_fusion.ids_ref, bf16[256,2048]{1,0:T(8,128)(2,1)S(1)} %get-tuple-element.114.refs_0_, bf16[256,2048]{1,0:T(8,128)(2,1)S(1)} %get-tuple-element.115.refs_1_, bf16[256,1536]{1,0:T(8,128)(2,1)S(1)} %get-tuple-element.116.refs_2_, ...), custom_call_target="tpu_custom_call" | custom-call | flops 137438953472 | bytes 1 | tf_op jit(solution)/shard_map/grads/pallas_call | solution.py:381
  167.3 1.0 expand.7.refs_17_
  168.4 6.7 %collective-permute-done.36.refs_16_ = bf16[1024,2304]{1,0:T(8,128)(2,1)S(1)} collective-permute-done((bf16[1024,2304]{1,0:T(8,128)(2,1)S(1)}, bf16[1024,2304]{1,0:T(8,128)(2,1)S(1)}, u32[]{:S(2)}, u32[]{:S(2)}) %collective-permute-start.36) | collective-permute-done | bytes 4718624 | tf_op jit(solution)/shard_map/ppermute | solution.py:563
  175.2 10.3 %grads.3 = (f32[1024,768]{1,0:T(8,128)}, f32[1024,768]{1,0:T(8,128)}, f32[384,2048]{1,0:T(8,128)}, f32[8,128]{1,0:T(8,128)S(1)}) custom-call(s32[6]{0:T(128)S(1)} %pad_add_fusion.ids_ref, bf16[256,2048]{1,0:T(8,128)(2,1)S(1)} %get-tuple-element.114.refs_0_, bf16[256,2048]{1,0:T(8,128)(2,1)S(1)} %get-tuple-element.115.refs_1_, ...), custom_call_target="tpu_custom_call" | custom-call | flops 137438953472 | bytes 1 | tf_op jit(solution)/shard_map/grads/pallas_call | solution.py:381
  185.6 2.0 %total.3 = bf16[128,2048]{1,0:T(8,128)(2,1)} custom-call(f32[128,2048]{1,0:T(8,128)S(1)} %copy-done.1, bf16[128,2048]{1,0:T(8,128)(2,1)} %collective-permute-done.28.refs_0_, bf16[128,2048]{1,0:T(8,128)(2,1)S(1)} %collective-permute-done.35.refs_1_, f32[8,128]{1,0:T(8,128)S(1)} %get-tuple-element.130.refs_2_), custom_call_target="tpu_custom_call" | custom-call | flops 1 | bytes 1 | tf_op jit(solution)/shard_map/total/pallas_call | solution.py:432
  (44 shorter events, 0.3 us)
Async XLA Ops:
  0.6 0.7 copy-start.4
  1.3 0.7 copy-start.5
  3.1 30.1 %collective-permute-start.3 = (bf16[144,2048]{1,0:T(8,128)(2,1)S(1)}, bf16[144,2048]{1,0:T(8,128)(2,1)S(1)}, u32[]{:S(2)}, u32[]{:S(2)}) collective-permute-start(bf16[144,2048]{1,0:T(8,128)(2,1)S(1)} %pack.1.refs_0_.meta_ref), channel_id=1, source_target_pairs={{0,8},{1,9},{2,10},{3,11},{4,12},{5,13},{6,14},{7,15},{8,0},{9,1},... | collective-permute-start | bytes 1769480 | tf_op jit(solution)/shard_map/ppermute | solution.py:485
  7.2 1.0 copy-start.2
  9.7 27.8 %collective-permute-start = (bf16[2,64,2048]{2,1,0:T(8,128)(2,1)S(1)}, bf16[2,64,2048]{2,1,0:T(8,128)(2,1)S(1)}, u32[]{:S(2)}, u32[]{:S(2)}) collective-permute-start(bf16[2,64,2048]{2,1,0:T(8,128)(2,1)S(1)} %get-tuple-element.70), channel_id=1, source_target_pairs={{0,1},{1,0},{2,3},{3,2},{4,5},{5,4},{6,7},{7,6},{8,9},{9,8},{10,11... | collective-permute-start | bytes 1572872 | tf_op jit(solution)/shard_map/ppermute | solution.py:485
  11.2 26.7 %collective-permute-start.1 = (bf16[2,64,2048]{2,1,0:T(8,128)(2,1)S(1)}, bf16[2,64,2048]{2,1,0:T(8,128)(2,1)S(1)}, u32[]{:S(2)}, u32[]{:S(2)}) collective-permute-start(bf16[2,64,2048]{2,1,0:T(8,128)(2,1)S(1)} %get-tuple-element.71), channel_id=1, source_target_pairs={{0,2},{1,3},{2,0},{3,1},{4,6},{5,7},{6,4},{7,5},{8,10},{9,11},{10,... | collective-permute-start | bytes 1572872 | tf_op jit(solution)/shard_map/ppermute | solution.py:485
  12.8 25.2 %collective-permute-start.2 = (bf16[2,64,2048]{2,1,0:T(8,128)(2,1)S(1)}, bf16[2,64,2048]{2,1,0:T(8,128)(2,1)S(1)}, u32[]{:S(2)}, u32[]{:S(2)}) collective-permute-start(bf16[2,64,2048]{2,1,0:T(8,128)(2,1)S(1)} %get-tuple-element.72), channel_id=1, source_target_pairs={{0,3},{1,2},{2,1},{3,0},{4,7},{5,6},{6,5},{7,4},{8,11},{9,10},{10,... | collective-permute-start | bytes 1572872 | tf_op jit(solution)/shard_map/ppermute | solution.py:485
  34.4 12.9 %collective-permute-start.7 = (bf16[1,64,2048]{2,1,0:T(8,128)(2,1)S(1)}, bf16[1,64,2048]{2,1,0:T(8,128)(2,1)S(1)}, u32[]{:S(2)}, u32[]{:S(2)}) collective-permute-start(bf16[1,64,2048]{2,1,0:T(8,128)(2,1)S(1)} %get-tuple-element.82), channel_id=1, source_target_pairs={{0,1},{1,0},{2,3},{3,2},{4,5},{5,4},{6,7},{7,6},{8,9},{9,8},{10,11... | collective-permute-start | bytes 786440 | tf_op jit(solution)/shard_map/ppermute | solution.py:485
  36.0 12.9 %collective-permute-start.8 = (bf16[1,64,2048]{2,1,0:T(8,128)(2,1)S(1)}, bf16[1,64,2048]{2,1,0:T(8,128)(2,1)S(1)}, u32[]{:S(2)}, u32[]{:S(2)}) collective-permute-start(bf16[1,64,2048]{2,1,0:T(8,128)(2,1)S(1)} %get-tuple-element.83), channel_id=1, source_target_pairs={{0,2},{1,3},{2,0},{3,1},{4,6},{5,7},{6,4},{7,5},{8,10},{9,11},{10,... | collective-permute-start | bytes 786440 | tf_op jit(solution)/shard_map/ppermute | solution.py:485
  37.5 12.9 %collective-permute-start.9 = (bf16[1,64,2048]{2,1,0:T(8,128)(2,1)S(1)}, bf16[1,64,2048]{2,1,0:T(8,128)(2,1)S(1)}, u32[]{:S(2)}, u32[]{:S(2)}) collective-permute-start(bf16[1,64,2048]{2,1,0:T(8,128)(2,1)S(1)} %get-tuple-element.84), channel_id=1, source_target_pairs={{0,3},{1,2},{2,1},{3,0},{4,7},{5,6},{6,5},{7,4},{8,11},{9,10},{10,... | collective-permute-start | bytes 786440 | tf_op jit(solution)/shard_map/ppermute | solution.py:485
  38.0 24.5 %collective-permute-start.10 = (bf16[128,2048]{1,0:T(8,128)(2,1)S(1)}, bf16[128,2048]{1,0:T(8,128)(2,1)S(1)}, u32[]{:S(2)}, u32[]{:S(2)}) collective-permute-start(bf16[128,2048]{1,0:T(8,128)(2,1)S(1)} %get-tuple-element.86), channel_id=1, source_target_pairs={{0,8},{1,9},{2,10},{3,11},{4,12},{5,13},{6,14},{7,15},{8,0},{9,1},... | collective-permute-start | bytes 1572872 | tf_op jit(solution)/shard_map/ppermute | solution.py:485
  38.0 30.2 %collective-permute-start.14 = (bf16[144,2048]{1,0:T(8,128)(2,1)S(1)}, bf16[144,2048]{1,0:T(8,128)(2,1)S(1)}, u32[]{:S(2)}, u32[]{:S(2)}) collective-permute-start(bf16[144,2048]{1,0:T(8,128)(2,1)S(1)} %get-tuple-element.92), channel_id=1, source_target_pairs={{0,4},{1,5},{2,6},{3,7},{4,0},{5,1},{6,2},{7,3},{8,12},{9,13},{10,... | collective-permute-start | bytes 1769480 | tf_op jit(solution)/shard_map/ppermute | solution.py:485
  47.3 9.3 %collective-permute-start.4 = (bf16[64,2048]{1,0:T(8,128)(2,1)S(1)}, bf16[64,2048]{1,0:T(8,128)(2,1)S(1)}, u32[]{:S(2)}, u32[]{:S(2)}) collective-permute-start(bf16[64,2048]{1,0:T(8,128)(2,1)S(1)} %get-tuple-element.79), channel_id=1, source_target_pairs={{0,1},{1,0},{2,3},{3,2},{4,5},{5,4},{6,7},{7,6},{8,9},{9,8},{10,11... | collective-permute-start | bytes 786440 | tf_op jit(solution)/shard_map/ppermute | solution.py:485
  48.9 12.2 %collective-permute-start.5 = (bf16[64,2048]{1,0:T(8,128)(2,1)S(1)}, bf16[64,2048]{1,0:T(8,128)(2,1)S(1)}, u32[]{:S(2)}, u32[]{:S(2)}) collective-permute-start(bf16[64,2048]{1,0:T(8,128)(2,1)S(1)} %get-tuple-element.80), channel_id=1, source_target_pairs={{0,2},{1,3},{2,0},{3,1},{4,6},{5,7},{6,4},{7,5},{8,10},{9,11},{10,... | collective-permute-start | bytes 786440 | tf_op jit(solution)/shard_map/ppermute | solution.py:485
  50.4 10.6 %collective-permute-start.6 = (bf16[64,2048]{1,0:T(8,128)(2,1)S(1)}, bf16[64,2048]{1,0:T(8,128)(2,1)S(1)}, u32[]{:S(2)}, u32[]{:S(2)}) collective-permute-start(bf16[64,2048]{1,0:T(8,128)(2,1)S(1)} %get-tuple-element.81), channel_id=1, source_target_pairs={{0,3},{1,2},{2,1},{3,0},{4,7},{5,6},{6,5},{7,4},{8,11},{9,10},{10,... | collective-permute-start | bytes 786440 | tf_op jit(solution)/shard_map/ppermute | solution.py:485
  61.1 19.8 %copy-start.3 = (bf16[128,2048]{1,0:T(8,128)(2,1)S(1)}, bf16[128,2048]{1,0:T(8,128)(2,1)}, u32[]{:S(2)}) copy-start(bf16[128,2048]{1,0:T(8,128)(2,1)} %refs_3_.1) | copy-start | bytes 1572868
  63.8 12.1 %collective-permute-start.15 = (bf16[128,2048]{1,0:T(8,128)(2,1)S(1)}, bf16[128,2048]{1,0:T(8,128)(2,1)S(1)}, u32[]{:S(2)}, u32[]{:S(2)}) collective-permute-start(bf16[128,2048]{1,0:T(8,128)(2,1)S(1)} %get-tuple-element.93), channel_id=1, source_target_pairs={{0,4},{1,5},{2,6},{3,7},{4,0},{5,1},{6,2},{7,3},{8,12},{9,13},{10,... | collective-permute-start | bytes 1572872 | tf_op jit(solution)/shard_map/ppermute | solution.py:485
  64.7 15.3 %collective-permute-start.11 = (bf16[1,64,2048]{2,1,0:T(8,128)(2,1)S(1)}, bf16[1,64,2048]{2,1,0:T(8,128)(2,1)S(1)}, u32[]{:S(2)}, u32[]{:S(2)}) collective-permute-start(bf16[1,64,2048]{2,1,0:T(8,128)(2,1)S(1)} %get-tuple-element.88), channel_id=1, source_target_pairs={{0,1},{1,0},{2,3},{3,2},{4,5},{5,4},{6,7},{7,6},{8,9},{9,8},{10,11... | collective-permute-start | bytes 786440 | tf_op jit(solution)/shard_map/ppermute | solution.py:485
  65.2 15.7 %collective-permute-start.12 = (bf16[1,64,2048]{2,1,0:T(8,128)(2,1)S(1)}, bf16[1,64,2048]{2,1,0:T(8,128)(2,1)S(1)}, u32[]{:S(2)}, u32[]{:S(2)}) collective-permute-start(bf16[1,64,2048]{2,1,0:T(8,128)(2,1)S(1)} %get-tuple-element.89), channel_id=1, source_target_pairs={{0,2},{1,3},{2,0},{3,1},{4,6},{5,7},{6,4},{7,5},{8,10},{9,11},{10,... | collective-permute-start | bytes 786440 | tf_op jit(solution)/shard_map/ppermute | solution.py:485
  66.7 14.5 %collective-permute-start.13 = (bf16[1,64,2048]{2,1,0:T(8,128)(2,1)S(1)}, bf16[1,64,2048]{2,1,0:T(8,128)(2,1)S(1)}, u32[]{:S(2)}, u32[]{:S(2)}) collective-permute-start(bf16[1,64,2048]{2,1,0:T(8,128)(2,1)S(1)} %get-tuple-element.90), channel_id=1, source_target_pairs={{0,3},{1,2},{2,1},{3,0},{4,7},{5,6},{6,5},{7,4},{8,11},{9,10},{10,... | collective-permute-start | bytes 786440 | tf_op jit(solution)/shard_map/ppermute | solution.py:485
  77.3 14.9 %collective-permute-start.21 = (bf16[2,64,2048]{2,1,0:T(8,128)(2,1)S(1)}, bf16[2,64,2048]{2,1,0:T(8,128)(2,1)S(1)}, u32[]{:S(2)}, u32[]{:S(2)}) collective-permute-start(bf16[2,64,2048]{2,1,0:T(8,128)(2,1)S(1)} %get-tuple-element.99), channel_id=1, source_target_pairs={{0,1},{1,0},{2,3},{3,2},{4,5},{5,4},{6,7},{7,6},{8,9},{9,8},{10,11... | collective-permute-start | bytes 1572872 | tf_op jit(solution)/shard_map/ppermute | solution.py:485
  78.4 25.7 %collective-permute-start.22 = (bf16[2,64,2048]{2,1,0:T(8,128)(2,1)S(1)}, bf16[2,64,2048]{2,1,0:T(8,128)(2,1)S(1)}, u32[]{:S(2)}, u32[]{:S(2)}) collective-permute-start(bf16[2,64,2048]{2,1,0:T(8,128)(2,1)S(1)} %get-tuple-element.100), channel_id=1, source_target_pairs={{0,2},{1,3},{2,0},{3,1},{4,6},{5,7},{6,4},{7,5},{8,10},{9,11},{10,... | collective-permute-start | bytes 1572872 | tf_op jit(solution)/shard_map/ppermute | solution.py:485
  79.9 25.8 %collective-permute-start.23 = (bf16[2,64,2048]{2,1,0:T(8,128)(2,1)S(1)}, bf16[2,64,2048]{2,1,0:T(8,128)(2,1)S(1)}, u32[]{:S(2)}, u32[]{:S(2)}) collective-permute-start(bf16[2,64,2048]{2,1,0:T(8,128)(2,1)S(1)} %get-tuple-element.101), channel_id=1, source_target_pairs={{0,3},{1,2},{2,1},{3,0},{4,7},{5,6},{6,5},{7,4},{8,11},{9,10},{10,... | collective-permute-start | bytes 1572872 | tf_op jit(solution)/shard_map/ppermute | solution.py:485
  80.9 30.1 %collective-permute-start.20 = (bf16[128,2048]{1,0:T(8,128)(2,1)S(1)}, bf16[128,2048]{1,0:T(8,128)(2,1)S(1)}, u32[]{:S(2)}, u32[]{:S(2)}) collective-permute-start(bf16[128,2048]{1,0:T(8,128)(2,1)S(1)} %copy-done.3), channel_id=1, source_target_pairs={{0,4},{1,5},{2,6},{3,7},{4,0},{5,1},{6,2},{7,3},{8,12},{9,13},{10,... | collective-permute-start | bytes 1572872 | tf_op jit(solution)/shard_map/ppermute | solution.py:485
  81.2 31.7 %collective-permute-start.19 = (bf16[144,2048]{1,0:T(8,128)(2,1)S(1)}, bf16[144,2048]{1,0:T(8,128)(2,1)S(1)}, u32[]{:S(2)}, u32[]{:S(2)}) collective-permute-start(bf16[144,2048]{1,0:T(8,128)(2,1)S(1)} %pack.1.refs_0_.meta_ref), channel_id=1, source_target_pairs={{0,4},{1,5},{2,6},{3,7},{4,0},{5,1},{6,2},{7,3},{8,12},{9,13},{10,... | collective-permute-start | bytes 1769480 | tf_op jit(solution)/shard_map/ppermute | solution.py:485
  92.3 23.7 %collective-permute-start.16 = (bf16[64,2048]{1,0:T(8,128)(2,1)S(1)}, bf16[64,2048]{1,0:T(8,128)(2,1)S(1)}, u32[]{:S(2)}, u32[]{:S(2)}) collective-permute-start(bf16[64,2048]{1,0:T(8,128)(2,1)S(1)} %get-tuple-element.96), channel_id=1, source_target_pairs={{0,1},{1,0},{2,3},{3,2},{4,5},{5,4},{6,7},{7,6},{8,9},{9,8},{10,11... | collective-permute-start | bytes 786440 | tf_op jit(solution)/shard_map/ppermute | solution.py:485
  104.1 12.5 %collective-permute-start.17 = (bf16[64,2048]{1,0:T(8,128)(2,1)S(1)}, bf16[64,2048]{1,0:T(8,128)(2,1)S(1)}, u32[]{:S(2)}, u32[]{:S(2)}) collective-permute-start(bf16[64,2048]{1,0:T(8,128)(2,1)S(1)} %get-tuple-element.97), channel_id=1, source_target_pairs={{0,2},{1,3},{2,0},{3,1},{4,6},{5,7},{6,4},{7,5},{8,10},{9,11},{10,... | collective-permute-start | bytes 786440 | tf_op jit(solution)/shard_map/ppermute | solution.py:485
  105.8 10.9 %collective-permute-start.18 = (bf16[64,2048]{1,0:T(8,128)(2,1)S(1)}, bf16[64,2048]{1,0:T(8,128)(2,1)S(1)}, u32[]{:S(2)}, u32[]{:S(2)}) collective-permute-start(bf16[64,2048]{1,0:T(8,128)(2,1)S(1)} %get-tuple-element.98), channel_id=1, source_target_pairs={{0,3},{1,2},{2,1},{3,0},{4,7},{5,6},{6,5},{7,4},{8,11},{9,10},{10,... | collective-permute-start | bytes 786440 | tf_op jit(solution)/shard_map/ppermute | solution.py:485
  111.0 11.1 %collective-permute-start.25 = (bf16[64,2048]{1,0:T(8,128)(2,1)S(1)}, bf16[64,2048]{1,0:T(8,128)(2,1)S(1)}, u32[]{:S(2)}, u32[]{:S(2)}) collective-permute-start(bf16[64,2048]{1,0:T(8,128)(2,1)S(1)} %get-tuple-element.104), channel_id=1, source_target_pairs={{0,1},{1,0},{2,3},{3,2},{4,5},{5,4},{6,7},{7,6},{8,9},{9,8},{10,11... | collective-permute-start | bytes 786440 | tf_op jit(solution)/shard_map/ppermute | solution.py:485
  112.9 10.4 %collective-permute-start.26 = (bf16[64,2048]{1,0:T(8,128)(2,1)S(1)}, bf16[64,2048]{1,0:T(8,128)(2,1)S(1)}, u32[]{:S(2)}, u32[]{:S(2)}) collective-permute-start(bf16[64,2048]{1,0:T(8,128)(2,1)S(1)} %get-tuple-element.105), channel_id=1, source_target_pairs={{0,2},{1,3},{2,0},{3,1},{4,6},{5,7},{6,4},{7,5},{8,10},{9,11},{10,... | collective-permute-start | bytes 786440 | tf_op jit(solution)/shard_map/ppermute | solution.py:485
  116.0 34.5 %collective-permute-start.29 = (bf16[2,64,2048]{2,1,0:T(8,128)(2,1)S(1)}, bf16[2,64,2048]{2,1,0:T(8,128)(2,1)S(1)}, u32[]{:S(2)}, u32[]{:S(2)}) collective-permute-start(bf16[2,64,2048]{2,1,0:T(8,128)(2,1)S(1)} %get-tuple-element.107), channel_id=1, source_target_pairs={{0,1},{1,0},{2,3},{3,2},{4,5},{5,4},{6,7},{7,6},{8,9},{9,8},{10,11... | collective-permute-start | bytes 1572872 | tf_op jit(solution)/shard_map/ppermute | solution.py:485
  117.6 32.8 %collective-permute-start.24 = (bf16[128,2048]{1,0:T(8,128)(2,1)S(1)}, bf16[128,2048]{1,0:T(8,128)(2,1)S(1)}, u32[]{:S(2)}, u32[]{:S(2)}) collective-permute-start(bf16[128,2048]{1,0:T(8,128)(2,1)S(1)} %expand.5.refs_4_), channel_id=1, source_target_pairs={{0,8},{1,9},{2,10},{3,11},{4,12},{5,13},{6,14},{7,15},{8,0},{9,1},... | collective-permute-start | bytes 1572872 | tf_op jit(solution)/shard_map/ppermute | solution.py:485
  121.1 29.4 %collective-permute-start.30 = (bf16[2,64,2048]{2,1,0:T(8,128)(2,1)S(1)}, bf16[2,64,2048]{2,1,0:T(8,128)(2,1)S(1)}, u32[]{:S(2)}, u32[]{:S(2)}) collective-permute-start(bf16[2,64,2048]{2,1,0:T(8,128)(2,1)S(1)} %get-tuple-element.108), channel_id=1, source_target_pairs={{0,2},{1,3},{2,0},{3,1},{4,6},{5,7},{6,4},{7,5},{8,10},{9,11},{10,... | collective-permute-start | bytes 1572872 | tf_op jit(solution)/shard_map/ppermute | solution.py:485
  122.1 28.4 %collective-permute-start.31 = (bf16[2,64,2048]{2,1,0:T(8,128)(2,1)S(1)}, bf16[2,64,2048]{2,1,0:T(8,128)(2,1)S(1)}, u32[]{:S(2)}, u32[]{:S(2)}) collective-permute-start(bf16[2,64,2048]{2,1,0:T(8,128)(2,1)S(1)} %get-tuple-element.109), channel_id=1, source_target_pairs={{0,3},{1,2},{2,1},{3,0},{4,7},{5,6},{6,5},{7,4},{8,11},{9,10},{10,... | collective-permute-start | bytes 1572872 | tf_op jit(solution)/shard_map/ppermute | solution.py:485
  123.3 21.9 %collective-permute-start.27 = (bf16[64,2048]{1,0:T(8,128)(2,1)S(1)}, bf16[64,2048]{1,0:T(8,128)(2,1)S(1)}, u32[]{:S(2)}, u32[]{:S(2)}) collective-permute-start(bf16[64,2048]{1,0:T(8,128)(2,1)S(1)} %get-tuple-element.106), channel_id=1, source_target_pairs={{0,3},{1,2},{2,1},{3,0},{4,7},{5,6},{6,5},{7,4},{8,11},{9,10},{10,... | collective-permute-start | bytes 786440 | tf_op jit(solution)/shard_map/ppermute | solution.py:485
  146.9 38.6 %collective-permute-start.28 = (bf16[128,2048]{1,0:T(8,128)(2,1)}, bf16[128,2048]{1,0:T(8,128)(2,1)}, u32[]{:S(2)}, u32[]{:S(2)}) collective-permute-start(bf16[128,2048]{1,0:T(8,128)(2,1)} %expand.6.refs_1_), channel_id=1, source_target_pairs={{0,12},{1,13},{2,14},{3,15},{4,8},{5,9},{6,10},{7,11},{8,4},{9,5},... | collective-permute-start | bytes 1572872 | tf_op jit(solution)/shard_map/ppermute | solution.py:485
  150.5 5.4 %copy-start = (f32[128,2048]{1,0:T(8,128)}, f32[128,2048]{1,0:T(8,128)S(1)}, u32[]{:S(2)}) copy-start(f32[128,2048]{1,0:T(8,128)S(1)} %total.2.refs_8_.own_ref) | copy-start | bytes 3145732
  155.9 11.3 %collective-permute-start.32 = (bf16[64,2048]{1,0:T(8,128)(2,1)S(1)}, bf16[64,2048]{1,0:T(8,128)(2,1)S(1)}, u32[]{:S(2)}, u32[]{:S(2)}) collective-permute-start(bf16[64,2048]{1,0:T(8,128)(2,1)S(1)} %get-tuple-element.111), channel_id=1, source_target_pairs={{0,1},{1,0},{2,3},{3,2},{4,5},{5,4},{6,7},{7,6},{8,9},{9,8},{10,11... | collective-permute-start | bytes 786440 | tf_op jit(solution)/shard_map/ppermute | solution.py:485
  157.7 9.5 %collective-permute-start.33 = (bf16[64,2048]{1,0:T(8,128)(2,1)S(1)}, bf16[64,2048]{1,0:T(8,128)(2,1)S(1)}, u32[]{:S(2)}, u32[]{:S(2)}) collective-permute-start(bf16[64,2048]{1,0:T(8,128)(2,1)S(1)} %get-tuple-element.112), channel_id=1, source_target_pairs={{0,2},{1,3},{2,0},{3,1},{4,6},{5,7},{6,4},{7,5},{8,10},{9,11},{10,... | collective-permute-start | bytes 786440 | tf_op jit(solution)/shard_map/ppermute | solution.py:485
  159.7 7.6 %collective-permute-start.34 = (bf16[64,2048]{1,0:T(8,128)(2,1)S(1)}, bf16[64,2048]{1,0:T(8,128)(2,1)S(1)}, u32[]{:S(2)}, u32[]{:S(2)}) collective-permute-start(bf16[64,2048]{1,0:T(8,128)(2,1)S(1)} %get-tuple-element.113), channel_id=1, source_target_pairs={{0,3},{1,2},{2,1},{3,0},{4,7},{5,6},{6,5},{7,4},{8,11},{9,10},{10,... | collective-permute-start | bytes 786440 | tf_op jit(solution)/shard_map/ppermute | solution.py:485
  167.2 8.0 %collective-permute-start.36 = (bf16[1024,2304]{1,0:T(8,128)(2,1)S(1)}, bf16[1024,2304]{1,0:T(8,128)(2,1)S(1)}, u32[]{:S(2)}, u32[]{:S(2)}) collective-permute-start(bf16[1024,2304]{1,0:T(8,128)(2,1)S(1)} %grads.2.refs_4_), channel_id=1, source_target_pairs={{0,16},{16,0},{1,17},{17,1},{2,18},{18,2},{3,19},{19,3},{4,20},{20... | collective-permute-start | bytes 14155784 | tf_op jit(solution)/shard_map/ppermute | solution.py:563
  168.3 17.2 %copy-start.1 = (f32[128,2048]{1,0:T(8,128)S(1)}, f32[128,2048]{1,0:T(8,128)}, u32[]{:S(2)}) copy-start(f32[128,2048]{1,0:T(8,128)} %copy-done) | copy-start | bytes 3145732
  168.4 17.2 %collective-permute-start.35 = (bf16[128,2048]{1,0:T(8,128)(2,1)S(1)}, bf16[128,2048]{1,0:T(8,128)(2,1)S(1)}, u32[]{:S(2)}, u32[]{:S(2)}) collective-permute-start(bf16[128,2048]{1,0:T(8,128)(2,1)S(1)} %expand.7.refs_17_), channel_id=1, source_target_pairs={{0,4},{1,5},{2,6},{3,7},{4,0},{5,1},{6,2},{7,3},{8,12},{9,13},{10,... | collective-permute-start | bytes 1572872 | tf_op jit(solution)/shard_map/ppermute | solution.py:485
where the time goes:
time: 188 us
  waiting for transfers between devices  75.2 us (40%)
  Pallas kernels  58.6 us (31%)
  starting transfers between devices  50.3 us (27%)
  local copies, waits for them, and re-layouts  2.41 us (1%)
    ppermute x36, waiting for transfers between devices, swap(): return lax.ppermute(value, 'expert', pairs)  68.5 us
    ppermute x36, starting transfers between devices, swap(): return lax.ppermute(value, 'expert', pairs)  50.2 us
    pallas_call x4, Pallas kernels, expert(): pl.pallas_call(functools.partial(expert_kernel, count, bool(begun)), in_s...  19.4 us
    pallas_call x2, Pallas kernels, grads(): pl.pallas_call(functools.partial(grads_kernel, len(saved), add), in_specs...  17.9 us
    pallas_call x5, Pallas kernels, select(): pl.pallas_call(functools.partial(select_kernel, count, cap, top, parts, l...  6.74 us
    ppermute x1, waiting for transfers between devices, local(): received = lax.ppermute(last, 'dp', [(0, 1), (1, 0)])  6.74 us
    pallas_call x4, Pallas kernels, expand(): pl.pallas_call(functools.partial(expand_kernel, count, top), grid=(1,), o...  4.93 us
    pallas_call x1, Pallas kernels, flip(): pl.pallas_call(flip_kernel, in_specs=[HBM] * 3 + [ANYWHERE], out_specs=[V...  4.67 us
  transfers between devices with their start and end apart: 37, of which 9 were waited for; matrix products, arithmetic and copies ran while one was open for 0% of the time, Pallas kernels for 30%

commit v1 on v0

--- a/solution.py
+++ b/solution.py
@@ -11,7 +11,7 @@
 F32 = jnp.float32
 META = 16
 PARAMS = pltpu.CompilerParams(vmem_limit_bytes=8 << 20)
-LARGE = pltpu.CompilerParams(vmem_limit_bytes=15 << 20)
+LARGE = pltpu.CompilerParams(vmem_limit_bytes=18 << 20)
 VMEM = pl.BlockSpec(memory_space=pltpu.VMEM)
 SMEM = pl.BlockSpec(memory_space=pltpu.SMEM)
 ANYWHERE = pl.BlockSpec(memory_space=pl.ANY)
@@ -278,9 +278,10 @@
 STEPS = 4
 
 
-def grads_kernel(planes, add, ids_ref, *refs):
+def grads_kernel(planes, add, based, ids_ref, *refs):
     saved = [refs[4 * which : 4 * which + 4] for which in range(planes)]
-    refs = refs[4 * planes :]
+    base = refs[4 * planes : 4 * planes + based]
+    refs = refs[4 * planes + based :]
     model, units = saved[0][0].shape[1], saved[0][3].shape[1]
     half = ids_ref[ids_ref.shape[0] - (2 if add else 1)]
     height, width = model // 2 // STEPS, model // STEPS
@@ -293,7 +294,8 @@
     else:
         _, sent_out, sent_ref, sems = refs
     own_units = pl.ds(pl.multiple_of(half * (units // 2), 128), units // 2)
-    flipped_hidden = [kept[3][:, own_units].T for kept in saved]
+    flipped_hidden = jnp.concatenate([kept[3][:, own_units].T for kept in saved], axis=1)
+    pair_units = jnp.concatenate([kept[2][...] for kept in saved], axis=0)
 
     def fetch(step):
         at = slice(step * height, (step + 1) * height)
@@ -323,10 +325,12 @@
         slot = step % 2
         across = slice(step * width, (step + 1) * width)
         own_rows = pl.ds(pl.multiple_of(half * (model // 2) + step * height, 128), height)
-        both, down = 0.0, 0.0
-        for flipped, (rows_ref, cots_ref, pair_units_ref, _) in zip(flipped_hidden, saved):
-            both = both + dot(rows_ref[:, own_rows].T, pair_units_ref[...])
-            down = down + dot(flipped, cots_ref[:, across])
+        flipped = jnp.concatenate([kept[0][:, own_rows].T for kept in saved], axis=1)
+        both = dot(flipped, pair_units)
+        down = dot(flipped_hidden, jnp.concatenate([kept[1][:, across] for kept in saved], axis=0))
+        if based:
+            both = both + base[0][step * height : (step + 1) * height, :]
+            down = down + base[1][:, across]
         if step >= 2:
             for copy in moves(step - 2):
                 copy.wait()
@@ -361,7 +365,7 @@
             copy.wait()
 
 
-def grads(ids, saved, received, flops, after):
+def grads(ids, saved, base, received, flops, after):
     model, units = saved[0][0].shape[1], saved[0][3].shape[1]
     height = model // 2 // STEPS
     sent_width = 3 * units
@@ -379,15 +383,50 @@
     if add:
         scratch.append(pltpu.SemaphoreType.DMA((2,)))
     return pl.pallas_call(
-        functools.partial(grads_kernel, len(saved), add),
-        in_specs=[SMEM] + [VMEM] * (4 * len(saved)) + [ANYWHERE] * (1 + add),
+        functools.partial(grads_kernel, len(saved), add, len(base)),
+        in_specs=[SMEM] + [VMEM] * (4 * len(saved) + len(base)) + [ANYWHERE] * (1 + add),
         out_specs=[HBM] * len(shapes) + [VMEM] * add,
         out_shape=[array(shape, dtype) for shape in shapes] + [array((8, 128), F32)] * add,
         scratch_shapes=scratch,
         compiler_params=LARGE,
         cost_estimate=estimate(flops),
         name="grads",
-    )(ids, *in_vmem(*(part for kept in saved for part in kept)), *received, after)
+    )(ids, *in_vmem(*(part for kept in saved for part in kept), *base), *received, after)
+
+
+def part_kernel(planes, ids_ref, *refs):
+    saved = [refs[4 * which : 4 * which + 4] for which in range(planes)]
+    both_ref, down_ref = refs[-2:]
+    model, units = saved[0][0].shape[1], saved[0][3].shape[1]
+    half = ids_ref[ids_ref.shape[0] - 1]
+    height, width = model // 2 // STEPS, model // STEPS
+    own_units = pl.ds(pl.multiple_of(half * (units // 2), 128), units // 2)
+    flipped_hidden = jnp.concatenate([kept[3][:, own_units].T for kept in saved], axis=1)
+    pair_units = jnp.concatenate([kept[2][...] for kept in saved], axis=0)
+    for step in range(STEPS):
+        across = slice(step * width, (step + 1) * width)
+        own_rows = pl.ds(pl.multiple_of(half * (model // 2) + step * height, 128), height)
+        flipped = jnp.concatenate([kept[0][:, own_rows].T for kept in saved], axis=1)
+        both_ref[step * height : (step + 1) * height, :] = dot(flipped, pair_units)
+        down_ref[:, across] = dot(
+            flipped_hidden, jnp.concatenate([kept[1][:, across] for kept in saved], axis=0)
+        )
+
+
+def part(ids, saved, flops, after):
+    model, units = saved[0][0].shape[1], saved[0][3].shape[1]
+    return pl.pallas_call(
+        functools.partial(part_kernel, len(saved)),
+        in_specs=[SMEM] + [VMEM] * (4 * len(saved)) + [ANYWHERE],
+        out_specs=[VMEM] * 2,
+        out_shape=[
+            resident(model // 2, 2 * units, dtype=F32),
+            resident(units // 2, model, dtype=F32),
+        ],
+        compiler_params=PARAMS,
+        cost_estimate=estimate(flops),
+        name="part",
+    )(ids, *in_vmem(*(part for kept in saved for part in kept)), after)
 
 
 def expand_kernel(count, top, ids_ref, meta_ref, *refs):
@@ -534,6 +573,7 @@
         return sent[0]
 
     last, weights, own, received, results = None, None, None, None, None
+    base, based = [], []
     for kind, plane, size in chain:
         after = [] if last is None else [last]
         flops = 1 << size
@@ -558,12 +598,17 @@
         elif kind == "total":
             own = last = total(own, partial[:plane], F32, flops, last)
             del partial[:plane]
+        elif kind == "part":
+            based = list(saved)
+            base = part(ids, [saved[other] for other in based], flops, last)
+            last = base[1]
         elif kind == "lend":
-            (last,) = grads(ids, [saved[other] for other in planes], [], flops, last)
+            rest = [saved[other] for other in planes if other not in based]
+            (last,) = grads(ids, rest, base, [], flops, last)
             received = lax.ppermute(last, "dp", [(0, 1), (1, 0)])
         elif kind == "finish":
             kept = [saved[other] for other in planes]
-            *results, last = grads(ids, kept, [received], flops, last)
+            *results, last = grads(ids, kept, [], [received], flops, last)
     input_grad = total(own, partial, BF16, 1, last)
     return (input_grad, *(value[None] for value in results))
 

time: 188 us -> 188 us (level)
  no operation moved by 1% of the time
where the time goes in v1:
time: 188 us
  waiting for transfers between devices  75.2 us (40%)
  Pallas kernels  58.8 us (31%)
  starting transfers between devices  50.3 us (27%)
  local copies, waits for them, and re-layouts  2.41 us (1%)
    ppermute x36, waiting for transfers between devices, swap(): return lax.ppermute(value, 'expert', pairs)  68.5 us
    ppermute x36, starting transfers between devices, swap(): return lax.ppermute(value, 'expert', pairs)  50.2 us
    pallas_call x4, Pallas kernels, expert(): pl.pallas_call(functools.partial(expert_kernel, count, bool(begun)), in_s...  19.5 us
    pallas_call x2, Pallas kernels, grads(): pl.pallas_call(functools.partial(grads_kernel, len(saved), add, len(base)...  18.1 us
    ppermute x1, waiting for transfers between devices, local(): received = lax.ppermute(last, 'dp', [(0, 1), (1, 0)])  6.74 us
    pallas_call x5, Pallas kernels, select(): pl.pallas_call(functools.partial(select_kernel, count, cap, top, parts, l...  6.74 us
    pallas_call x4, Pallas kernels, expand(): pl.pallas_call(functools.partial(expand_kernel, count, top), grid=(1,), o...  4.92 us
    pallas_call x1, Pallas kernels, flip(): pl.pallas_call(flip_kernel, in_specs=[HBM] * 3 + [ANYWHERE], out_specs=[V...  4.67 us
  transfers between devices with their start and end apart: 37, of which 9 were waited for; matrix products, arithmetic and copies ran while one was open for 0% of the time, Pallas kernels for 30%

profile of v1, /device:TPU:0, one launch (start us, length us, event | category | flops | bytes accessed | tf_op | source)
XLA Modules:
  0.0 187.8 jit_solution(16142956023509949940)
XLA Ops:
  0.6 0.7 copy-done.4
  1.3 0.7 copy-done.5
  2.0 1.1 pack.1.refs_0_.meta_ref
  3.1 4.1 %collective-permute-start.3 = (bf16[144,2048]{1,0:T(8,128)(2,1)S(1)}, bf16[144,2048]{1,0:T(8,128)(2,1)S(1)}, u32[]{:S(2)}, u32[]{:S(2)}) collective-permute-start(bf16[144,2048]{1,0:T(8,128)(2,1)S(1)} %pack.1.refs_0_.meta_ref), channel_id=1, source_target_pairs={{0,8},{1,9},{2,10},{3,11},{4,12},{5,13},{6,14},{7,15},{8,0},{9,1},... | collective-permute-start | bytes 1769480 | tf_op jit(solution)/shard_map/ppermute | solution.py:524
  7.3 1.0 copy-done.2
  8.3 1.4 select.5
  9.7 1.6 collective-permute-start
  11.2 1.5 collective-permute-start.1
  12.8 0.5 collective-permute-start.2
  13.2 4.7 %flip.1 = (bf16[2048,768]{1,0:T(8,128)(2,1)S(1)}, bf16[2048,768]{1,0:T(8,128)(2,1)S(1)}, bf16[1536,2048]{1,0:T(8,128)(2,1)S(1)}, bf16[2048,768]{1,0:T(8,128)(2,1)S(1)}) custom-call(bf16[2048,768]{1,0:T(8,128)(2,1)} %bitcast.12, bf16[2048,768]{1,0:T(8,128)(2,1)} %bitcast.13, bf16[768,2048]{1,0:T(8,128)(2,1)} %bitcast.14, ...), custom_call_target="tpu_custom_call" | custom-call | flops 1 | bytes 1 | tf_op jit(solution)/shard_map/flip/pallas_call | solution.py:173
  17.9 15.2 %collective-permute-done.3.refs_0_.refs_2_.meta_ref = bf16[144,2048]{1,0:T(8,128)(2,1)S(1)} collective-permute-done((bf16[144,2048]{1,0:T(8,128)(2,1)S(1)}, bf16[144,2048]{1,0:T(8,128)(2,1)S(1)}, u32[]{:S(2)}, u32[]{:S(2)}) %collective-permute-start.3) | collective-permute-done | bytes 589856 | tf_op jit(solution)/shard_map/ppermute | solution.py:524
  33.1 1.3 select.6
  34.4 1.6 collective-permute-start.7
  36.0 1.5 collective-permute-start.8
  37.5 0.4 collective-permute-start.9
  38.0 4.1 %collective-permute-start.14 = (bf16[144,2048]{1,0:T(8,128)(2,1)S(1)}, bf16[144,2048]{1,0:T(8,128)(2,1)S(1)}, u32[]{:S(2)}, u32[]{:S(2)}) collective-permute-start(bf16[144,2048]{1,0:T(8,128)(2,1)S(1)} %get-tuple-element.92), channel_id=1, source_target_pairs={{0,4},{1,5},{2,6},{3,7},{4,0},{5,1},{6,2},{7,3},{8,12},{9,13},{10,... | collective-permute-start | bytes 1769480 | tf_op jit(solution)/shard_map/ppermute | solution.py:524
  42.1 5.2 %expert.4 = (bf16[64,2048]{1,0:T(8,128)(2,1)S(1)}, bf16[64,2048]{1,0:T(8,128)(2,1)S(1)}, bf16[64,2048]{1,0:T(8,128)(2,1)S(1)}, bf16[64,2048]{1,0:T(8,128)(2,1)S(...) custom-call(bf16[2,64,2048]{2,1,0:T(8,128)(2,1)S(1)} %get-tuple-elem, ...), custom_call_target="tpu_custom_call" | custom-call | flops 1 | bytes 1 | tf_op jit(solution)/shard_map/expert/pallas_call | solution.py:266
  47.3 1.6 collective-permute-start.4
  48.9 1.5 collective-permute-start.5
  50.4 0.5 collective-permute-start.6
  50.9 1.8 begin.1
  52.7 3.9 %collective-permute-done.4.refs_1_ = bf16[64,2048]{1,0:T(8,128)(2,1)S(1)} collective-permute-done((bf16[64,2048]{1,0:T(8,128)(2,1)S(1)}, bf16[64,2048]{1,0:T(8,128)(2,1)S(1)}, u32[]{:S(2)}, u32[]{:S(2)}) %collective-permute-start.4) | collective-permute-done | bytes 262176 | tf_op jit(solution)/shard_map/ppermute | solution.py:524
  56.6 4.4 %collective-permute-done.5.refs_2_ = bf16[64,2048]{1,0:T(8,128)(2,1)S(1)} collective-permute-done((bf16[64,2048]{1,0:T(8,128)(2,1)S(1)}, bf16[64,2048]{1,0:T(8,128)(2,1)S(1)}, u32[]{:S(2)}, u32[]{:S(2)}) %collective-permute-start.5) | collective-permute-done | bytes 262176 | tf_op jit(solution)/shard_map/ppermute | solution.py:524
  61.1 1.0 expand.4.refs_3_.own_ref
  62.1 0.4 collective-permute-done.10.refs_1_.refs_2_
  62.5 1.3 select.7
  63.8 0.8 collective-permute-start.15
  64.7 0.5 collective-permute-start.11
  65.2 1.5 collective-permute-start.12
  66.7 1.4 collective-permute-start.13
  68.1 7.8 %collective-permute-done.15.refs_1_ = bf16[128,2048]{1,0:T(8,128)(2,1)S(1)} collective-permute-done((bf16[128,2048]{1,0:T(8,128)(2,1)S(1)}, bf16[128,2048]{1,0:T(8,128)(2,1)S(1)}, u32[]{:S(2)}, u32[]{:S(2)}) %collective-permute-start.15) | collective-permute-done | bytes 524320 | tf_op jit(solution)/shard_map/ppermute | solution.py:524
  75.9 1.4 select.8
  77.3 1.1 collective-permute-start.21
  78.4 1.5 collective-permute-start.22
  79.9 1.0 collective-permute-start.23
  80.9 0.3 collective-permute-start.20
  81.2 1.7 collective-permute-start.19
  82.9 3.6 %expert.5 = (bf16[64,2048]{1,0:T(8,128)(2,1)S(1)}, bf16[64,2048]{1,0:T(8,128)(2,1)S(1)}, bf16[64,2048]{1,0:T(8,128)(2,1)S(1)}, bf16[64,2048]{1,0:T(8,128)(2,1)S(...) custom-call(bf16[1,64,2048]{2,1,0:T(8,128)(2,1)S(1)} %get-tuple-element.87.refs_2_.re, ...), custom_call_target="tpu_custom_call" | custom-call | flops 536870912 | bytes 1 | tf_op jit(solution)/shard_map/expert/pallas_call | solution.py:266
  86.5 5.8 %collective-permute-done.21.refs_1_ = bf16[2,64,2048]{2,1,0:T(8,128)(2,1)S(1)} collective-permute-done((bf16[2,64,2048]{2,1,0:T(8,128)(2,1)S(1)}, bf16[2,64,2048]{2,1,0:T(8,128)(2,1)S(1)}, u32[]{:S(2)}, u32[]{:S(2)}) %collective-permute-start.21) | collective-permute-done | bytes 524320 | tf_op jit(solution)/shard_map/ppermute | solution.py:524
  92.3 1.0 collective-permute-start.16
  93.3 10.8 %collective-permute-done.22.refs_2_ = bf16[2,64,2048]{2,1,0:T(8,128)(2,1)S(1)} collective-permute-done((bf16[2,64,2048]{2,1,0:T(8,128)(2,1)S(1)}, bf16[2,64,2048]{2,1,0:T(8,128)(2,1)S(1)}, u32[]{:S(2)}, u32[]{:S(2)}) %collective-permute-start.22) | collective-permute-done | bytes 524320 | tf_op jit(solution)/shard_map/ppermute | solution.py:524
  104.1 1.7 collective-permute-start.17
  105.8 5.3 %expert.6 = (bf16[64,2048]{1,0:T(8,128)(2,1)S(1)}, bf16[64,2048]{1,0:T(8,128)(2,1)S(1)}, bf16[64,2048]{1,0:T(8,128)(2,1)S(1)}, bf16[64,2048]{1,0:T(8,128)(2,1)S(...) custom-call(bf16[2,64,2048]{2,1,0:T(8,128)(2,1)S(1)} %get-tuple-elem, ...), custom_call_target="tpu_custom_call" | custom-call | flops 1 | bytes 1 | tf_op jit(solution)/shard_map/expert/pallas_call | solution.py:266
  111.0 1.9 collective-permute-start.25
  112.9 1.7 collective-permute-start.26
  114.6 1.4 select.9
  116.0 0.6 collective-permute-start.29
  116.6 1.0 expand.5.refs_4_
  117.6 3.4 %collective-permute-start.24 = (bf16[128,2048]{1,0:T(8,128)(2,1)S(1)}, bf16[128,2048]{1,0:T(8,128)(2,1)S(1)}, u32[]{:S(2)}, u32[]{:S(2)}) collective-permute-start(bf16[128,2048]{1,0:T(8,128)(2,1)S(1)} %expand.5.refs_4_), channel_id=1, source_target_pairs={{0,8},{1,9},{2,10},{3,11},{4,12},{5,13},{6,14},{7,15},{8,0},{9,1},... | collective-permute-start | bytes 1572872 | tf_op jit(solution)/shard_map/ppermute | solution.py:524
  121.1 1.0 collective-permute-start.30
  122.1 1.2 collective-permute-start.31
  123.3 1.8 collective-permute-start.27
  125.0 20.1 %collective-permute-done.27.refs_3_ = bf16[64,2048]{1,0:T(8,128)(2,1)S(1)} collective-permute-done((bf16[64,2048]{1,0:T(8,128)(2,1)S(1)}, bf16[64,2048]{1,0:T(8,128)(2,1)S(1)}, u32[]{:S(2)}, u32[]{:S(2)}) %collective-permute-start.27) | collective-permute-done | bytes 262176 | tf_op jit(solution)/shard_map/ppermute | solution.py:524
  145.1 1.8 expand.6.refs_1_
  146.9 3.5 %collective-permute-start.28 = (bf16[128,2048]{1,0:T(8,128)(2,1)}, bf16[128,2048]{1,0:T(8,128)(2,1)}, u32[]{:S(2)}, u32[]{:S(2)}) collective-permute-start(bf16[128,2048]{1,0:T(8,128)(2,1)} %expand.6.refs_1_), channel_id=1, source_target_pairs={{0,12},{1,13},{2,14},{3,15},{4,8},{5,9},{6,10},{7,11},{8,4},{9,5},... | collective-permute-start | bytes 1572872 | tf_op jit(solution)/shard_map/ppermute | solution.py:524
  150.4 0.1 total.2.refs_8_.own_ref
  150.5 5.4 %expert.7 = (bf16[64,2048]{1,0:T(8,128)(2,1)S(1)}, bf16[64,2048]{1,0:T(8,128)(2,1)S(1)}, bf16[64,2048]{1,0:T(8,128)(2,1)S(1)}, bf16[64,2048]{1,0:T(8,128)(2,1)S(...) custom-call(bf16[2,64,2048]{2,1,0:T(8,128)(2,1)S(1)} %get-tuple-elem, ...), custom_call_target="tpu_custom_call" | custom-call | flops 1 | bytes 1 | tf_op jit(solution)/shard_map/expert/pallas_call | solution.py:266
  156.0 1.8 collective-permute-start.32
  157.8 1.9 %collective-permute-start.33 = (bf16[64,2048]{1,0:T(8,128)(2,1)S(1)}, bf16[64,2048]{1,0:T(8,128)(2,1)S(1)}, u32[]{:S(2)}, u32[]{:S(2)}) collective-permute-start(bf16[64,2048]{1,0:T(8,128)(2,1)S(1)} %get-tuple-element.112), channel_id=1, source_target_pairs={{0,2},{1,3},{2,0},{3,1},{4,6},{5,7},{6,4},{7,5},{8,10},{9,11},{10,... | collective-permute-start | bytes 786440 | tf_op jit(solution)/shard_map/ppermute | solution.py:524
  159.7 7.6 %grads.2.refs_4_ = bf16[1024,2304]{1,0:T(8,128)(2,1)S(1)} custom-call(s32[6]{0:T(128)S(1)} %pad_add_fusion.ids_ref, bf16[256,2048]{1,0:T(8,128)(2,1)S(1)} %get-tuple-element.114.refs_0_, bf16[256,2048]{1,0:T(8,128)(2,1)S(1)} %get-tuple-element.115.refs_1_, bf16[256,1536]{1,0:T(8,128)(2,1)S(1)} %get-tuple-element.116.refs_2_, ...), custom_call_target="tpu_custom_call" | custom-call | flops 137438953472 | bytes 1 | tf_op jit(solution)/shard_map/grads/pallas_call | solution.py:385
  167.4 1.0 expand.7.refs_17_
  168.5 6.7 %collective-permute-done.36.refs_16_ = bf16[1024,2304]{1,0:T(8,128)(2,1)S(1)} collective-permute-done((bf16[1024,2304]{1,0:T(8,128)(2,1)S(1)}, bf16[1024,2304]{1,0:T(8,128)(2,1)S(1)}, u32[]{:S(2)}, u32[]{:S(2)}) %collective-permute-start.36) | collective-permute-done | bytes 4718624 | tf_op jit(solution)/shard_map/ppermute | solution.py:608
  175.3 10.5 %grads.3 = (f32[1024,768]{1,0:T(8,128)}, f32[1024,768]{1,0:T(8,128)}, f32[384,2048]{1,0:T(8,128)}, f32[8,128]{1,0:T(8,128)S(1)}) custom-call(s32[6]{0:T(128)S(1)} %pad_add_fusion.ids_ref, bf16[256,2048]{1,0:T(8,128)(2,1)S(1)} %get-tuple-element.114.refs_0_, bf16[256,2048]{1,0:T(8,128)(2,1)S(1)} %get-tuple-element.115.refs_1_, ...), custom_call_target="tpu_custom_call" | custom-call | flops 137438953472 | bytes 1 | tf_op jit(solution)/shard_map/grads/pallas_call | solution.py:385
  185.8 2.0 %total.3 = bf16[128,2048]{1,0:T(8,128)(2,1)} custom-call(f32[128,2048]{1,0:T(8,128)S(1)} %copy-done.1, bf16[128,2048]{1,0:T(8,128)(2,1)} %collective-permute-done.28.refs_0_, bf16[128,2048]{1,0:T(8,128)(2,1)S(1)} %collective-permute-done.35.refs_1_, f32[8,128]{1,0:T(8,128)S(1)} %get-tuple-element.130.refs_2_), custom_call_target="tpu_custom_call" | custom-call | flops 1 | bytes 1 | tf_op jit(solution)/shard_map/total/pallas_call | solution.py:471
  (44 shorter events, 0.3 us)
Async XLA Ops:
  0.6 0.7 copy-start.4
  1.3 0.7 copy-start.5
  3.1 30.1 %collective-permute-start.3 = (bf16[144,2048]{1,0:T(8,128)(2,1)S(1)}, bf16[144,2048]{1,0:T(8,128)(2,1)S(1)}, u32[]{:S(2)}, u32[]{:S(2)}) collective-permute-start(bf16[144,2048]{1,0:T(8,128)(2,1)S(1)} %pack.1.refs_0_.meta_ref), channel_id=1, source_target_pairs={{0,8},{1,9},{2,10},{3,11},{4,12},{5,13},{6,14},{7,15},{8,0},{9,1},... | collective-permute-start | bytes 1769480 | tf_op jit(solution)/shard_map/ppermute | solution.py:524
  7.2 1.0 copy-start.2
  9.7 27.8 %collective-permute-start = (bf16[2,64,2048]{2,1,0:T(8,128)(2,1)S(1)}, bf16[2,64,2048]{2,1,0:T(8,128)(2,1)S(1)}, u32[]{:S(2)}, u32[]{:S(2)}) collective-permute-start(bf16[2,64,2048]{2,1,0:T(8,128)(2,1)S(1)} %get-tuple-element.70), channel_id=1, source_target_pairs={{0,1},{1,0},{2,3},{3,2},{4,5},{5,4},{6,7},{7,6},{8,9},{9,8},{10,11... | collective-permute-start | bytes 1572872 | tf_op jit(solution)/shard_map/ppermute | solution.py:524
  11.2 26.7 %collective-permute-start.1 = (bf16[2,64,2048]{2,1,0:T(8,128)(2,1)S(1)}, bf16[2,64,2048]{2,1,0:T(8,128)(2,1)S(1)}, u32[]{:S(2)}, u32[]{:S(2)}) collective-permute-start(bf16[2,64,2048]{2,1,0:T(8,128)(2,1)S(1)} %get-tuple-element.71), channel_id=1, source_target_pairs={{0,2},{1,3},{2,0},{3,1},{4,6},{5,7},{6,4},{7,5},{8,10},{9,11},{10,... | collective-permute-start | bytes 1572872 | tf_op jit(solution)/shard_map/ppermute | solution.py:524
  12.8 25.2 %collective-permute-start.2 = (bf16[2,64,2048]{2,1,0:T(8,128)(2,1)S(1)}, bf16[2,64,2048]{2,1,0:T(8,128)(2,1)S(1)}, u32[]{:S(2)}, u32[]{:S(2)}) collective-permute-start(bf16[2,64,2048]{2,1,0:T(8,128)(2,1)S(1)} %get-tuple-element.72), channel_id=1, source_target_pairs={{0,3},{1,2},{2,1},{3,0},{4,7},{5,6},{6,5},{7,4},{8,11},{9,10},{10,... | collective-permute-start | bytes 1572872 | tf_op jit(solution)/shard_map/ppermute | solution.py:524
  34.4 12.9 %collective-permute-start.7 = (bf16[1,64,2048]{2,1,0:T(8,128)(2,1)S(1)}, bf16[1,64,2048]{2,1,0:T(8,128)(2,1)S(1)}, u32[]{:S(2)}, u32[]{:S(2)}) collective-permute-start(bf16[1,64,2048]{2,1,0:T(8,128)(2,1)S(1)} %get-tuple-element.82), channel_id=1, source_target_pairs={{0,1},{1,0},{2,3},{3,2},{4,5},{5,4},{6,7},{7,6},{8,9},{9,8},{10,11... | collective-permute-start | bytes 786440 | tf_op jit(solution)/shard_map/ppermute | solution.py:524
  36.0 12.9 %collective-permute-start.8 = (bf16[1,64,2048]{2,1,0:T(8,128)(2,1)S(1)}, bf16[1,64,2048]{2,1,0:T(8,128)(2,1)S(1)}, u32[]{:S(2)}, u32[]{:S(2)}) collective-permute-start(bf16[1,64,2048]{2,1,0:T(8,128)(2,1)S(1)} %get-tuple-element.83), channel_id=1, source_target_pairs={{0,2},{1,3},{2,0},{3,1},{4,6},{5,7},{6,4},{7,5},{8,10},{9,11},{10,... | collective-permute-start | bytes 786440 | tf_op jit(solution)/shard_map/ppermute | solution.py:524
  37.5 12.9 %collective-permute-start.9 = (bf16[1,64,2048]{2,1,0:T(8,128)(2,1)S(1)}, bf16[1,64,2048]{2,1,0:T(8,128)(2,1)S(1)}, u32[]{:S(2)}, u32[]{:S(2)}) collective-permute-start(bf16[1,64,2048]{2,1,0:T(8,128)(2,1)S(1)} %get-tuple-element.84), channel_id=1, source_target_pairs={{0,3},{1,2},{2,1},{3,0},{4,7},{5,6},{6,5},{7,4},{8,11},{9,10},{10,... | collective-permute-start | bytes 786440 | tf_op jit(solution)/shard_map/ppermute | solution.py:524
  38.0 24.5 %collective-permute-start.10 = (bf16[128,2048]{1,0:T(8,128)(2,1)S(1)}, bf16[128,2048]{1,0:T(8,128)(2,1)S(1)}, u32[]{:S(2)}, u32[]{:S(2)}) collective-permute-start(bf16[128,2048]{1,0:T(8,128)(2,1)S(1)} %get-tuple-element.86), channel_id=1, source_target_pairs={{0,8},{1,9},{2,10},{3,11},{4,12},{5,13},{6,14},{7,15},{8,0},{9,1},... | collective-permute-start | bytes 1572872 | tf_op jit(solution)/shard_map/ppermute | solution.py:524
  38.0 30.2 %collective-permute-start.14 = (bf16[144,2048]{1,0:T(8,128)(2,1)S(1)}, bf16[144,2048]{1,0:T(8,128)(2,1)S(1)}, u32[]{:S(2)}, u32[]{:S(2)}) collective-permute-start(bf16[144,2048]{1,0:T(8,128)(2,1)S(1)} %get-tuple-element.92), channel_id=1, source_target_pairs={{0,4},{1,5},{2,6},{3,7},{4,0},{5,1},{6,2},{7,3},{8,12},{9,13},{10,... | collective-permute-start | bytes 1769480 | tf_op jit(solution)/shard_map/ppermute | solution.py:524
  47.3 9.3 %collective-permute-start.4 = (bf16[64,2048]{1,0:T(8,128)(2,1)S(1)}, bf16[64,2048]{1,0:T(8,128)(2,1)S(1)}, u32[]{:S(2)}, u32[]{:S(2)}) collective-permute-start(bf16[64,2048]{1,0:T(8,128)(2,1)S(1)} %get-tuple-element.79), channel_id=1, source_target_pairs={{0,1},{1,0},{2,3},{3,2},{4,5},{5,4},{6,7},{7,6},{8,9},{9,8},{10,11... | collective-permute-start | bytes 786440 | tf_op jit(solution)/shard_map/ppermute | solution.py:524
  48.9 12.2 %collective-permute-start.5 = (bf16[64,2048]{1,0:T(8,128)(2,1)S(1)}, bf16[64,2048]{1,0:T(8,128)(2,1)S(1)}, u32[]{:S(2)}, u32[]{:S(2)}) collective-permute-start(bf16[64,2048]{1,0:T(8,128)(2,1)S(1)} %get-tuple-element.80), channel_id=1, source_target_pairs={{0,2},{1,3},{2,0},{3,1},{4,6},{5,7},{6,4},{7,5},{8,10},{9,11},{10,... | collective-permute-start | bytes 786440 | tf_op jit(solution)/shard_map/ppermute | solution.py:524
  50.4 10.6 %collective-permute-start.6 = (bf16[64,2048]{1,0:T(8,128)(2,1)S(1)}, bf16[64,2048]{1,0:T(8,128)(2,1)S(1)}, u32[]{:S(2)}, u32[]{:S(2)}) collective-permute-start(bf16[64,2048]{1,0:T(8,128)(2,1)S(1)} %get-tuple-element.81), channel_id=1, source_target_pairs={{0,3},{1,2},{2,1},{3,0},{4,7},{5,6},{6,5},{7,4},{8,11},{9,10},{10,... | collective-permute-start | bytes 786440 | tf_op jit(solution)/shard_map/ppermute | solution.py:524
  61.1 19.8 %copy-start.3 = (bf16[128,2048]{1,0:T(8,128)(2,1)S(1)}, bf16[128,2048]{1,0:T(8,128)(2,1)}, u32[]{:S(2)}) copy-start(bf16[128,2048]{1,0:T(8,128)(2,1)} %refs_3_.1) | copy-start | bytes 1572868
  63.8 12.1 %collective-permute-start.15 = (bf16[128,2048]{1,0:T(8,128)(2,1)S(1)}, bf16[128,2048]{1,0:T(8,128)(2,1)S(1)}, u32[]{:S(2)}, u32[]{:S(2)}) collective-permute-start(bf16[128,2048]{1,0:T(8,128)(2,1)S(1)} %get-tuple-element.93), channel_id=1, source_target_pairs={{0,4},{1,5},{2,6},{3,7},{4,0},{5,1},{6,2},{7,3},{8,12},{9,13},{10,... | collective-permute-start | bytes 1572872 | tf_op jit(solution)/shard_map/ppermute | solution.py:524
  64.7 15.3 %collective-permute-start.11 = (bf16[1,64,2048]{2,1,0:T(8,128)(2,1)S(1)}, bf16[1,64,2048]{2,1,0:T(8,128)(2,1)S(1)}, u32[]{:S(2)}, u32[]{:S(2)}) collective-permute-start(bf16[1,64,2048]{2,1,0:T(8,128)(2,1)S(1)} %get-tuple-element.88), channel_id=1, source_target_pairs={{0,1},{1,0},{2,3},{3,2},{4,5},{5,4},{6,7},{7,6},{8,9},{9,8},{10,11... | collective-permute-start | bytes 786440 | tf_op jit(solution)/shard_map/ppermute | solution.py:524
  65.2 15.7 %collective-permute-start.12 = (bf16[1,64,2048]{2,1,0:T(8,128)(2,1)S(1)}, bf16[1,64,2048]{2,1,0:T(8,128)(2,1)S(1)}, u32[]{:S(2)}, u32[]{:S(2)}) collective-permute-start(bf16[1,64,2048]{2,1,0:T(8,128)(2,1)S(1)} %get-tuple-element.89), channel_id=1, source_target_pairs={{0,2},{1,3},{2,0},{3,1},{4,6},{5,7},{6,4},{7,5},{8,10},{9,11},{10,... | collective-permute-start | bytes 786440 | tf_op jit(solution)/shard_map/ppermute | solution.py:524
  66.7 14.5 %collective-permute-start.13 = (bf16[1,64,2048]{2,1,0:T(8,128)(2,1)S(1)}, bf16[1,64,2048]{2,1,0:T(8,128)(2,1)S(1)}, u32[]{:S(2)}, u32[]{:S(2)}) collective-permute-start(bf16[1,64,2048]{2,1,0:T(8,128)(2,1)S(1)} %get-tuple-element.90), channel_id=1, source_target_pairs={{0,3},{1,2},{2,1},{3,0},{4,7},{5,6},{6,5},{7,4},{8,11},{9,10},{10,... | collective-permute-start | bytes 786440 | tf_op jit(solution)/shard_map/ppermute | solution.py:524
  77.3 14.9 %collective-permute-start.21 = (bf16[2,64,2048]{2,1,0:T(8,128)(2,1)S(1)}, bf16[2,64,2048]{2,1,0:T(8,128)(2,1)S(1)}, u32[]{:S(2)}, u32[]{:S(2)}) collective-permute-start(bf16[2,64,2048]{2,1,0:T(8,128)(2,1)S(1)} %get-tuple-element.99), channel_id=1, source_target_pairs={{0,1},{1,0},{2,3},{3,2},{4,5},{5,4},{6,7},{7,6},{8,9},{9,8},{10,11... | collective-permute-start | bytes 1572872 | tf_op jit(solution)/shard_map/ppermute | solution.py:524
  78.4 25.7 %collective-permute-start.22 = (bf16[2,64,2048]{2,1,0:T(8,128)(2,1)S(1)}, bf16[2,64,2048]{2,1,0:T(8,128)(2,1)S(1)}, u32[]{:S(2)}, u32[]{:S(2)}) collective-permute-start(bf16[2,64,2048]{2,1,0:T(8,128)(2,1)S(1)} %get-tuple-element.100), channel_id=1, source_target_pairs={{0,2},{1,3},{2,0},{3,1},{4,6},{5,7},{6,4},{7,5},{8,10},{9,11},{10,... | collective-permute-start | bytes 1572872 | tf_op jit(solution)/shard_map/ppermute | solution.py:524
  79.9 25.8 %collective-permute-start.23 = (bf16[2,64,2048]{2,1,0:T(8,128)(2,1)S(1)}, bf16[2,64,2048]{2,1,0:T(8,128)(2,1)S(1)}, u32[]{:S(2)}, u32[]{:S(2)}) collective-permute-start(bf16[2,64,2048]{2,1,0:T(8,128)(2,1)S(1)} %get-tuple-element.101), channel_id=1, source_target_pairs={{0,3},{1,2},{2,1},{3,0},{4,7},{5,6},{6,5},{7,4},{8,11},{9,10},{10,... | collective-permute-start | bytes 1572872 | tf_op jit(solution)/shard_map/ppermute | solution.py:524
  80.9 30.1 %collective-permute-start.20 = (bf16[128,2048]{1,0:T(8,128)(2,1)S(1)}, bf16[128,2048]{1,0:T(8,128)(2,1)S(1)}, u32[]{:S(2)}, u32[]{:S(2)}) collective-permute-start(bf16[128,2048]{1,0:T(8,128)(2,1)S(1)} %copy-done.3), channel_id=1, source_target_pairs={{0,4},{1,5},{2,6},{3,7},{4,0},{5,1},{6,2},{7,3},{8,12},{9,13},{10,... | collective-permute-start | bytes 1572872 | tf_op jit(solution)/shard_map/ppermute | solution.py:524
  81.2 31.7 %collective-permute-start.19 = (bf16[144,2048]{1,0:T(8,128)(2,1)S(1)}, bf16[144,2048]{1,0:T(8,128)(2,1)S(1)}, u32[]{:S(2)}, u32[]{:S(2)}) collective-permute-start(bf16[144,2048]{1,0:T(8,128)(2,1)S(1)} %pack.1.refs_0_.meta_ref), channel_id=1, source_target_pairs={{0,4},{1,5},{2,6},{3,7},{4,0},{5,1},{6,2},{7,3},{8,12},{9,13},{10,... | collective-permute-start | bytes 1769480 | tf_op jit(solution)/shard_map/ppermute | solution.py:524
  92.3 23.7 %collective-permute-start.16 = (bf16[64,2048]{1,0:T(8,128)(2,1)S(1)}, bf16[64,2048]{1,0:T(8,128)(2,1)S(1)}, u32[]{:S(2)}, u32[]{:S(2)}) collective-permute-start(bf16[64,2048]{1,0:T(8,128)(2,1)S(1)} %get-tuple-element.96), channel_id=1, source_target_pairs={{0,1},{1,0},{2,3},{3,2},{4,5},{5,4},{6,7},{7,6},{8,9},{9,8},{10,11... | collective-permute-start | bytes 786440 | tf_op jit(solution)/shard_map/ppermute | solution.py:524
  104.1 12.5 %collective-permute-start.17 = (bf16[64,2048]{1,0:T(8,128)(2,1)S(1)}, bf16[64,2048]{1,0:T(8,128)(2,1)S(1)}, u32[]{:S(2)}, u32[]{:S(2)}) collective-permute-start(bf16[64,2048]{1,0:T(8,128)(2,1)S(1)} %get-tuple-element.97), channel_id=1, source_target_pairs={{0,2},{1,3},{2,0},{3,1},{4,6},{5,7},{6,4},{7,5},{8,10},{9,11},{10,... | collective-permute-start | bytes 786440 | tf_op jit(solution)/shard_map/ppermute | solution.py:524
  105.8 10.9 %collective-permute-start.18 = (bf16[64,2048]{1,0:T(8,128)(2,1)S(1)}, bf16[64,2048]{1,0:T(8,128)(2,1)S(1)}, u32[]{:S(2)}, u32[]{:S(2)}) collective-permute-start(bf16[64,2048]{1,0:T(8,128)(2,1)S(1)} %get-tuple-element.98), channel_id=1, source_target_pairs={{0,3},{1,2},{2,1},{3,0},{4,7},{5,6},{6,5},{7,4},{8,11},{9,10},{10,... | collective-permute-start | bytes 786440 | tf_op jit(solution)/shard_map/ppermute | solution.py:524
  111.0 11.1 %collective-permute-start.25 = (bf16[64,2048]{1,0:T(8,128)(2,1)S(1)}, bf16[64,2048]{1,0:T(8,128)(2,1)S(1)}, u32[]{:S(2)}, u32[]{:S(2)}) collective-permute-start(bf16[64,2048]{1,0:T(8,128)(2,1)S(1)} %get-tuple-element.104), channel_id=1, source_target_pairs={{0,1},{1,0},{2,3},{3,2},{4,5},{5,4},{6,7},{7,6},{8,9},{9,8},{10,11... | collective-permute-start | bytes 786440 | tf_op jit(solution)/shard_map/ppermute | solution.py:524
  112.9 10.4 %collective-permute-start.26 = (bf16[64,2048]{1,0:T(8,128)(2,1)S(1)}, bf16[64,2048]{1,0:T(8,128)(2,1)S(1)}, u32[]{:S(2)}, u32[]{:S(2)}) collective-permute-start(bf16[64,2048]{1,0:T(8,128)(2,1)S(1)} %get-tuple-element.105), channel_id=1, source_target_pairs={{0,2},{1,3},{2,0},{3,1},{4,6},{5,7},{6,4},{7,5},{8,10},{9,11},{10,... | collective-permute-start | bytes 786440 | tf_op jit(solution)/shard_map/ppermute | solution.py:524
  116.0 34.5 %collective-permute-start.29 = (bf16[2,64,2048]{2,1,0:T(8,128)(2,1)S(1)}, bf16[2,64,2048]{2,1,0:T(8,128)(2,1)S(1)}, u32[]{:S(2)}, u32[]{:S(2)}) collective-permute-start(bf16[2,64,2048]{2,1,0:T(8,128)(2,1)S(1)} %get-tuple-element.107), channel_id=1, source_target_pairs={{0,1},{1,0},{2,3},{3,2},{4,5},{5,4},{6,7},{7,6},{8,9},{9,8},{10,11... | collective-permute-start | bytes 1572872 | tf_op jit(solution)/shard_map/ppermute | solution.py:524
  117.6 32.8 %collective-permute-start.24 = (bf16[128,2048]{1,0:T(8,128)(2,1)S(1)}, bf16[128,2048]{1,0:T(8,128)(2,1)S(1)}, u32[]{:S(2)}, u32[]{:S(2)}) collective-permute-start(bf16[128,2048]{1,0:T(8,128)(2,1)S(1)} %expand.5.refs_4_), channel_id=1, source_target_pairs={{0,8},{1,9},{2,10},{3,11},{4,12},{5,13},{6,14},{7,15},{8,0},{9,1},... | collective-permute-start | bytes 1572872 | tf_op jit(solution)/shard_map/ppermute | solution.py:524
  121.1 29.4 %collective-permute-start.30 = (bf16[2,64,2048]{2,1,0:T(8,128)(2,1)S(1)}, bf16[2,64,2048]{2,1,0:T(8,128)(2,1)S(1)}, u32[]{:S(2)}, u32[]{:S(2)}) collective-permute-start(bf16[2,64,2048]{2,1,0:T(8,128)(2,1)S(1)} %get-tuple-element.108), channel_id=1, source_target_pairs={{0,2},{1,3},{2,0},{3,1},{4,6},{5,7},{6,4},{7,5},{8,10},{9,11},{10,... | collective-permute-start | bytes 1572872 | tf_op jit(solution)/shard_map/ppermute | solution.py:524
  122.1 28.4 %collective-permute-start.31 = (bf16[2,64,2048]{2,1,0:T(8,128)(2,1)S(1)}, bf16[2,64,2048]{2,1,0:T(8,128)(2,1)S(1)}, u32[]{:S(2)}, u32[]{:S(2)}) collective-permute-start(bf16[2,64,2048]{2,1,0:T(8,128)(2,1)S(1)} %get-tuple-element.109), channel_id=1, source_target_pairs={{0,3},{1,2},{2,1},{3,0},{4,7},{5,6},{6,5},{7,4},{8,11},{9,10},{10,... | collective-permute-start | bytes 1572872 | tf_op jit(solution)/shard_map/ppermute | solution.py:524
  123.3 21.9 %collective-permute-start.27 = (bf16[64,2048]{1,0:T(8,128)(2,1)S(1)}, bf16[64,2048]{1,0:T(8,128)(2,1)S(1)}, u32[]{:S(2)}, u32[]{:S(2)}) collective-permute-start(bf16[64,2048]{1,0:T(8,128)(2,1)S(1)} %get-tuple-element.106), channel_id=1, source_target_pairs={{0,3},{1,2},{2,1},{3,0},{4,7},{5,6},{6,5},{7,4},{8,11},{9,10},{10,... | collective-permute-start | bytes 786440 | tf_op jit(solution)/shard_map/ppermute | solution.py:524
  146.9 38.8 %collective-permute-start.28 = (bf16[128,2048]{1,0:T(8,128)(2,1)}, bf16[128,2048]{1,0:T(8,128)(2,1)}, u32[]{:S(2)}, u32[]{:S(2)}) collective-permute-start(bf16[128,2048]{1,0:T(8,128)(2,1)} %expand.6.refs_1_), channel_id=1, source_target_pairs={{0,12},{1,13},{2,14},{3,15},{4,8},{5,9},{6,10},{7,11},{8,4},{9,5},... | collective-permute-start | bytes 1572872 | tf_op jit(solution)/shard_map/ppermute | solution.py:524
  150.5 5.5 %copy-start = (f32[128,2048]{1,0:T(8,128)}, f32[128,2048]{1,0:T(8,128)S(1)}, u32[]{:S(2)}) copy-start(f32[128,2048]{1,0:T(8,128)S(1)} %total.2.refs_8_.own_ref) | copy-start | bytes 3145732
  156.0 11.4 %collective-permute-start.32 = (bf16[64,2048]{1,0:T(8,128)(2,1)S(1)}, bf16[64,2048]{1,0:T(8,128)(2,1)S(1)}, u32[]{:S(2)}, u32[]{:S(2)}) collective-permute-start(bf16[64,2048]{1,0:T(8,128)(2,1)S(1)} %get-tuple-element.111), channel_id=1, source_target_pairs={{0,1},{1,0},{2,3},{3,2},{4,5},{5,4},{6,7},{7,6},{8,9},{9,8},{10,11... | collective-permute-start | bytes 786440 | tf_op jit(solution)/shard_map/ppermute | solution.py:524
  157.8 9.6 %collective-permute-start.33 = (bf16[64,2048]{1,0:T(8,128)(2,1)S(1)}, bf16[64,2048]{1,0:T(8,128)(2,1)S(1)}, u32[]{:S(2)}, u32[]{:S(2)}) collective-permute-start(bf16[64,2048]{1,0:T(8,128)(2,1)S(1)} %get-tuple-element.112), channel_id=1, source_target_pairs={{0,2},{1,3},{2,0},{3,1},{4,6},{5,7},{6,4},{7,5},{8,10},{9,11},{10,... | collective-permute-start | bytes 786440 | tf_op jit(solution)/shard_map/ppermute | solution.py:524
  159.7 7.7 %collective-permute-start.34 = (bf16[64,2048]{1,0:T(8,128)(2,1)S(1)}, bf16[64,2048]{1,0:T(8,128)(2,1)S(1)}, u32[]{:S(2)}, u32[]{:S(2)}) collective-permute-start(bf16[64,2048]{1,0:T(8,128)(2,1)S(1)} %get-tuple-element.113), channel_id=1, source_target_pairs={{0,3},{1,2},{2,1},{3,0},{4,7},{5,6},{6,5},{7,4},{8,11},{9,10},{10,... | collective-permute-start | bytes 786440 | tf_op jit(solution)/shard_map/ppermute | solution.py:524
  167.3 8.0 %collective-permute-start.36 = (bf16[1024,2304]{1,0:T(8,128)(2,1)S(1)}, bf16[1024,2304]{1,0:T(8,128)(2,1)S(1)}, u32[]{:S(2)}, u32[]{:S(2)}) collective-permute-start(bf16[1024,2304]{1,0:T(8,128)(2,1)S(1)} %grads.2.refs_4_), channel_id=1, source_target_pairs={{0,16},{16,0},{1,17},{17,1},{2,18},{18,2},{3,19},{19,3},{4,20},{20... | collective-permute-start | bytes 14155784 | tf_op jit(solution)/shard_map/ppermute | solution.py:608
  168.4 17.4 %copy-start.1 = (f32[128,2048]{1,0:T(8,128)S(1)}, f32[128,2048]{1,0:T(8,128)}, u32[]{:S(2)}) copy-start(f32[128,2048]{1,0:T(8,128)} %copy-done) | copy-start | bytes 3145732
  168.4 17.3 %collective-permute-start.35 = (bf16[128,2048]{1,0:T(8,128)(2,1)S(1)}, bf16[128,2048]{1,0:T(8,128)(2,1)S(1)}, u32[]{:S(2)}, u32[]{:S(2)}) collective-permute-start(bf16[128,2048]{1,0:T(8,128)(2,1)S(1)} %expand.7.refs_17_), channel_id=1, source_target_pairs={{0,4},{1,5},{2,6},{3,7},{4,0},{5,1},{6,2},{7,3},{8,12},{9,13},{10,... | collective-permute-start | bytes 1572872 | tf_op jit(solution)/shard_map/ppermute | solution.py:524

commit v2 on v1

--- a/solution.py
+++ b/solution.py
@@ -278,127 +278,64 @@
 STEPS = 4
 
 
-def grads_kernel(planes, add, based, ids_ref, *refs):
+def lend_kernel(planes, ids_ref, *refs):
     saved = [refs[4 * which : 4 * which + 4] for which in range(planes)]
-    base = refs[4 * planes : 4 * planes + based]
-    refs = refs[4 * planes + based :]
+    sent_out, sent_ref, sems = refs[-3:]
     model, units = saved[0][0].shape[1], saved[0][3].shape[1]
-    half = ids_ref[ids_ref.shape[0] - (2 if add else 1)]
+    half = ids_ref[ids_ref.shape[0] - 1]
     height, width = model // 2 // STEPS, model // STEPS
     rest = units // 2 - height
     fold = height // rest
     part = width // fold
-    if add:
-        other_in, _, gate_out, up_out, down_out, token, gate_ref, up_ref, down_ref, other_ref, sems, other_sems = refs
-        token[...] = jnp.zeros(token.shape, F32)
-    else:
-        _, sent_out, sent_ref, sems = refs
     own_units = pl.ds(pl.multiple_of(half * (units // 2), 128), units // 2)
     flipped_hidden = jnp.concatenate([kept[3][:, own_units].T for kept in saved], axis=1)
     pair_units = jnp.concatenate([kept[2][...] for kept in saved], axis=0)
-
-    def fetch(step):
+    copies = []
+    for step in range(STEPS):
         at = slice(step * height, (step + 1) * height)
-        slot = step % 2
-        return pltpu.make_async_copy(other_in.at[at], other_ref.at[slot], other_sems.at[slot])
-
-    def moves(step):
-        at = slice(step * height, (step + 1) * height)
-        across = slice(step * width, (step + 1) * width)
-        slot = step % 2
-        if add:
-            pairs = (
-                (gate_ref.at[slot], gate_out.at[at]),
-                (up_ref.at[slot], up_out.at[at]),
-                (down_ref.at[slot], down_out.at[:, across]),
-            )
-        else:
-            pairs = ((sent_ref.at[slot], sent_out.at[at]),)
-        return [
-            pltpu.make_async_copy(source, target, sems.at[slot, which])
-            for which, (source, target) in enumerate(pairs)
-        ]
-
-    if add:
-        fetch(0).start()
-    for step in range(STEPS):
-        slot = step % 2
         across = slice(step * width, (step + 1) * width)
         own_rows = pl.ds(pl.multiple_of(half * (model // 2) + step * height, 128), height)
         flipped = jnp.concatenate([kept[0][:, own_rows].T for kept in saved], axis=1)
         both = dot(flipped, pair_units)
         down = dot(flipped_hidden, jnp.concatenate([kept[1][:, across] for kept in saved], axis=0))
-        if based:
-            both = both + base[0][step * height : (step + 1) * height, :]
-            down = down + base[1][:, across]
+        slot = step % 2
         if step >= 2:
-            for copy in moves(step - 2):
-                copy.wait()
-        if add:
-            fetch(step).wait()
-            if step + 1 < STEPS:
-                fetch(step + 1).start()
-            gate_ref[slot] = both[:, :units] + other_ref[slot, :, :units].astype(F32)
-            up_ref[slot] = both[:, units:] + other_ref[slot, :, units : 2 * units].astype(F32)
-            down_ref[slot, :height, :] = down[:height] + other_ref[
-                slot, :, 2 * units : 2 * units + width
-            ].astype(F32)
-            for which in range(fold):
-                columns = slice(which * part, (which + 1) * part)
-                lower = slice(which * rest, (which + 1) * rest)
-                down_ref[slot, height:, columns] = down[height:, columns] + other_ref[
-                    slot, lower, 2 * units + width :
-                ].astype(F32)
-        else:
-            sent_ref[slot, :, : 2 * units] = both.astype(BF16)
-            down = down.astype(BF16)
-            sent_ref[slot, :, 2 * units : 2 * units + width] = down[:height]
-            for which in range(fold):
-                lower = slice(which * rest, (which + 1) * rest)
-                sent_ref[slot, lower, 2 * units + width :] = down[
-                    height:, which * part : (which + 1) * part
-                ]
-        for copy in moves(step):
-            copy.start()
-    for step in range(STEPS - 2, STEPS):
-        for copy in moves(step):
-            copy.wait()
-
-
-def grads(ids, saved, base, received, flops, after):
+            copies[step - 2].wait()
+        sent_ref[slot, :, : 2 * units] = both.astype(BF16)
+        down = down.astype(BF16)
+        sent_ref[slot, :, 2 * units : 2 * units + width] = down[:height]
+        for which in range(fold):
+            lower = slice(which * rest, (which + 1) * rest)
+            sent_ref[slot, lower, 2 * units + width :] = down[
+                height:, which * part : (which + 1) * part
+            ]
+        copy = pltpu.make_async_copy(sent_ref.at[slot], sent_out.at[at], sems.at[slot])
+        copy.start()
+        copies.append(copy)
+    for copy in copies[-2:]:
+        copy.wait()
+
+
+def lend(ids, saved, flops, after):
     model, units = saved[0][0].shape[1], saved[0][3].shape[1]
     height = model // 2 // STEPS
-    sent_width = 3 * units
-    add = bool(received)
-    if add:
-        shapes = [(model // 2, units), (model // 2, units), (units // 2, model)]
-        stages = [(2, height, units), (2, height, units), (2, units // 2, model // STEPS)]
-        dtype = F32
-    else:
-        shapes, stages, dtype = [(model // 2, sent_width)], [(2, height, sent_width)], BF16
-    scratch = [pltpu.VMEM(shape, dtype) for shape in stages]
-    if add:
-        scratch.append(pltpu.VMEM((2, height, sent_width), BF16))
-    scratch.append(pltpu.SemaphoreType.DMA((2, len(shapes))))
-    if add:
-        scratch.append(pltpu.SemaphoreType.DMA((2,)))
-    return pl.pallas_call(
-        functools.partial(grads_kernel, len(saved), add, len(base)),
-        in_specs=[SMEM] + [VMEM] * (4 * len(saved) + len(base)) + [ANYWHERE] * (1 + add),
-        out_specs=[HBM] * len(shapes) + [VMEM] * add,
-        out_shape=[array(shape, dtype) for shape in shapes] + [array((8, 128), F32)] * add,
-        scratch_shapes=scratch,
+    return pl.pallas_call(
+        functools.partial(lend_kernel, len(saved)),
+        in_specs=[SMEM] + [VMEM] * (4 * len(saved)) + [ANYWHERE],
+        out_specs=HBM,
+        out_shape=array((model // 2, 3 * units)),
+        scratch_shapes=[pltpu.VMEM((2, height, 3 * units), BF16), pltpu.SemaphoreType.DMA((2,))],
         compiler_params=LARGE,
         cost_estimate=estimate(flops),
-        name="grads",
-    )(ids, *in_vmem(*(part for kept in saved for part in kept), *base), *received, after)
-
-
-def part_kernel(planes, ids_ref, *refs):
+        name="lend",
+    )(ids, *in_vmem(*(part for kept in saved for part in kept)), after)
+
+
+def share_kernel(planes, ids_ref, *refs):
     saved = [refs[4 * which : 4 * which + 4] for which in range(planes)]
     both_ref, down_ref = refs[-2:]
     model, units = saved[0][0].shape[1], saved[0][3].shape[1]
-    half = ids_ref[ids_ref.shape[0] - 1]
+    half = ids_ref[ids_ref.shape[0] - 2]
     height, width = model // 2 // STEPS, model // STEPS
     own_units = pl.ds(pl.multiple_of(half * (units // 2), 128), units // 2)
     flipped_hidden = jnp.concatenate([kept[3][:, own_units].T for kept in saved], axis=1)
@@ -413,20 +350,74 @@
         )
 
 
-def part(ids, saved, flops, after):
+def share(ids, saved, flops, after):
     model, units = saved[0][0].shape[1], saved[0][3].shape[1]
     return pl.pallas_call(
-        functools.partial(part_kernel, len(saved)),
+        functools.partial(share_kernel, len(saved)),
         in_specs=[SMEM] + [VMEM] * (4 * len(saved)) + [ANYWHERE],
         out_specs=[VMEM] * 2,
         out_shape=[
             resident(model // 2, 2 * units, dtype=F32),
             resident(units // 2, model, dtype=F32),
         ],
-        compiler_params=PARAMS,
-        cost_estimate=estimate(flops),
-        name="part",
+        compiler_params=LARGE,
+        cost_estimate=estimate(flops),
+        name="share",
     )(ids, *in_vmem(*(part for kept in saved for part in kept)), after)
+
+
+def finish_kernel(
+    both_ref, down_ref, other, _, gate_out, up_out, down_out, token, gate_ref, up_ref, own_ref, sems
+):
+    model, units = down_ref.shape[1], down_ref.shape[0] * 2
+    height, width = model // 2 // STEPS, model // STEPS
+    rest = units // 2 - height
+    fold = height // rest
+    part = width // fold
+    token[...] = jnp.zeros(token.shape, F32)
+    copies = []
+    for step in range(STEPS):
+        at = slice(step * height, (step + 1) * height)
+        across = slice(step * width, (step + 1) * width)
+        both = both_ref[at, :] + other[at, : 2 * units].astype(F32)
+        gate_ref[at, :] = both[:, :units]
+        up_ref[at, :] = both[:, units:]
+        own_ref[:height, across] = down_ref[:height, across] + other[
+            at, 2 * units : 2 * units + width
+        ].astype(F32)
+        for which in range(fold):
+            lower = slice(step * height + which * rest, step * height + (which + 1) * rest)
+            target = slice(step * width + which * part, step * width + (which + 1) * part)
+            own_ref[height:, target] = down_ref[height:, target] + other[
+                lower, 2 * units + width :
+            ].astype(F32)
+        moves = (
+            (gate_ref.at[at], gate_out.at[at]),
+            (up_ref.at[at], up_out.at[at]),
+            (own_ref.at[:, across], down_out.at[:, across]),
+        )
+        for which, (source, target) in enumerate(moves):
+            copy = pltpu.make_async_copy(source, target, sems.at[step, which])
+            copy.start()
+            copies.append(copy)
+    for copy in copies:
+        copy.wait()
+
+
+def finish(sums, received, flops, after):
+    model, units = sums[1].shape[1], sums[1].shape[0] * 2
+    shapes = [(model // 2, units), (model // 2, units), (units // 2, model)]
+    return pl.pallas_call(
+        finish_kernel,
+        in_specs=[VMEM] * 3 + [ANYWHERE],
+        out_specs=[HBM] * 3 + [VMEM],
+        out_shape=[array(shape, F32) for shape in shapes] + [array((8, 128), F32)],
+        scratch_shapes=[pltpu.VMEM(shape, F32) for shape in shapes]
+        + [pltpu.SemaphoreType.DMA((STEPS, 3))],
+        compiler_params=LARGE,
+        cost_estimate=estimate(flops),
+        name="finish",
+    )(*in_vmem(*sums), received, after)
 
 
 def expand_kernel(count, top, ids_ref, meta_ref, *refs):
@@ -491,13 +482,14 @@
     ("expert", 2, 29),
     ("expert", 3, 0),
     ("both", 1, 0),
-    ("expand", 2, 0),
+    ("expand", 2, 28),
     ("expand", 3, 0),
     ("total", 1, 0),
     ("expert", 1, 0),
     ("lend", 0, 37),
     ("expand", 1, 37),
-    ("finish", 0, 37),
+    ("share", 0, 30),
+    ("finish", 0, 0),
 )
 LATE = ()
 
@@ -508,7 +500,7 @@
     for plane in order:
         chain += [("both", plane, 0), ("expert", plane, 0)]
         chain += [("expand", plane, 0)]
-    return chain + [("lend", 0, 0), ("finish", 0, 0)]
+    return chain + [("lend", 0, 0), ("share", 0, 0), ("finish", 0, 0)]
 
 
 def local(tokens, cotangent, experts, mixing, gate_matrix, up_matrix, down_matrix):
@@ -572,8 +564,7 @@
             cots[other] = swap(copies[1], other * inner)
         return sent[0]
 
-    last, weights, own, received, results = None, None, None, None, None
-    base, based = [], []
+    last, weights, own, received, sums, results = None, None, None, None, None, None
     for kind, plane, size in chain:
         after = [] if last is None else [last]
         flops = 1 << size
@@ -598,17 +589,14 @@
         elif kind == "total":
             own = last = total(own, partial[:plane], F32, flops, last)
             del partial[:plane]
-        elif kind == "part":
-            based = list(saved)
-            base = part(ids, [saved[other] for other in based], flops, last)
-            last = base[1]
         elif kind == "lend":
-            rest = [saved[other] for other in planes if other not in based]
-            (last,) = grads(ids, rest, base, [], flops, last)
+            last = lend(ids, [saved[other] for other in planes], flops, last)
             received = lax.ppermute(last, "dp", [(0, 1), (1, 0)])
+        elif kind == "share":
+            sums = share(ids, [saved[other] for other in planes], flops, last)
+            last = sums[1]
         elif kind == "finish":
-            kept = [saved[other] for other in planes]
-            *results, last = grads(ids, kept, [], [received], flops, last)
+            *results, last = finish(sums, received, flops, last)
     input_grad = total(own, partial, BF16, 1, last)
     return (input_grad, *(value[None] for value in results))
 

time: 188 us -> 185 us (0.984)
  waiting for transfers between devices: 75.2 us -> 73.2 us
    ppermute x1, waiting for transfers between devices: 6.74 us -> 1.02 us  [local(): received = lax.ppermute(last, 'dp', [(0, 1), (1, 0)])]
    ppermute x36, waiting for transfers between devices: 68.5 us -> 72.2 us  [swap(): return lax.ppermute(value, 'expert', pairs)]
    pallas_call x2 -> x3, Pallas kernels: 18.1 us -> 17.3 us  [the longest x1 7.84 us: lend(): pl.pallas_call(functools.partial(lend_kernel, len(saved)), in_specs=[SMEM...]
  transfers between devices with their start and end apart: 37 -> 37, of which waited for: 9 -> 10; matrix products, arithmetic and copies ran while one was open for 0% -> 0% of each run, Pallas kernels for 30% -> 30%
where the time goes in v2:
time: 185 us
  waiting for transfers between devices  73.2 us (40%)
  Pallas kernels  58.2 us (31%)
  starting transfers between devices  50.3 us (27%)
  local copies, waits for them, and re-layouts  2.41 us (1%)
    ppermute x36, waiting for transfers between devices, swap(): return lax.ppermute(value, 'expert', pairs)  72.2 us
    ppermute x36, starting transfers between devices, swap(): return lax.ppermute(value, 'expert', pairs)  50.3 us
    pallas_call x4, Pallas kernels, expert(): pl.pallas_call(functools.partial(expert_kernel, count, bool(begun)), in_s...  19.5 us
    pallas_call x1, Pallas kernels, lend(): pl.pallas_call(functools.partial(lend_kernel, len(saved)), in_specs=[SMEM...  7.84 us
    pallas_call x5, Pallas kernels, select(): pl.pallas_call(functools.partial(select_kernel, count, cap, top, parts, l...  6.74 us
    pallas_call x1, Pallas kernels, share(): pl.pallas_call(functools.partial(share_kernel, len(saved)), in_specs=[SME...  5.72 us
    pallas_call x4, Pallas kernels, expand(): pl.pallas_call(functools.partial(expand_kernel, count, top), grid=(1,), o...  4.92 us
    pallas_call x1, Pallas kernels, flip(): pl.pallas_call(flip_kernel, in_specs=[HBM] * 3 + [ANYWHERE], out_specs=[V...  4.67 us
  transfers between devices with their start and end apart: 37, of which 10 were waited for; matrix products, arithmetic and copies ran while one was open for 0% of the time, Pallas kernels for 30%

profile of v2, /device:TPU:0, one launch (start us, length us, event | category | flops | bytes accessed | tf_op | source)
XLA Modules:
  0.0 185.2 jit_solution(1864995592916898357)
XLA Ops:
  0.6 0.7 copy-done.4
  1.3 0.7 copy-done.5
  2.0 1.1 pack.1.refs_0_.meta_ref
  3.1 4.1 %collective-permute-start.3 = (bf16[144,2048]{1,0:T(8,128)(2,1)S(1)}, bf16[144,2048]{1,0:T(8,128)(2,1)S(1)}, u32[]{:S(2)}, u32[]{:S(2)}) collective-permute-start(bf16[144,2048]{1,0:T(8,128)(2,1)S(1)} %pack.1.refs_0_.meta_ref), channel_id=1, source_target_pairs={{0,8},{1,9},{2,10},{3,11},{4,12},{5,13},{6,14},{7,15},{8,0},{9,1},... | collective-permute-start | bytes 1769480 | tf_op jit(solution)/shard_map/ppermute | solution.py:516
  7.3 1.0 copy-done.2
  8.3 1.4 select.5
  9.7 1.6 collective-permute-start
  11.2 1.5 collective-permute-start.1
  12.8 0.5 collective-permute-start.2
  13.2 4.7 %flip.1 = (bf16[2048,768]{1,0:T(8,128)(2,1)S(1)}, bf16[2048,768]{1,0:T(8,128)(2,1)S(1)}, bf16[1536,2048]{1,0:T(8,128)(2,1)S(1)}, bf16[2048,768]{1,0:T(8,128)(2,1)S(1)}) custom-call(bf16[2048,768]{1,0:T(8,128)(2,1)} %bitcast.12, bf16[2048,768]{1,0:T(8,128)(2,1)} %bitcast.13, bf16[768,2048]{1,0:T(8,128)(2,1)} %bitcast.14, ...), custom_call_target="tpu_custom_call" | custom-call | flops 1 | bytes 1 | tf_op jit(solution)/shard_map/flip/pallas_call | solution.py:173
  17.9 15.2 %collective-permute-done.3.refs_0_.refs_2_.meta_ref = bf16[144,2048]{1,0:T(8,128)(2,1)S(1)} collective-permute-done((bf16[144,2048]{1,0:T(8,128)(2,1)S(1)}, bf16[144,2048]{1,0:T(8,128)(2,1)S(1)}, u32[]{:S(2)}, u32[]{:S(2)}) %collective-permute-start.3) | collective-permute-done | bytes 589856 | tf_op jit(solution)/shard_map/ppermute | solution.py:516
  33.1 1.3 select.6
  34.4 1.6 collective-permute-start.7
  36.0 1.5 collective-permute-start.8
  37.5 0.4 collective-permute-start.9
  38.0 4.1 %collective-permute-start.14 = (bf16[144,2048]{1,0:T(8,128)(2,1)S(1)}, bf16[144,2048]{1,0:T(8,128)(2,1)S(1)}, u32[]{:S(2)}, u32[]{:S(2)}) collective-permute-start(bf16[144,2048]{1,0:T(8,128)(2,1)S(1)} %get-tuple-element.94), channel_id=1, source_target_pairs={{0,4},{1,5},{2,6},{3,7},{4,0},{5,1},{6,2},{7,3},{8,12},{9,13},{10,... | collective-permute-start | bytes 1769480 | tf_op jit(solution)/shard_map/ppermute | solution.py:516
  42.1 5.2 %expert.4 = (bf16[64,2048]{1,0:T(8,128)(2,1)S(1)}, bf16[64,2048]{1,0:T(8,128)(2,1)S(1)}, bf16[64,2048]{1,0:T(8,128)(2,1)S(1)}, bf16[64,2048]{1,0:T(8,128)(2,1)S(...) custom-call(bf16[2,64,2048]{2,1,0:T(8,128)(2,1)S(1)} %get-tuple-elem, ...), custom_call_target="tpu_custom_call" | custom-call | flops 1 | bytes 1 | tf_op jit(solution)/shard_map/expert/pallas_call | solution.py:266
  47.3 1.6 collective-permute-start.4
  48.9 1.5 collective-permute-start.5
  50.4 0.5 collective-permute-start.6
  50.9 1.8 begin.1
  52.7 3.9 %collective-permute-done.4.refs_1_ = bf16[64,2048]{1,0:T(8,128)(2,1)S(1)} collective-permute-done((bf16[64,2048]{1,0:T(8,128)(2,1)S(1)}, bf16[64,2048]{1,0:T(8,128)(2,1)S(1)}, u32[]{:S(2)}, u32[]{:S(2)}) %collective-permute-start.4) | collective-permute-done | bytes 262176 | tf_op jit(solution)/shard_map/ppermute | solution.py:516
  56.6 4.4 %collective-permute-done.5.refs_2_ = bf16[64,2048]{1,0:T(8,128)(2,1)S(1)} collective-permute-done((bf16[64,2048]{1,0:T(8,128)(2,1)S(1)}, bf16[64,2048]{1,0:T(8,128)(2,1)S(1)}, u32[]{:S(2)}, u32[]{:S(2)}) %collective-permute-start.5) | collective-permute-done | bytes 262176 | tf_op jit(solution)/shard_map/ppermute | solution.py:516
  61.1 1.0 expand.4.refs_3_.own_ref
  62.1 0.4 collective-permute-done.10.refs_1_.refs_2_
  62.5 1.3 select.7
  63.8 0.8 collective-permute-start.15
  64.7 0.5 collective-permute-start.11
  65.2 1.5 collective-permute-start.12
  66.7 1.4 collective-permute-start.13
  68.1 7.8 %collective-permute-done.15.refs_1_ = bf16[128,2048]{1,0:T(8,128)(2,1)S(1)} collective-permute-done((bf16[128,2048]{1,0:T(8,128)(2,1)S(1)}, bf16[128,2048]{1,0:T(8,128)(2,1)S(1)}, u32[]{:S(2)}, u32[]{:S(2)}) %collective-permute-start.15) | collective-permute-done | bytes 524320 | tf_op jit(solution)/shard_map/ppermute | solution.py:516
  75.9 1.4 select.8
  77.3 1.1 collective-permute-start.21
  78.4 1.5 collective-permute-start.22
  79.9 1.0 collective-permute-start.23
  81.2 1.7 collective-permute-start.19
  82.9 3.6 %expert.5 = (bf16[64,2048]{1,0:T(8,128)(2,1)S(1)}, bf16[64,2048]{1,0:T(8,128)(2,1)S(1)}, bf16[64,2048]{1,0:T(8,128)(2,1)S(1)}, bf16[64,2048]{1,0:T(8,128)(2,1)S(...) custom-call(bf16[1,64,2048]{2,1,0:T(8,128)(2,1)S(1)} %get-tuple-element.89.refs_2_.re, ...), custom_call_target="tpu_custom_call" | custom-call | flops 536870912 | bytes 1 | tf_op jit(solution)/shard_map/expert/pallas_call | solution.py:266
  86.5 5.8 %collective-permute-done.21.refs_1_ = bf16[2,64,2048]{2,1,0:T(8,128)(2,1)S(1)} collective-permute-done((bf16[2,64,2048]{2,1,0:T(8,128)(2,1)S(1)}, bf16[2,64,2048]{2,1,0:T(8,128)(2,1)S(1)}, u32[]{:S(2)}, u32[]{:S(2)}) %collective-permute-start.21) | collective-permute-done | bytes 524320 | tf_op jit(solution)/shard_map/ppermute | solution.py:516
  92.3 1.0 collective-permute-start.16
  93.3 10.8 %collective-permute-done.22.refs_2_ = bf16[2,64,2048]{2,1,0:T(8,128)(2,1)S(1)} collective-permute-done((bf16[2,64,2048]{2,1,0:T(8,128)(2,1)S(1)}, bf16[2,64,2048]{2,1,0:T(8,128)(2,1)S(1)}, u32[]{:S(2)}, u32[]{:S(2)}) %collective-permute-start.22) | collective-permute-done | bytes 524320 | tf_op jit(solution)/shard_map/ppermute | solution.py:516
  104.1 1.7 collective-permute-start.17
  105.8 5.2 %expert.6 = (bf16[64,2048]{1,0:T(8,128)(2,1)S(1)}, bf16[64,2048]{1,0:T(8,128)(2,1)S(1)}, bf16[64,2048]{1,0:T(8,128)(2,1)S(1)}, bf16[64,2048]{1,0:T(8,128)(2,1)S(...) custom-call(bf16[2,64,2048]{2,1,0:T(8,128)(2,1)S(1)} %get-tuple-elem, ...), custom_call_target="tpu_custom_call" | custom-call | flops 1 | bytes 1 | tf_op jit(solution)/shard_map/expert/pallas_call | solution.py:266
  111.0 1.9 %collective-permute-start.25 = (bf16[64,2048]{1,0:T(8,128)(2,1)S(1)}, bf16[64,2048]{1,0:T(8,128)(2,1)S(1)}, u32[]{:S(2)}, u32[]{:S(2)}) collective-permute-start(bf16[64,2048]{1,0:T(8,128)(2,1)S(1)} %get-tuple-element.106), channel_id=1, source_target_pairs={{0,1},{1,0},{2,3},{3,2},{4,5},{5,4},{6,7},{7,6},{8,9},{9,8},{10,11... | collective-permute-start | bytes 786440 | tf_op jit(solution)/shard_map/ppermute | solution.py:516
  112.9 1.7 collective-permute-start.26
  114.6 1.4 select.9
  116.0 0.6 collective-permute-start.29
  116.6 1.0 expand.5.refs_4_
  117.6 3.5 %collective-permute-start.24 = (bf16[128,2048]{1,0:T(8,128)(2,1)S(1)}, bf16[128,2048]{1,0:T(8,128)(2,1)S(1)}, u32[]{:S(2)}, u32[]{:S(2)}) collective-permute-start(bf16[128,2048]{1,0:T(8,128)(2,1)S(1)} %expand.5.refs_4_), channel_id=1, source_target_pairs={{0,8},{1,9},{2,10},{3,11},{4,12},{5,13},{6,14},{7,15},{8,0},{9,1},... | collective-permute-start | bytes 1572872 | tf_op jit(solution)/shard_map/ppermute | solution.py:516
  121.1 1.0 collective-permute-start.30
  122.1 1.2 collective-permute-start.31
  123.3 1.8 collective-permute-start.27
  125.0 20.1 %collective-permute-done.27.refs_3_ = bf16[64,2048]{1,0:T(8,128)(2,1)S(1)} collective-permute-done((bf16[64,2048]{1,0:T(8,128)(2,1)S(1)}, bf16[64,2048]{1,0:T(8,128)(2,1)S(1)}, u32[]{:S(2)}, u32[]{:S(2)}) %collective-permute-start.27) | collective-permute-done | bytes 262176 | tf_op jit(solution)/shard_map/ppermute | solution.py:516
  145.1 1.8 expand.6.refs_1_
  146.9 3.5 %collective-permute-start.28 = (bf16[128,2048]{1,0:T(8,128)(2,1)}, bf16[128,2048]{1,0:T(8,128)(2,1)}, u32[]{:S(2)}, u32[]{:S(2)}) collective-permute-start(bf16[128,2048]{1,0:T(8,128)(2,1)} %expand.6.refs_1_), channel_id=1, source_target_pairs={{0,12},{1,13},{2,14},{3,15},{4,8},{5,9},{6,10},{7,11},{8,4},{9,5},... | collective-permute-start | bytes 1572872 | tf_op jit(solution)/shard_map/ppermute | solution.py:516
  150.5 5.5 %expert.7 = (bf16[64,2048]{1,0:T(8,128)(2,1)S(1)}, bf16[64,2048]{1,0:T(8,128)(2,1)S(1)}, bf16[64,2048]{1,0:T(8,128)(2,1)S(1)}, bf16[64,2048]{1,0:T(8,128)(2,1)S(...) custom-call(bf16[2,64,2048]{2,1,0:T(8,128)(2,1)S(1)} %get-tuple-elem, ...), custom_call_target="tpu_custom_call" | custom-call | flops 1 | bytes 1 | tf_op jit(solution)/shard_map/expert/pallas_call | solution.py:266
  156.1 1.8 collective-permute-start.32
  157.9 1.9 %collective-permute-start.33 = (bf16[64,2048]{1,0:T(8,128)(2,1)S(1)}, bf16[64,2048]{1,0:T(8,128)(2,1)S(1)}, u32[]{:S(2)}, u32[]{:S(2)}) collective-permute-start(bf16[64,2048]{1,0:T(8,128)(2,1)S(1)} %get-tuple-element.114), channel_id=1, source_target_pairs={{0,2},{1,3},{2,0},{3,1},{4,6},{5,7},{6,4},{7,5},{8,10},{9,11},{10,... | collective-permute-start | bytes 786440 | tf_op jit(solution)/shard_map/ppermute | solution.py:516
  159.8 7.8 %lend.1.refs_4_ = bf16[1024,2304]{1,0:T(8,128)(2,1)S(1)} custom-call(s32[6]{0:T(128)S(1)} %pad_add_fusion.ids_ref, bf16[256,2048]{1,0:T(8,128)(2,1)S(1)} %get-tuple-element.116.refs_0_, bf16[256,2048]{1,0:T(8,128)(2,1)S(1)} %get-tuple-element.117.refs_1_, bf16[256,1536]{1,0:T(8,128)(2,1)S(1)} %get-tuple-element.118.refs_2_, ...), custom_call_target="tpu_custom_call" | custom-call | flops 137438953472 | bytes 1 | tf_op jit(solution)/shard_map/lend/pallas_call | solution.py:322
  167.7 1.0 expand.7.refs_16_
  168.9 5.7 %share.1 = (f32[1024,1536]{1,0:T(8,128)S(1)}, f32[384,2048]{1,0:T(8,128)S(1)}) custom-call(s32[6]{0:T(128)S(1)} %pad_add_fusion.ids_ref, bf16[256,2048]{1,0:T(8,128)(2,1)S(1)} %get-tuple-element.116.refs_0_, bf16[256,2048]{1,0:T(8,128)(2,1)S(1)} %get-tuple-element.117.refs_1_, bf16[256,1536]{1,0:T(8,128)(2,1)S(1)} %get-tuple-element.118.refs_2_, ...), custom_call_target="tpu_custom_call" | custom-call | flops 1073741824 | bytes 1 | tf_op jit(solution)/shard_map/share/pallas_call | solution.py:355
  174.6 1.0 collective-permute-done.36.other
  175.6 3.8 %finish.1 = (f32[1024,768]{1,0:T(8,128)}, f32[1024,768]{1,0:T(8,128)}, f32[384,2048]{1,0:T(8,128)}, f32[8,128]{1,0:T(8,128)S(1)}) custom-call(f32[1024,1536]{1,0:T(8,128)S(1)} %get-tuple-element.132.both_ref, f32[384,2048]{1,0:T(8,128)S(1)} %get-tuple-element.133.down_ref._, bf16[1024,2304]{1,0:T(8,128)(2,1)S(1)} %collective-permute-done.36.other, ...), custom_call_target="tpu_custom_call" | custom-call | flops 1 | bytes 1 | tf_op jit(solution)/shard_map/finish/pallas_call | solution.py:410
  179.4 3.7 %collective-permute-done.35.refs_1_ = bf16[128,2048]{1,0:T(8,128)(2,1)S(1)} collective-permute-done((bf16[128,2048]{1,0:T(8,128)(2,1)S(1)}, bf16[128,2048]{1,0:T(8,128)(2,1)S(1)}, u32[]{:S(2)}, u32[]{:S(2)}) %collective-permute-start.35) | collective-permute-done | bytes 524320 | tf_op jit(solution)/shard_map/ppermute | solution.py:516
  183.1 2.0 %total.3 = bf16[128,2048]{1,0:T(8,128)(2,1)} custom-call(f32[128,2048]{1,0:T(8,128)S(1)} %copy-done.1, bf16[128,2048]{1,0:T(8,128)(2,1)} %collective-permute-done.28.refs_0_, bf16[128,2048]{1,0:T(8,128)(2,1)S(1)} %collective-permute-done.35.refs_1_, f32[8,128]{1,0:T(8,128)S(1)} %get-tuple-element.134.refs_2_), custom_call_target="tpu_custom_call" | custom-call | flops 1 | bytes 1 | tf_op jit(solution)/shard_map/total/pallas_call | solution.py:462
  (45 shorter events, 0.7 us)
Async XLA Ops:
  0.6 0.7 copy-start.4
  1.3 0.7 copy-start.5
  3.1 30.1 %collective-permute-start.3 = (bf16[144,2048]{1,0:T(8,128)(2,1)S(1)}, bf16[144,2048]{1,0:T(8,128)(2,1)S(1)}, u32[]{:S(2)}, u32[]{:S(2)}) collective-permute-start(bf16[144,2048]{1,0:T(8,128)(2,1)S(1)} %pack.1.refs_0_.meta_ref), channel_id=1, source_target_pairs={{0,8},{1,9},{2,10},{3,11},{4,12},{5,13},{6,14},{7,15},{8,0},{9,1},... | collective-permute-start | bytes 1769480 | tf_op jit(solution)/shard_map/ppermute | solution.py:516
  7.2 1.0 copy-start.2
  9.7 27.8 %collective-permute-start = (bf16[2,64,2048]{2,1,0:T(8,128)(2,1)S(1)}, bf16[2,64,2048]{2,1,0:T(8,128)(2,1)S(1)}, u32[]{:S(2)}, u32[]{:S(2)}) collective-permute-start(bf16[2,64,2048]{2,1,0:T(8,128)(2,1)S(1)} %get-tuple-element.72), channel_id=1, source_target_pairs={{0,1},{1,0},{2,3},{3,2},{4,5},{5,4},{6,7},{7,6},{8,9},{9,8},{10,11... | collective-permute-start | bytes 1572872 | tf_op jit(solution)/shard_map/ppermute | solution.py:516
  11.2 26.7 %collective-permute-start.1 = (bf16[2,64,2048]{2,1,0:T(8,128)(2,1)S(1)}, bf16[2,64,2048]{2,1,0:T(8,128)(2,1)S(1)}, u32[]{:S(2)}, u32[]{:S(2)}) collective-permute-start(bf16[2,64,2048]{2,1,0:T(8,128)(2,1)S(1)} %get-tuple-element.73), channel_id=1, source_target_pairs={{0,2},{1,3},{2,0},{3,1},{4,6},{5,7},{6,4},{7,5},{8,10},{9,11},{10,... | collective-permute-start | bytes 1572872 | tf_op jit(solution)/shard_map/ppermute | solution.py:516
  12.8 25.2 %collective-permute-start.2 = (bf16[2,64,2048]{2,1,0:T(8,128)(2,1)S(1)}, bf16[2,64,2048]{2,1,0:T(8,128)(2,1)S(1)}, u32[]{:S(2)}, u32[]{:S(2)}) collective-permute-start(bf16[2,64,2048]{2,1,0:T(8,128)(2,1)S(1)} %get-tuple-element.74), channel_id=1, source_target_pairs={{0,3},{1,2},{2,1},{3,0},{4,7},{5,6},{6,5},{7,4},{8,11},{9,10},{10,... | collective-permute-start | bytes 1572872 | tf_op jit(solution)/shard_map/ppermute | solution.py:516
  34.4 12.9 %collective-permute-start.7 = (bf16[1,64,2048]{2,1,0:T(8,128)(2,1)S(1)}, bf16[1,64,2048]{2,1,0:T(8,128)(2,1)S(1)}, u32[]{:S(2)}, u32[]{:S(2)}) collective-permute-start(bf16[1,64,2048]{2,1,0:T(8,128)(2,1)S(1)} %get-tuple-element.84), channel_id=1, source_target_pairs={{0,1},{1,0},{2,3},{3,2},{4,5},{5,4},{6,7},{7,6},{8,9},{9,8},{10,11... | collective-permute-start | bytes 786440 | tf_op jit(solution)/shard_map/ppermute | solution.py:516
  36.0 12.9 %collective-permute-start.8 = (bf16[1,64,2048]{2,1,0:T(8,128)(2,1)S(1)}, bf16[1,64,2048]{2,1,0:T(8,128)(2,1)S(1)}, u32[]{:S(2)}, u32[]{:S(2)}) collective-permute-start(bf16[1,64,2048]{2,1,0:T(8,128)(2,1)S(1)} %get-tuple-element.85), channel_id=1, source_target_pairs={{0,2},{1,3},{2,0},{3,1},{4,6},{5,7},{6,4},{7,5},{8,10},{9,11},{10,... | collective-permute-start | bytes 786440 | tf_op jit(solution)/shard_map/ppermute | solution.py:516
  37.5 12.9 %collective-permute-start.9 = (bf16[1,64,2048]{2,1,0:T(8,128)(2,1)S(1)}, bf16[1,64,2048]{2,1,0:T(8,128)(2,1)S(1)}, u32[]{:S(2)}, u32[]{:S(2)}) collective-permute-start(bf16[1,64,2048]{2,1,0:T(8,128)(2,1)S(1)} %get-tuple-element.86), channel_id=1, source_target_pairs={{0,3},{1,2},{2,1},{3,0},{4,7},{5,6},{6,5},{7,4},{8,11},{9,10},{10,... | collective-permute-start | bytes 786440 | tf_op jit(solution)/shard_map/ppermute | solution.py:516
  38.0 24.5 %collective-permute-start.10 = (bf16[128,2048]{1,0:T(8,128)(2,1)S(1)}, bf16[128,2048]{1,0:T(8,128)(2,1)S(1)}, u32[]{:S(2)}, u32[]{:S(2)}) collective-permute-start(bf16[128,2048]{1,0:T(8,128)(2,1)S(1)} %get-tuple-element.88), channel_id=1, source_target_pairs={{0,8},{1,9},{2,10},{3,11},{4,12},{5,13},{6,14},{7,15},{8,0},{9,1},... | collective-permute-start | bytes 1572872 | tf_op jit(solution)/shard_map/ppermute | solution.py:516
  38.0 30.2 %collective-permute-start.14 = (bf16[144,2048]{1,0:T(8,128)(2,1)S(1)}, bf16[144,2048]{1,0:T(8,128)(2,1)S(1)}, u32[]{:S(2)}, u32[]{:S(2)}) collective-permute-start(bf16[144,2048]{1,0:T(8,128)(2,1)S(1)} %get-tuple-element.94), channel_id=1, source_target_pairs={{0,4},{1,5},{2,6},{3,7},{4,0},{5,1},{6,2},{7,3},{8,12},{9,13},{10,... | collective-permute-start | bytes 1769480 | tf_op jit(solution)/shard_map/ppermute | solution.py:516
  47.3 9.3 %collective-permute-start.4 = (bf16[64,2048]{1,0:T(8,128)(2,1)S(1)}, bf16[64,2048]{1,0:T(8,128)(2,1)S(1)}, u32[]{:S(2)}, u32[]{:S(2)}) collective-permute-start(bf16[64,2048]{1,0:T(8,128)(2,1)S(1)} %get-tuple-element.81), channel_id=1, source_target_pairs={{0,1},{1,0},{2,3},{3,2},{4,5},{5,4},{6,7},{7,6},{8,9},{9,8},{10,11... | collective-permute-start | bytes 786440 | tf_op jit(solution)/shard_map/ppermute | solution.py:516
  48.9 12.2 %collective-permute-start.5 = (bf16[64,2048]{1,0:T(8,128)(2,1)S(1)}, bf16[64,2048]{1,0:T(8,128)(2,1)S(1)}, u32[]{:S(2)}, u32[]{:S(2)}) collective-permute-start(bf16[64,2048]{1,0:T(8,128)(2,1)S(1)} %get-tuple-element.82), channel_id=1, source_target_pairs={{0,2},{1,3},{2,0},{3,1},{4,6},{5,7},{6,4},{7,5},{8,10},{9,11},{10,... | collective-permute-start | bytes 786440 | tf_op jit(solution)/shard_map/ppermute | solution.py:516
  50.4 10.6 %collective-permute-start.6 = (bf16[64,2048]{1,0:T(8,128)(2,1)S(1)}, bf16[64,2048]{1,0:T(8,128)(2,1)S(1)}, u32[]{:S(2)}, u32[]{:S(2)}) collective-permute-start(bf16[64,2048]{1,0:T(8,128)(2,1)S(1)} %get-tuple-element.83), channel_id=1, source_target_pairs={{0,3},{1,2},{2,1},{3,0},{4,7},{5,6},{6,5},{7,4},{8,11},{9,10},{10,... | collective-permute-start | bytes 786440 | tf_op jit(solution)/shard_map/ppermute | solution.py:516
  61.1 19.8 %copy-start.3 = (bf16[128,2048]{1,0:T(8,128)(2,1)S(1)}, bf16[128,2048]{1,0:T(8,128)(2,1)}, u32[]{:S(2)}) copy-start(bf16[128,2048]{1,0:T(8,128)(2,1)} %refs_3_.1) | copy-start | bytes 1572868
  63.8 12.1 %collective-permute-start.15 = (bf16[128,2048]{1,0:T(8,128)(2,1)S(1)}, bf16[128,2048]{1,0:T(8,128)(2,1)S(1)}, u32[]{:S(2)}, u32[]{:S(2)}) collective-permute-start(bf16[128,2048]{1,0:T(8,128)(2,1)S(1)} %get-tuple-element.95), channel_id=1, source_target_pairs={{0,4},{1,5},{2,6},{3,7},{4,0},{5,1},{6,2},{7,3},{8,12},{9,13},{10,... | collective-permute-start | bytes 1572872 | tf_op jit(solution)/shard_map/ppermute | solution.py:516
  64.7 15.3 %collective-permute-start.11 = (bf16[1,64,2048]{2,1,0:T(8,128)(2,1)S(1)}, bf16[1,64,2048]{2,1,0:T(8,128)(2,1)S(1)}, u32[]{:S(2)}, u32[]{:S(2)}) collective-permute-start(bf16[1,64,2048]{2,1,0:T(8,128)(2,1)S(1)} %get-tuple-element.90), channel_id=1, source_target_pairs={{0,1},{1,0},{2,3},{3,2},{4,5},{5,4},{6,7},{7,6},{8,9},{9,8},{10,11... | collective-permute-start | bytes 786440 | tf_op jit(solution)/shard_map/ppermute | solution.py:516
  65.2 15.7 %collective-permute-start.12 = (bf16[1,64,2048]{2,1,0:T(8,128)(2,1)S(1)}, bf16[1,64,2048]{2,1,0:T(8,128)(2,1)S(1)}, u32[]{:S(2)}, u32[]{:S(2)}) collective-permute-start(bf16[1,64,2048]{2,1,0:T(8,128)(2,1)S(1)} %get-tuple-element.91), channel_id=1, source_target_pairs={{0,2},{1,3},{2,0},{3,1},{4,6},{5,7},{6,4},{7,5},{8,10},{9,11},{10,... | collective-permute-start | bytes 786440 | tf_op jit(solution)/shard_map/ppermute | solution.py:516
  66.7 14.5 %collective-permute-start.13 = (bf16[1,64,2048]{2,1,0:T(8,128)(2,1)S(1)}, bf16[1,64,2048]{2,1,0:T(8,128)(2,1)S(1)}, u32[]{:S(2)}, u32[]{:S(2)}) collective-permute-start(bf16[1,64,2048]{2,1,0:T(8,128)(2,1)S(1)} %get-tuple-element.92), channel_id=1, source_target_pairs={{0,3},{1,2},{2,1},{3,0},{4,7},{5,6},{6,5},{7,4},{8,11},{9,10},{10,... | collective-permute-start | bytes 786440 | tf_op jit(solution)/shard_map/ppermute | solution.py:516
  77.3 14.9 %collective-permute-start.21 = (bf16[2,64,2048]{2,1,0:T(8,128)(2,1)S(1)}, bf16[2,64,2048]{2,1,0:T(8,128)(2,1)S(1)}, u32[]{:S(2)}, u32[]{:S(2)}) collective-permute-start(bf16[2,64,2048]{2,1,0:T(8,128)(2,1)S(1)} %get-tuple-element.101), channel_id=1, source_target_pairs={{0,1},{1,0},{2,3},{3,2},{4,5},{5,4},{6,7},{7,6},{8,9},{9,8},{10,11... | collective-permute-start | bytes 1572872 | tf_op jit(solution)/shard_map/ppermute | solution.py:516
  78.4 25.7 %collective-permute-start.22 = (bf16[2,64,2048]{2,1,0:T(8,128)(2,1)S(1)}, bf16[2,64,2048]{2,1,0:T(8,128)(2,1)S(1)}, u32[]{:S(2)}, u32[]{:S(2)}) collective-permute-start(bf16[2,64,2048]{2,1,0:T(8,128)(2,1)S(1)} %get-tuple-element.102), channel_id=1, source_target_pairs={{0,2},{1,3},{2,0},{3,1},{4,6},{5,7},{6,4},{7,5},{8,10},{9,11},{10,... | collective-permute-start | bytes 1572872 | tf_op jit(solution)/shard_map/ppermute | solution.py:516
  79.9 25.8 %collective-permute-start.23 = (bf16[2,64,2048]{2,1,0:T(8,128)(2,1)S(1)}, bf16[2,64,2048]{2,1,0:T(8,128)(2,1)S(1)}, u32[]{:S(2)}, u32[]{:S(2)}) collective-permute-start(bf16[2,64,2048]{2,1,0:T(8,128)(2,1)S(1)} %get-tuple-element.103), channel_id=1, source_target_pairs={{0,3},{1,2},{2,1},{3,0},{4,7},{5,6},{6,5},{7,4},{8,11},{9,10},{10,... | collective-permute-start | bytes 1572872 | tf_op jit(solution)/shard_map/ppermute | solution.py:516
  80.9 30.1 %collective-permute-start.20 = (bf16[128,2048]{1,0:T(8,128)(2,1)S(1)}, bf16[128,2048]{1,0:T(8,128)(2,1)S(1)}, u32[]{:S(2)}, u32[]{:S(2)}) collective-permute-start(bf16[128,2048]{1,0:T(8,128)(2,1)S(1)} %copy-done.3), channel_id=1, source_target_pairs={{0,4},{1,5},{2,6},{3,7},{4,0},{5,1},{6,2},{7,3},{8,12},{9,13},{10,... | collective-permute-start | bytes 1572872 | tf_op jit(solution)/shard_map/ppermute | solution.py:516
  81.2 31.7 %collective-permute-start.19 = (bf16[144,2048]{1,0:T(8,128)(2,1)S(1)}, bf16[144,2048]{1,0:T(8,128)(2,1)S(1)}, u32[]{:S(2)}, u32[]{:S(2)}) collective-permute-start(bf16[144,2048]{1,0:T(8,128)(2,1)S(1)} %pack.1.refs_0_.meta_ref), channel_id=1, source_target_pairs={{0,4},{1,5},{2,6},{3,7},{4,0},{5,1},{6,2},{7,3},{8,12},{9,13},{10,... | collective-permute-start | bytes 1769480 | tf_op jit(solution)/shard_map/ppermute | solution.py:516
  92.3 23.7 %collective-permute-start.16 = (bf16[64,2048]{1,0:T(8,128)(2,1)S(1)}, bf16[64,2048]{1,0:T(8,128)(2,1)S(1)}, u32[]{:S(2)}, u32[]{:S(2)}) collective-permute-start(bf16[64,2048]{1,0:T(8,128)(2,1)S(1)} %get-tuple-element.98), channel_id=1, source_target_pairs={{0,1},{1,0},{2,3},{3,2},{4,5},{5,4},{6,7},{7,6},{8,9},{9,8},{10,11... | collective-permute-start | bytes 786440 | tf_op jit(solution)/shard_map/ppermute | solution.py:516
  104.1 12.5 %collective-permute-start.17 = (bf16[64,2048]{1,0:T(8,128)(2,1)S(1)}, bf16[64,2048]{1,0:T(8,128)(2,1)S(1)}, u32[]{:S(2)}, u32[]{:S(2)}) collective-permute-start(bf16[64,2048]{1,0:T(8,128)(2,1)S(1)} %get-tuple-element.99), channel_id=1, source_target_pairs={{0,2},{1,3},{2,0},{3,1},{4,6},{5,7},{6,4},{7,5},{8,10},{9,11},{10,... | collective-permute-start | bytes 786440 | tf_op jit(solution)/shard_map/ppermute | solution.py:516
  105.8 10.8 %collective-permute-start.18 = (bf16[64,2048]{1,0:T(8,128)(2,1)S(1)}, bf16[64,2048]{1,0:T(8,128)(2,1)S(1)}, u32[]{:S(2)}, u32[]{:S(2)}) collective-permute-start(bf16[64,2048]{1,0:T(8,128)(2,1)S(1)} %get-tuple-element.100), channel_id=1, source_target_pairs={{0,3},{1,2},{2,1},{3,0},{4,7},{5,6},{6,5},{7,4},{8,11},{9,10},{10,... | collective-permute-start | bytes 786440 | tf_op jit(solution)/shard_map/ppermute | solution.py:516
  111.0 11.1 %collective-permute-start.25 = (bf16[64,2048]{1,0:T(8,128)(2,1)S(1)}, bf16[64,2048]{1,0:T(8,128)(2,1)S(1)}, u32[]{:S(2)}, u32[]{:S(2)}) collective-permute-start(bf16[64,2048]{1,0:T(8,128)(2,1)S(1)} %get-tuple-element.106), channel_id=1, source_target_pairs={{0,1},{1,0},{2,3},{3,2},{4,5},{5,4},{6,7},{7,6},{8,9},{9,8},{10,11... | collective-permute-start | bytes 786440 | tf_op jit(solution)/shard_map/ppermute | solution.py:516
  112.9 10.4 %collective-permute-start.26 = (bf16[64,2048]{1,0:T(8,128)(2,1)S(1)}, bf16[64,2048]{1,0:T(8,128)(2,1)S(1)}, u32[]{:S(2)}, u32[]{:S(2)}) collective-permute-start(bf16[64,2048]{1,0:T(8,128)(2,1)S(1)} %get-tuple-element.107), channel_id=1, source_target_pairs={{0,2},{1,3},{2,0},{3,1},{4,6},{5,7},{6,4},{7,5},{8,10},{9,11},{10,... | collective-permute-start | bytes 786440 | tf_op jit(solution)/shard_map/ppermute | solution.py:516
  116.0 34.5 %collective-permute-start.29 = (bf16[2,64,2048]{2,1,0:T(8,128)(2,1)S(1)}, bf16[2,64,2048]{2,1,0:T(8,128)(2,1)S(1)}, u32[]{:S(2)}, u32[]{:S(2)}) collective-permute-start(bf16[2,64,2048]{2,1,0:T(8,128)(2,1)S(1)} %get-tuple-element.109), channel_id=1, source_target_pairs={{0,1},{1,0},{2,3},{3,2},{4,5},{5,4},{6,7},{7,6},{8,9},{9,8},{10,11... | collective-permute-start | bytes 1572872 | tf_op jit(solution)/shard_map/ppermute | solution.py:516
  117.6 32.8 %collective-permute-start.24 = (bf16[128,2048]{1,0:T(8,128)(2,1)S(1)}, bf16[128,2048]{1,0:T(8,128)(2,1)S(1)}, u32[]{:S(2)}, u32[]{:S(2)}) collective-permute-start(bf16[128,2048]{1,0:T(8,128)(2,1)S(1)} %expand.5.refs_4_), channel_id=1, source_target_pairs={{0,8},{1,9},{2,10},{3,11},{4,12},{5,13},{6,14},{7,15},{8,0},{9,1},... | collective-permute-start | bytes 1572872 | tf_op jit(solution)/shard_map/ppermute | solution.py:516
  121.1 29.4 %collective-permute-start.30 = (bf16[2,64,2048]{2,1,0:T(8,128)(2,1)S(1)}, bf16[2,64,2048]{2,1,0:T(8,128)(2,1)S(1)}, u32[]{:S(2)}, u32[]{:S(2)}) collective-permute-start(bf16[2,64,2048]{2,1,0:T(8,128)(2,1)S(1)} %get-tuple-element.110), channel_id=1, source_target_pairs={{0,2},{1,3},{2,0},{3,1},{4,6},{5,7},{6,4},{7,5},{8,10},{9,11},{10,... | collective-permute-start | bytes 1572872 | tf_op jit(solution)/shard_map/ppermute | solution.py:516
  122.1 28.4 %collective-permute-start.31 = (bf16[2,64,2048]{2,1,0:T(8,128)(2,1)S(1)}, bf16[2,64,2048]{2,1,0:T(8,128)(2,1)S(1)}, u32[]{:S(2)}, u32[]{:S(2)}) collective-permute-start(bf16[2,64,2048]{2,1,0:T(8,128)(2,1)S(1)} %get-tuple-element.111), channel_id=1, source_target_pairs={{0,3},{1,2},{2,1},{3,0},{4,7},{5,6},{6,5},{7,4},{8,11},{9,10},{10,... | collective-permute-start | bytes 1572872 | tf_op jit(solution)/shard_map/ppermute | solution.py:516
  123.3 21.9 %collective-permute-start.27 = (bf16[64,2048]{1,0:T(8,128)(2,1)S(1)}, bf16[64,2048]{1,0:T(8,128)(2,1)S(1)}, u32[]{:S(2)}, u32[]{:S(2)}) collective-permute-start(bf16[64,2048]{1,0:T(8,128)(2,1)S(1)} %get-tuple-element.108), channel_id=1, source_target_pairs={{0,3},{1,2},{2,1},{3,0},{4,7},{5,6},{6,5},{7,4},{8,11},{9,10},{10,... | collective-permute-start | bytes 786440 | tf_op jit(solution)/shard_map/ppermute | solution.py:516
  146.9 32.5 %collective-permute-start.28 = (bf16[128,2048]{1,0:T(8,128)(2,1)}, bf16[128,2048]{1,0:T(8,128)(2,1)}, u32[]{:S(2)}, u32[]{:S(2)}) collective-permute-start(bf16[128,2048]{1,0:T(8,128)(2,1)} %expand.6.refs_1_), channel_id=1, source_target_pairs={{0,12},{1,13},{2,14},{3,15},{4,8},{5,9},{6,10},{7,11},{8,4},{9,5},... | collective-permute-start | bytes 1572872 | tf_op jit(solution)/shard_map/ppermute | solution.py:516
  150.5 5.5 %copy-start = (f32[128,2048]{1,0:T(8,128)}, f32[128,2048]{1,0:T(8,128)S(1)}, u32[]{:S(2)}) copy-start(f32[128,2048]{1,0:T(8,128)S(1)} %total.2.refs_8_.own_ref) | copy-start | bytes 3145732
  156.1 11.7 %collective-permute-start.32 = (bf16[64,2048]{1,0:T(8,128)(2,1)S(1)}, bf16[64,2048]{1,0:T(8,128)(2,1)S(1)}, u32[]{:S(2)}, u32[]{:S(2)}) collective-permute-start(bf16[64,2048]{1,0:T(8,128)(2,1)S(1)} %get-tuple-element.113), channel_id=1, source_target_pairs={{0,1},{1,0},{2,3},{3,2},{4,5},{5,4},{6,7},{7,6},{8,9},{9,8},{10,11... | collective-permute-start | bytes 786440 | tf_op jit(solution)/shard_map/ppermute | solution.py:516
  157.9 9.9 %collective-permute-start.33 = (bf16[64,2048]{1,0:T(8,128)(2,1)S(1)}, bf16[64,2048]{1,0:T(8,128)(2,1)S(1)}, u32[]{:S(2)}, u32[]{:S(2)}) collective-permute-start(bf16[64,2048]{1,0:T(8,128)(2,1)S(1)} %get-tuple-element.114), channel_id=1, source_target_pairs={{0,2},{1,3},{2,0},{3,1},{4,6},{5,7},{6,4},{7,5},{8,10},{9,11},{10,... | collective-permute-start | bytes 786440 | tf_op jit(solution)/shard_map/ppermute | solution.py:516
  159.8 8.0 %collective-permute-start.34 = (bf16[64,2048]{1,0:T(8,128)(2,1)S(1)}, bf16[64,2048]{1,0:T(8,128)(2,1)S(1)}, u32[]{:S(2)}, u32[]{:S(2)}) collective-permute-start(bf16[64,2048]{1,0:T(8,128)(2,1)S(1)} %get-tuple-element.115), channel_id=1, source_target_pairs={{0,3},{1,2},{2,1},{3,0},{4,7},{5,6},{6,5},{7,4},{8,11},{9,10},{10,... | collective-permute-start | bytes 786440 | tf_op jit(solution)/shard_map/ppermute | solution.py:516
  167.6 8.0 %collective-permute-start.36 = (bf16[1024,2304]{1,0:T(8,128)(2,1)S(1)}, bf16[1024,2304]{1,0:T(8,128)(2,1)S(1)}, u32[]{:S(2)}, u32[]{:S(2)}) collective-permute-start(bf16[1024,2304]{1,0:T(8,128)(2,1)S(1)} %lend.1.refs_4_), channel_id=1, source_target_pairs={{0,16},{16,0},{1,17},{17,1},{2,18},{18,2},{3,19},{19,3},{4,20},{20... | collective-permute-start | bytes 14155784 | tf_op jit(solution)/shard_map/ppermute | solution.py:594
  168.8 14.4 %collective-permute-start.35 = (bf16[128,2048]{1,0:T(8,128)(2,1)S(1)}, bf16[128,2048]{1,0:T(8,128)(2,1)S(1)}, u32[]{:S(2)}, u32[]{:S(2)}) collective-permute-start(bf16[128,2048]{1,0:T(8,128)(2,1)S(1)} %expand.7.refs_16_), channel_id=1, source_target_pairs={{0,4},{1,5},{2,6},{3,7},{4,0},{5,1},{6,2},{7,3},{8,12},{9,13},{10,... | collective-permute-start | bytes 1572872 | tf_op jit(solution)/shard_map/ppermute | solution.py:516
  175.6 7.5 %copy-start.1 = (f32[128,2048]{1,0:T(8,128)S(1)}, f32[128,2048]{1,0:T(8,128)}, u32[]{:S(2)}) copy-start(f32[128,2048]{1,0:T(8,128)} %copy-done) | copy-start | bytes 3145732

commit v3 on v2

--- a/solution.py
+++ b/solution.py
@@ -42,7 +42,7 @@
     return pltpu.VMEM(shape, dtype)
 
 
-def pack_kernel(in_ref, experts_ref, mixing_ref, out_ref, block_ref, sems):
+def pack_kernel(in_ref, experts_ref, mixing_ref, out_ref, meta_ref, block_ref, sems):
     tokens, model = in_ref.shape
     rows = pltpu.make_async_copy(in_ref, out_ref.at[:tokens], sems.at[0])
     rows.start()
@@ -54,6 +54,7 @@
     if META > 4 * mixing.shape[0]:
         block.append(jnp.zeros((META - 4 * mixing.shape[0], tokens), F32))
     block_ref[:, :tokens] = jnp.concatenate(block, axis=0).astype(BF16)
+    meta_ref[...] = block_ref[:, :tokens]
     block_ref[:, tokens:] = jnp.zeros((META, model - tokens), BF16)
     routing = pltpu.make_async_copy(block_ref, out_ref.at[tokens:], sems.at[1])
     routing.start()
@@ -65,9 +66,9 @@
     rows, model = tokens.shape
     return pl.pallas_call(
         pack_kernel,
-        out_shape=array((rows + META, model)),
+        out_shape=[array((rows + META, model)), array((META, rows))],
         in_specs=[HBM, VMEM, VMEM],
-        out_specs=HBM,
+        out_specs=[HBM, VMEM],
         scratch_shapes=[pltpu.VMEM((META, model), BF16), pltpu.SemaphoreType.DMA((2,))],
         compiler_params=PARAMS,
         cost_estimate=estimate(flops),
@@ -98,10 +99,16 @@
     return jnp.concatenate(onehot, axis=0), jnp.concatenate(slot_weight, axis=0)
 
 
-def select_kernel(count, cap, top, parts, copied, ids_ref, *refs):
-    packed_ref, cots_ref = refs[:2]
-    sources = refs[2 : 2 + copied]
-    targets, sems = refs[-1 - copied : -1], refs[-1]
+def select_kernel(count, cap, top, parts, copied, join, ids_ref, *refs):
+    packed_ref, cots_ref, meta_ref = refs[:3]
+    sources = list(refs[3 : 3 + copied])
+    targets, sems = list(refs[-1 - copied : -1]), refs[-1]
+    if join:
+        rows, width = sources[0].shape
+        whole = targets[0]
+        targets[0] = whole.at[:rows]
+        sources.append(meta_ref)
+        targets.append(whole.at[rows:, : meta_ref.shape[1]])
     outs = refs[-1 - copied - count : -1 - copied]
     copies = [
         pltpu.make_async_copy(source, target, sems.at[which])
@@ -110,8 +117,9 @@
     for copy in copies:
         copy.start()
     model = packed_ref.shape[1]
-    tokens = packed_ref.shape[0] - META
-    masks, weight = slot_masks(ids_ref, packed_ref[tokens:, :tokens], count, cap, top)
+    tokens = meta_ref.shape[1] if meta_ref.shape[0] == META else packed_ref.shape[0] - META
+    block = meta_ref[...] if meta_ref.shape[0] == META else packed_ref[tokens:, :tokens]
+    masks, weight = slot_masks(ids_ref, block, count, cap, top)
     onehot = masks.astype(BF16)
     step = min(512, model)
     for start in range(0, model, step):
@@ -128,21 +136,25 @@
         copy.wait()
 
 
-def select(ids, packed, cots, cap, top, parts, copied, flops, after):
+def select(ids, packed, cots, meta, cap, top, parts, copied, join, flops, after):
     count = ids.shape[0] - 2
     model = packed.shape[1]
     result = pl.pallas_call(
-        functools.partial(select_kernel, count, cap, top, parts, len(copied)),
+        functools.partial(select_kernel, count, cap, top, parts, len(copied), join),
         out_shape=[array((len(parts), cap, model))] * count
-        + [array(value.shape) for value in copied],
-        in_specs=[SMEM, VMEM, VMEM if "cots" in parts else ANYWHERE]
+        + [
+            array((value.shape[0] + META * (join and which == 0), value.shape[1]))
+            for which, value in enumerate(copied)
+        ],
+        in_specs=[SMEM, VMEM if "rows" in parts or meta is None else ANYWHERE]
+        + [VMEM if "cots" in parts else ANYWHERE, ANYWHERE if meta is None else VMEM]
         + [ANYWHERE] * (len(copied) + len(after)),
         out_specs=[VMEM] * count + [HBM] * len(copied),
-        scratch_shapes=[pltpu.SemaphoreType.DMA((max(1, len(copied)),))],
+        scratch_shapes=[pltpu.SemaphoreType.DMA((1 + len(copied),))],
         compiler_params=PARAMS,
         cost_estimate=estimate(flops),
         name="select",
-    )(ids, packed, cots, *copied, *after)
+    )(ids, packed, cots, packed if meta is None else meta, *copied, *after)
     return result[:count], result[count:]
 
 
@@ -432,23 +444,24 @@
         out[:, columns] = value.astype(out.dtype)
 
 
-def expand(ids, packed, back, top, dtype, flops, after):
+def expand(ids, packed, meta, back, top, dtype, flops, after):
     count = len(back)
     cap, model = back[0].shape
-    tokens = packed.shape[0] - META
+    tokens = packed.shape[0] - META if meta is None else meta.shape[1]
+    at = tokens // META if meta is None else 0
     whole = lambda *shape: pl.BlockSpec(shape, lambda s: (0, 0))
     return pl.pallas_call(
         functools.partial(expand_kernel, count, top),
         grid=(1,),
         out_shape=array((tokens, model), dtype),
-        in_specs=[SMEM, pl.BlockSpec((META, tokens), lambda s: (tokens // META, 0))]
+        in_specs=[SMEM, pl.BlockSpec((META, tokens), lambda s: (at, 0))]
         + [whole(cap, model)] * count
         + [ANYWHERE],
         out_specs=whole(tokens, model),
         compiler_params=PARAMS,
         cost_estimate=estimate(flops),
         name="expand",
-    )(ids, packed, *back, after)
+    )(ids, packed if meta is None else meta, *back, after)
 
 
 def total_kernel(count, own_ref, *refs):
@@ -523,7 +536,8 @@
     ids = jnp.concatenate([plane_ids, jnp.stack([core, 1 - core])])
     chain = FOUR_PLANES if outer == 4 else many_planes(outer)
     planes = [plane for kind, plane, _ in chain if kind == "expert"]
-    packed = {0: pack(tokens, experts, mixing)}
+    first, routing = pack(tokens, experts, mixing)
+    packed, metas = {0: first}, {}
     cots = {0: cotangent}
     arrived, returned, partial, saved, begun = {}, {}, [], {}, {}
     late = LATE if outer == 4 else ()
@@ -531,7 +545,11 @@
     split = [plane for kind, plane, _ in chain if kind == "rows"]
     for plane in planes[1:]:
         if plane == plane & -plane and plane not in late_planes:
-            packed[plane] = swap(packed[0], plane * inner)
+            if plane in split:
+                packed[plane] = swap(tokens, plane * inner)
+                metas[plane] = swap(routing, plane * inner)
+            else:
+                packed[plane] = swap(packed[0], plane * inner)
             if plane not in split:
                 cots[plane] = swap(cotangent, plane * inner)
 
@@ -549,7 +567,11 @@
         if waiting:
             copied += [packed[0], cotangent]
         value = cots.get(plane, cotangent)
-        sent, copies = select(ids, packed[plane], value, cap, top, parts, copied, flops, last)
+        meta = metas.get(plane)
+        join = meta is not None and bool(onward) and "rows" in parts
+        sent, copies = select(
+            ids, packed[plane], value, meta, cap, top, parts, copied, join, flops, last
+        )
         copies = list(copies)
         arrived[plane, kind] = swap_inner(sent)
         for part, held in (("rows", packed), ("cots", cots)):
@@ -582,9 +604,9 @@
             returned[plane] = swap_inner(pair_cot)
             last = pair_cot[0]
         elif kind == "own":
-            own = last = expand(ids, packed[0], returned[0], top, F32, flops, last)
+            own = last = expand(ids, packed[0], None, returned[0], top, F32, flops, last)
         elif kind == "expand":
-            last = expand(ids, packed[plane], returned[plane], top, BF16, flops, last)
+            last = expand(ids, packed[plane], metas.get(plane), returned[plane], top, BF16, flops, last)
             partial.append(swap(last, plane * inner))
         elif kind == "total":
             own = last = total(own, partial[:plane], F32, flops, last)

time: 185 us -> 182 us (0.984)
  starting transfers between devices: 50.3 us -> 47.5 us
    ppermute x36 -> x37, starting transfers between devices: 50.3 us -> 47.4 us  [swap(): return lax.ppermute(value, 'expert', pairs)]
    ppermute x36 -> x37, waiting for transfers between devices: 72.2 us -> 72.8 us  [swap(): return lax.ppermute(value, 'expert', pairs)]
  transfers between devices with their start and end apart: 37 -> 38, of which waited for: 10 -> 16; matrix products, arithmetic and copies ran while one was open for 0% -> 0% of each run, Pallas kernels for 30% -> 31%
where the time goes in v3:
time: 182 us
  waiting for transfers between devices  72.8 us (40%)
  Pallas kernels  58.2 us (32%)
  starting transfers between devices  47.5 us (26%)
  local copies, waits for them, and re-layouts  2.42 us (1%)
    ppermute x37, waiting for transfers between devices, swap(): return lax.ppermute(value, 'expert', pairs)  72.8 us
    ppermute x37, starting transfers between devices, swap(): return lax.ppermute(value, 'expert', pairs)  47.4 us
    pallas_call x4, Pallas kernels, expert(): pl.pallas_call(functools.partial(expert_kernel, count, bool(begun)), in_s...  19.6 us
    pallas_call x1, Pallas kernels, lend(): pl.pallas_call(functools.partial(lend_kernel, len(saved)), in_specs=[SMEM...  7.84 us
    pallas_call x5, Pallas kernels, select(): pl.pallas_call(functools.partial(select_kernel, count, cap, top, parts, l...  6.68 us
    pallas_call x1, Pallas kernels, share(): pl.pallas_call(functools.partial(share_kernel, len(saved)), in_specs=[SME...  5.7 us
    pallas_call x4, Pallas kernels, expand(): pl.pallas_call(functools.partial(expand_kernel, count, top), grid=(1,), o...  4.92 us
    pallas_call x1, Pallas kernels, flip(): pl.pallas_call(flip_kernel, in_specs=[HBM] * 3 + [ANYWHERE], out_specs=[V...  4.67 us
  transfers between devices with their start and end apart: 38, of which 16 were waited for; matrix products, arithmetic and copies ran while one was open for 0% of the time, Pallas kernels for 31%

profile of v3, /device:TPU:0, one launch (start us, length us, event | category | flops | bytes accessed | tf_op | source)
XLA Modules:
  0.0 181.9 jit_solution(920781192821565658)
XLA Ops:
  0.6 4.1 %collective-permute-start.3 = (bf16[128,2048]{1,0:T(8,128)(2,1)}, bf16[128,2048]{1,0:T(8,128)(2,1)S(1)}, u32[]{:S(2)}, u32[]{:S(2)}) collective-permute-start(bf16[128,2048]{1,0:T(8,128)(2,1)} %in_ref.1), channel_id=1, source_target_pairs={{0,8},{1,9},{2,10},{3,11},{4,12},{5,13},{6,14},{7,15},{8,0},{9,1},... | collective-permute-start | bytes 1572872 | tf_op jit(solution)/shard_map/ppermute | solution.py:529
  4.8 0.7 copy-done.4
  5.5 0.7 copy-done.5
  6.2 1.1 pack.1
  7.3 1.0 copy-done.2
  8.3 1.4 select.5
  9.7 1.6 collective-permute-start
  11.2 1.5 collective-permute-start.1
  13.3 4.7 %flip.1 = (bf16[2048,768]{1,0:T(8,128)(2,1)S(1)}, bf16[2048,768]{1,0:T(8,128)(2,1)S(1)}, bf16[1536,2048]{1,0:T(8,128)(2,1)S(1)}, bf16[2048,768]{1,0:T(8,128)(2,1)S(1)}) custom-call(bf16[2048,768]{1,0:T(8,128)(2,1)} %bitcast.12, bf16[2048,768]{1,0:T(8,128)(2,1)} %bitcast.13, bf16[768,2048]{1,0:T(8,128)(2,1)} %bitcast.14, ...), custom_call_target="tpu_custom_call" | custom-call | flops 1 | bytes 1 | tf_op jit(solution)/shard_map/flip/pallas_call | solution.py:185
  18.0 10.3 %collective-permute-done.4.refs_2_.meta_ref = bf16[16,128]{1,0:T(8,128)(2,1)S(1)} collective-permute-done((bf16[16,128]{1,0:T(8,128)(2,1)S(1)}, bf16[16,128]{1,0:T(8,128)(2,1)S(1)}, u32[]{:S(2)}, u32[]{:S(2)}) %collective-permute-start.4) | collective-permute-done | bytes 4128 | tf_op jit(solution)/shard_map/ppermute | solution.py:529
  28.3 1.2 select.6
  29.5 1.6 collective-permute-start.8
  31.1 1.5 collective-permute-start.9
  33.0 2.7 %collective-permute-done.1.refs_2_ = bf16[2,64,2048]{2,1,0:T(8,128)(2,1)S(1)} collective-permute-done((bf16[2,64,2048]{2,1,0:T(8,128)(2,1)S(1)}, bf16[2,64,2048]{2,1,0:T(8,128)(2,1)S(1)}, u32[]{:S(2)}, u32[]{:S(2)}) %collective-permute-start.1) | collective-permute-done | bytes 524320 | tf_op jit(solution)/shard_map/ppermute | solution.py:529
  36.1 0.8 collective-permute-done.2.refs_3_
  36.8 1.6 collective-permute-start.15
  38.4 5.2 %expert.4 = (bf16[64,2048]{1,0:T(8,128)(2,1)S(1)}, bf16[64,2048]{1,0:T(8,128)(2,1)S(1)}, bf16[64,2048]{1,0:T(8,128)(2,1)S(1)}, bf16[64,2048]{1,0:T(8,128)(2,1)S(...) custom-call(bf16[2,64,2048]{2,1,0:T(8,128)(2,1)S(1)} %get-tuple-elem, ...), custom_call_target="tpu_custom_call" | custom-call | flops 1 | bytes 1 | tf_op jit(solution)/shard_map/expert/pallas_call | solution.py:278
  43.7 1.6 collective-permute-start.5
  45.5 2.5 %collective-permute-start.6 = (bf16[64,2048]{1,0:T(8,128)(2,1)S(1)}, bf16[64,2048]{1,0:T(8,128)(2,1)S(1)}, u32[]{:S(2)}, u32[]{:S(2)}) collective-permute-start(bf16[64,2048]{1,0:T(8,128)(2,1)S(1)} %get-tuple-element.86), channel_id=1, source_target_pairs={{0,2},{1,3},{2,0},{3,1},{4,6},{5,7},{6,4},{7,5},{8,10},{9,11},{10,... | collective-permute-start | bytes 786440 | tf_op jit(solution)/shard_map/ppermute | solution.py:529
  48.1 1.4 collective-permute-start.7
  49.6 1.8 %begin.1 = (bf16[256,2048]{1,0:T(8,128)(2,1)S(1)}, f32[256,768]{1,0:T(8,128)S(1)}, f32[256,768]{1,0:T(8,128)S(1)}) custom-call(bf16[1,64,2048]{2,1,0:T(8,128)(2,1)S(1)} %get-tuple-element.83.refs_8_.refs_0_, bf16[1,64,2048]{2,1,0:T(8,128)(2,1)S(1)} %collective-permute-done.8.refs_1_, bf16[1,64,2048]{2,1,0:T(8,128)(2,1)S(1)} %collective-permute-done.9.refs_2_, ...), custom_call_target="tpu_custom_call" | custom-call | flops 17179869184 | bytes 1 | tf_op jit(solution)/shard_map/begin/pallas_call | solution.py:218
  51.4 1.6 collective-permute-done.5.refs_1_
  53.0 5.7 %collective-permute-done.6.refs_2_ = bf16[64,2048]{1,0:T(8,128)(2,1)S(1)} collective-permute-done((bf16[64,2048]{1,0:T(8,128)(2,1)S(1)}, bf16[64,2048]{1,0:T(8,128)(2,1)S(1)}, u32[]{:S(2)}, u32[]{:S(2)}) %collective-permute-start.6) | collective-permute-done | bytes 262176 | tf_op jit(solution)/shard_map/ppermute | solution.py:529
  58.7 1.0 expand.4.refs_4_.own_ref
  59.8 1.3 select.7
  61.1 2.3 %collective-permute-start.16 = (bf16[128,2048]{1,0:T(8,128)(2,1)S(1)}, bf16[128,2048]{1,0:T(8,128)(2,1)S(1)}, u32[]{:S(2)}, u32[]{:S(2)}) collective-permute-start(bf16[128,2048]{1,0:T(8,128)(2,1)S(1)} %get-tuple-element.99), channel_id=1, source_target_pairs={{0,4},{1,5},{2,6},{3,7},{4,0},{5,1},{6,2},{7,3},{8,12},{9,13},{10,... | collective-permute-start | bytes 1572872 | tf_op jit(solution)/shard_map/ppermute | solution.py:529
  63.4 0.8 collective-permute-start.12
  64.2 1.1 collective-permute-start.13
  65.4 1.5 collective-permute-start.14
  66.8 6.0 %collective-permute-done.16.refs_1_ = bf16[128,2048]{1,0:T(8,128)(2,1)S(1)} collective-permute-done((bf16[128,2048]{1,0:T(8,128)(2,1)S(1)}, bf16[128,2048]{1,0:T(8,128)(2,1)S(1)}, u32[]{:S(2)}, u32[]{:S(2)}) %collective-permute-start.16) | collective-permute-done | bytes 524320 | tf_op jit(solution)/shard_map/ppermute | solution.py:529
  72.9 1.4 select.8
  74.3 3.2 %collective-permute-start.22 = (bf16[2,64,2048]{2,1,0:T(8,128)(2,1)S(1)}, bf16[2,64,2048]{2,1,0:T(8,128)(2,1)S(1)}, u32[]{:S(2)}, u32[]{:S(2)}) collective-permute-start(bf16[2,64,2048]{2,1,0:T(8,128)(2,1)S(1)} %get-tuple-element.105), channel_id=1, source_target_pairs={{0,1},{1,0},{2,3},{3,2},{4,5},{5,4},{6,7},{7,6},{8,9},{9,8},{10,11... | collective-permute-start | bytes 1572872 | tf_op jit(solution)/shard_map/ppermute | solution.py:529
  78.1 1.0 collective-permute-start.24
  79.1 1.7 collective-permute-start.21
  81.1 3.6 %expert.5 = (bf16[64,2048]{1,0:T(8,128)(2,1)S(1)}, bf16[64,2048]{1,0:T(8,128)(2,1)S(1)}, bf16[64,2048]{1,0:T(8,128)(2,1)S(1)}, bf16[64,2048]{1,0:T(8,128)(2,1)S(...) custom-call(bf16[1,64,2048]{2,1,0:T(8,128)(2,1)S(1)} %get-tuple-element.93.refs_3_.re, ...), custom_call_target="tpu_custom_call" | custom-call | flops 536870912 | bytes 1 | tf_op jit(solution)/shard_map/expert/pallas_call | solution.py:278
  84.6 5.7 %collective-permute-done.22.refs_1_ = bf16[2,64,2048]{2,1,0:T(8,128)(2,1)S(1)} collective-permute-done((bf16[2,64,2048]{2,1,0:T(8,128)(2,1)S(1)}, bf16[2,64,2048]{2,1,0:T(8,128)(2,1)S(1)}, u32[]{:S(2)}, u32[]{:S(2)}) %collective-permute-start.22) | collective-permute-done | bytes 524320 | tf_op jit(solution)/shard_map/ppermute | solution.py:529
  90.3 2.0 %collective-permute-start.17 = (bf16[64,2048]{1,0:T(8,128)(2,1)S(1)}, bf16[64,2048]{1,0:T(8,128)(2,1)S(1)}, u32[]{:S(2)}, u32[]{:S(2)}) collective-permute-start(bf16[64,2048]{1,0:T(8,128)(2,1)S(1)} %get-tuple-element.102), channel_id=1, source_target_pairs={{0,1},{1,0},{2,3},{3,2},{4,5},{5,4},{6,7},{7,6},{8,9},{9,8},{10,11... | collective-permute-start | bytes 786440 | tf_op jit(solution)/shard_map/ppermute | solution.py:529
  92.4 11.5 %collective-permute-done.23.refs_2_ = bf16[2,64,2048]{2,1,0:T(8,128)(2,1)S(1)} collective-permute-done((bf16[2,64,2048]{2,1,0:T(8,128)(2,1)S(1)}, bf16[2,64,2048]{2,1,0:T(8,128)(2,1)S(1)}, u32[]{:S(2)}, u32[]{:S(2)}) %collective-permute-start.23) | collective-permute-done | bytes 524320 | tf_op jit(solution)/shard_map/ppermute | solution.py:529
  103.9 0.7 collective-permute-start.19
  104.5 5.3 %expert.6 = (bf16[64,2048]{1,0:T(8,128)(2,1)S(1)}, bf16[64,2048]{1,0:T(8,128)(2,1)S(1)}, bf16[64,2048]{1,0:T(8,128)(2,1)S(1)}, bf16[64,2048]{1,0:T(8,128)(2,1)S(...) custom-call(bf16[2,64,2048]{2,1,0:T(8,128)(2,1)S(1)} %get-tuple-elem, ...), custom_call_target="tpu_custom_call" | custom-call | flops 1 | bytes 1 | tf_op jit(solution)/shard_map/expert/pallas_call | solution.py:278
  109.8 2.9 %collective-permute-start.26 = (bf16[64,2048]{1,0:T(8,128)(2,1)S(1)}, bf16[64,2048]{1,0:T(8,128)(2,1)S(1)}, u32[]{:S(2)}, u32[]{:S(2)}) collective-permute-start(bf16[64,2048]{1,0:T(8,128)(2,1)S(1)} %get-tuple-element.110), channel_id=1, source_target_pairs={{0,1},{1,0},{2,3},{3,2},{4,5},{5,4},{6,7},{7,6},{8,9},{9,8},{10,11... | collective-permute-start | bytes 786440 | tf_op jit(solution)/shard_map/ppermute | solution.py:529
  112.7 1.4 select.9
  114.1 0.6 collective-permute-start.30
  114.8 0.7 collective-permute-done.18.refs_2_
  115.5 1.0 expand.5.refs_4_
  116.6 1.5 collective-permute-start.31
  118.1 2.1 %collective-permute-done.26.refs_1_ = bf16[64,2048]{1,0:T(8,128)(2,1)S(1)} collective-permute-done((bf16[64,2048]{1,0:T(8,128)(2,1)S(1)}, bf16[64,2048]{1,0:T(8,128)(2,1)S(1)}, u32[]{:S(2)}, u32[]{:S(2)}) %collective-permute-start.26) | collective-permute-done | bytes 262176 | tf_op jit(solution)/shard_map/ppermute | solution.py:529
  120.2 1.2 collective-permute-start.32
  121.4 0.6 collective-permute-done.27.refs_2_
  122.0 1.2 collective-permute-start.28
  123.1 20.8 %collective-permute-done.28.refs_3_ = bf16[64,2048]{1,0:T(8,128)(2,1)S(1)} collective-permute-done((bf16[64,2048]{1,0:T(8,128)(2,1)S(1)}, bf16[64,2048]{1,0:T(8,128)(2,1)S(1)}, u32[]{:S(2)}, u32[]{:S(2)}) %collective-permute-start.28) | collective-permute-done | bytes 262176 | tf_op jit(solution)/shard_map/ppermute | solution.py:529
  144.0 1.8 %expand.6.refs_1_ = bf16[128,2048]{1,0:T(8,128)(2,1)} custom-call(s32[6]{0:T(128)S(1)} %pad_add_fusion.ids_ref, bf16[144,2048]{1,0:T(8,128)(2,1)S(1)} %collective-permute-done.15.refs_0_.refs_2_.meta_ref, bf16[64,2048]{1,0:T(8,128)(2,1)S(1)} %get-tuple-element.108.refs_3_.refs_0_, bf16[64,2048]{1,0:T(8,128)(2,1)S(1)} %collective-permute-done.26.refs_1_, ...), custom_call_target="tpu_custom_call" | custom-call | flops 1 | bytes 1 | tf_op jit(solution)/shard_map/expand/pallas_call | solution.py:453
  145.9 0.8 collective-permute-done.31.refs_2_
  146.8 5.5 %expert.7 = (bf16[64,2048]{1,0:T(8,128)(2,1)S(1)}, bf16[64,2048]{1,0:T(8,128)(2,1)S(1)}, bf16[64,2048]{1,0:T(8,128)(2,1)S(1)}, bf16[64,2048]{1,0:T(8,128)(2,1)S(...) custom-call(bf16[2,64,2048]{2,1,0:T(8,128)(2,1)S(1)} %get-tuple-elem, ...), custom_call_target="tpu_custom_call" | custom-call | flops 1 | bytes 1 | tf_op jit(solution)/shard_map/expert/pallas_call | solution.py:278
  152.3 1.0 collective-permute-start.33
  153.3 2.0 %collective-permute-start.34 = (bf16[64,2048]{1,0:T(8,128)(2,1)S(1)}, bf16[64,2048]{1,0:T(8,128)(2,1)S(1)}, u32[]{:S(2)}, u32[]{:S(2)}) collective-permute-start(bf16[64,2048]{1,0:T(8,128)(2,1)S(1)} %get-tuple-element.118), channel_id=1, source_target_pairs={{0,2},{1,3},{2,0},{3,1},{4,6},{5,7},{6,4},{7,5},{8,10},{9,11},{10,... | collective-permute-start | bytes 786440 | tf_op jit(solution)/shard_map/ppermute | solution.py:529
  155.2 0.6 collective-permute-start.35
  155.8 7.8 %lend.1.refs_4_ = bf16[1024,2304]{1,0:T(8,128)(2,1)S(1)} custom-call(s32[6]{0:T(128)S(1)} %pad_add_fusion.ids_ref, bf16[256,2048]{1,0:T(8,128)(2,1)S(1)} %get-tuple-element.120.refs_0_, bf16[256,2048]{1,0:T(8,128)(2,1)S(1)} %get-tuple-element.121.refs_1_, bf16[256,1536]{1,0:T(8,128)(2,1)S(1)} %get-tuple-element.122.refs_2_, ...), custom_call_target="tpu_custom_call" | custom-call | flops 137438953472 | bytes 1 | tf_op jit(solution)/shard_map/lend/pallas_call | solution.py:334
  163.8 1.0 expand.7.refs_16_
  164.8 2.5 %collective-permute-start.36 = (bf16[128,2048]{1,0:T(8,128)(2,1)S(1)}, bf16[128,2048]{1,0:T(8,128)(2,1)S(1)}, u32[]{:S(2)}, u32[]{:S(2)}) collective-permute-start(bf16[128,2048]{1,0:T(8,128)(2,1)S(1)} %expand.7.refs_16_), channel_id=1, source_target_pairs={{0,4},{1,5},{2,6},{3,7},{4,0},{5,1},{6,2},{7,3},{8,12},{9,13},{10,... | collective-permute-start | bytes 1572872 | tf_op jit(solution)/shard_map/ppermute | solution.py:529
  167.3 5.7 %share.1 = (f32[1024,1536]{1,0:T(8,128)S(1)}, f32[384,2048]{1,0:T(8,128)S(1)}) custom-call(s32[6]{0:T(128)S(1)} %pad_add_fusion.ids_ref, bf16[256,2048]{1,0:T(8,128)(2,1)S(1)} %get-tuple-element.120.refs_0_, bf16[256,2048]{1,0:T(8,128)(2,1)S(1)} %get-tuple-element.121.refs_1_, bf16[256,1536]{1,0:T(8,128)(2,1)S(1)} %get-tuple-element.122.refs_2_, ...), custom_call_target="tpu_custom_call" | custom-call | flops 1073741824 | bytes 1 | tf_op jit(solution)/shard_map/share/pallas_call | solution.py:367
  173.0 3.8 %finish.1 = (f32[1024,768]{1,0:T(8,128)}, f32[1024,768]{1,0:T(8,128)}, f32[384,2048]{1,0:T(8,128)}, f32[8,128]{1,0:T(8,128)S(1)}) custom-call(f32[1024,1536]{1,0:T(8,128)S(1)} %get-tuple-element.136.both_ref, f32[384,2048]{1,0:T(8,128)S(1)} %get-tuple-element.137.down_ref._, bf16[1024,2304]{1,0:T(8,128)(2,1)S(1)} %collective-permute-done.37.other, ...), custom_call_target="tpu_custom_call" | custom-call | flops 1 | bytes 1 | tf_op jit(solution)/shard_map/finish/pallas_call | solution.py:422
  176.8 3.0 %collective-permute-done.36.refs_1_ = bf16[128,2048]{1,0:T(8,128)(2,1)S(1)} collective-permute-done((bf16[128,2048]{1,0:T(8,128)(2,1)S(1)}, bf16[128,2048]{1,0:T(8,128)(2,1)S(1)}, u32[]{:S(2)}, u32[]{:S(2)}) %collective-permute-start.36) | collective-permute-done | bytes 524320 | tf_op jit(solution)/shard_map/ppermute | solution.py:529
  179.9 2.0 %total.3 = bf16[128,2048]{1,0:T(8,128)(2,1)} custom-call(f32[128,2048]{1,0:T(8,128)S(1)} %copy-done.1, bf16[128,2048]{1,0:T(8,128)(2,1)} %collective-permute-done.29.refs_0_, bf16[128,2048]{1,0:T(8,128)(2,1)S(1)} %collective-permute-done.36.refs_1_, f32[8,128]{1,0:T(8,128)S(1)} %get-tuple-element.138.refs_2_), custom_call_target="tpu_custom_call" | custom-call | flops 1 | bytes 1 | tf_op jit(solution)/shard_map/total/pallas_call | solution.py:475
  (47 shorter events, 2.9 us)
Async XLA Ops:
  0.6 27.7 %collective-permute-start.3 = (bf16[128,2048]{1,0:T(8,128)(2,1)}, bf16[128,2048]{1,0:T(8,128)(2,1)S(1)}, u32[]{:S(2)}, u32[]{:S(2)}) collective-permute-start(bf16[128,2048]{1,0:T(8,128)(2,1)} %in_ref.1), channel_id=1, source_target_pairs={{0,8},{1,9},{2,10},{3,11},{4,12},{5,13},{6,14},{7,15},{8,0},{9,1},... | collective-permute-start | bytes 1572872 | tf_op jit(solution)/shard_map/ppermute | solution.py:529
  4.8 0.7 copy-start.4
  5.5 0.7 copy-start.5
  7.2 1.0 copy-start.2
  9.7 22.9 %collective-permute-start = (bf16[2,64,2048]{2,1,0:T(8,128)(2,1)S(1)}, bf16[2,64,2048]{2,1,0:T(8,128)(2,1)S(1)}, u32[]{:S(2)}, u32[]{:S(2)}) collective-permute-start(bf16[2,64,2048]{2,1,0:T(8,128)(2,1)S(1)} %get-tuple-element.75), channel_id=1, source_target_pairs={{0,1},{1,0},{2,3},{3,2},{4,5},{5,4},{6,7},{7,6},{8,9},{9,8},{10,11... | collective-permute-start | bytes 1572872 | tf_op jit(solution)/shard_map/ppermute | solution.py:529
  11.2 24.5 %collective-permute-start.1 = (bf16[2,64,2048]{2,1,0:T(8,128)(2,1)S(1)}, bf16[2,64,2048]{2,1,0:T(8,128)(2,1)S(1)}, u32[]{:S(2)}, u32[]{:S(2)}) collective-permute-start(bf16[2,64,2048]{2,1,0:T(8,128)(2,1)S(1)} %get-tuple-element.76), channel_id=1, source_target_pairs={{0,2},{1,3},{2,0},{3,1},{4,6},{5,7},{6,4},{7,5},{8,10},{9,11},{10,... | collective-permute-start | bytes 1572872 | tf_op jit(solution)/shard_map/ppermute | solution.py:529
  12.8 24.1 %collective-permute-start.2 = (bf16[2,64,2048]{2,1,0:T(8,128)(2,1)S(1)}, bf16[2,64,2048]{2,1,0:T(8,128)(2,1)S(1)}, u32[]{:S(2)}, u32[]{:S(2)}) collective-permute-start(bf16[2,64,2048]{2,1,0:T(8,128)(2,1)S(1)} %get-tuple-element.77), channel_id=1, source_target_pairs={{0,3},{1,2},{2,1},{3,0},{4,7},{5,6},{6,5},{7,4},{8,11},{9,10},{10,... | collective-permute-start | bytes 1572872 | tf_op jit(solution)/shard_map/ppermute | solution.py:529
  13.2 15.0 %collective-permute-start.4 = (bf16[16,128]{1,0:T(8,128)(2,1)S(1)}, bf16[16,128]{1,0:T(8,128)(2,1)S(1)}, u32[]{:S(2)}, u32[]{:S(2)}) collective-permute-start(bf16[16,128]{1,0:T(8,128)(2,1)S(1)} %get-tuple-element.82), channel_id=1, source_target_pairs={{0,8},{1,9},{2,10},{3,11},{4,12},{5,13},{6,14},{7,15},{8,0},{9,1},... | collective-permute-start | bytes 12296 | tf_op jit(solution)/shard_map/ppermute | solution.py:529
  29.5 14.2 %collective-permute-start.8 = (bf16[1,64,2048]{2,1,0:T(8,128)(2,1)S(1)}, bf16[1,64,2048]{2,1,0:T(8,128)(2,1)S(1)}, u32[]{:S(2)}, u32[]{:S(2)}) collective-permute-start(bf16[1,64,2048]{2,1,0:T(8,128)(2,1)S(1)} %get-tuple-element.88), channel_id=1, source_target_pairs={{0,1},{1,0},{2,3},{3,2},{4,5},{5,4},{6,7},{7,6},{8,9},{9,8},{10,11... | collective-permute-start | bytes 786440 | tf_op jit(solution)/shard_map/ppermute | solution.py:529
  31.1 14.4 %collective-permute-start.9 = (bf16[1,64,2048]{2,1,0:T(8,128)(2,1)S(1)}, bf16[1,64,2048]{2,1,0:T(8,128)(2,1)S(1)}, u32[]{:S(2)}, u32[]{:S(2)}) collective-permute-start(bf16[1,64,2048]{2,1,0:T(8,128)(2,1)S(1)} %get-tuple-element.89), channel_id=1, source_target_pairs={{0,2},{1,3},{2,0},{3,1},{4,6},{5,7},{6,4},{7,5},{8,10},{9,11},{10,... | collective-permute-start | bytes 786440 | tf_op jit(solution)/shard_map/ppermute | solution.py:529
  32.6 15.5 %collective-permute-start.10 = (bf16[1,64,2048]{2,1,0:T(8,128)(2,1)S(1)}, bf16[1,64,2048]{2,1,0:T(8,128)(2,1)S(1)}, u32[]{:S(2)}, u32[]{:S(2)}) collective-permute-start(bf16[1,64,2048]{2,1,0:T(8,128)(2,1)S(1)} %get-tuple-element.90), channel_id=1, source_target_pairs={{0,3},{1,2},{2,1},{3,0},{4,7},{5,6},{6,5},{7,4},{8,11},{9,10},{10,... | collective-permute-start | bytes 786440 | tf_op jit(solution)/shard_map/ppermute | solution.py:529
  35.7 24.0 %collective-permute-start.11 = (bf16[128,2048]{1,0:T(8,128)(2,1)S(1)}, bf16[128,2048]{1,0:T(8,128)(2,1)S(1)}, u32[]{:S(2)}, u32[]{:S(2)}) collective-permute-start(bf16[128,2048]{1,0:T(8,128)(2,1)S(1)} %get-tuple-element.92), channel_id=1, source_target_pairs={{0,8},{1,9},{2,10},{3,11},{4,12},{5,13},{6,14},{7,15},{8,0},{9,1},... | collective-permute-start | bytes 1572872 | tf_op jit(solution)/shard_map/ppermute | solution.py:529
  36.8 30.0 %collective-permute-start.15 = (bf16[144,2048]{1,0:T(8,128)(2,1)S(1)}, bf16[144,2048]{1,0:T(8,128)(2,1)S(1)}, u32[]{:S(2)}, u32[]{:S(2)}) collective-permute-start(bf16[144,2048]{1,0:T(8,128)(2,1)S(1)} %get-tuple-element.98), channel_id=1, source_target_pairs={{0,4},{1,5},{2,6},{3,7},{4,0},{5,1},{6,2},{7,3},{8,12},{9,13},{10,... | collective-permute-start | bytes 1769480 | tf_op jit(solution)/shard_map/ppermute | solution.py:529
  43.7 9.3 %collective-permute-start.5 = (bf16[64,2048]{1,0:T(8,128)(2,1)S(1)}, bf16[64,2048]{1,0:T(8,128)(2,1)S(1)}, u32[]{:S(2)}, u32[]{:S(2)}) collective-permute-start(bf16[64,2048]{1,0:T(8,128)(2,1)S(1)} %get-tuple-element.85), channel_id=1, source_target_pairs={{0,1},{1,0},{2,3},{3,2},{4,5},{5,4},{6,7},{7,6},{8,9},{9,8},{10,11... | collective-permute-start | bytes 786440 | tf_op jit(solution)/shard_map/ppermute | solution.py:529
  45.5 13.2 %collective-permute-start.6 = (bf16[64,2048]{1,0:T(8,128)(2,1)S(1)}, bf16[64,2048]{1,0:T(8,128)(2,1)S(1)}, u32[]{:S(2)}, u32[]{:S(2)}) collective-permute-start(bf16[64,2048]{1,0:T(8,128)(2,1)S(1)} %get-tuple-element.86), channel_id=1, source_target_pairs={{0,2},{1,3},{2,0},{3,1},{4,6},{5,7},{6,4},{7,5},{8,10},{9,11},{10,... | collective-permute-start | bytes 786440 | tf_op jit(solution)/shard_map/ppermute | solution.py:529
  48.1 10.6 %collective-permute-start.7 = (bf16[64,2048]{1,0:T(8,128)(2,1)S(1)}, bf16[64,2048]{1,0:T(8,128)(2,1)S(1)}, u32[]{:S(2)}, u32[]{:S(2)}) collective-permute-start(bf16[64,2048]{1,0:T(8,128)(2,1)S(1)} %get-tuple-element.87), channel_id=1, source_target_pairs={{0,3},{1,2},{2,1},{3,0},{4,7},{5,6},{6,5},{7,4},{8,11},{9,10},{10,... | collective-permute-start | bytes 786440 | tf_op jit(solution)/shard_map/ppermute | solution.py:529
  59.7 19.3 %copy-start.3 = (bf16[128,2048]{1,0:T(8,128)(2,1)S(1)}, bf16[128,2048]{1,0:T(8,128)(2,1)}, u32[]{:S(2)}) copy-start(bf16[128,2048]{1,0:T(8,128)(2,1)} %refs_4_.1) | copy-start | bytes 1572868
  61.1 11.8 %collective-permute-start.16 = (bf16[128,2048]{1,0:T(8,128)(2,1)S(1)}, bf16[128,2048]{1,0:T(8,128)(2,1)S(1)}, u32[]{:S(2)}, u32[]{:S(2)}) collective-permute-start(bf16[128,2048]{1,0:T(8,128)(2,1)S(1)} %get-tuple-element.99), channel_id=1, source_target_pairs={{0,4},{1,5},{2,6},{3,7},{4,0},{5,1},{6,2},{7,3},{8,12},{9,13},{10,... | collective-permute-start | bytes 1572872 | tf_op jit(solution)/shard_map/ppermute | solution.py:529
  63.4 14.7 %collective-permute-start.12 = (bf16[1,64,2048]{2,1,0:T(8,128)(2,1)S(1)}, bf16[1,64,2048]{2,1,0:T(8,128)(2,1)S(1)}, u32[]{:S(2)}, u32[]{:S(2)}) collective-permute-start(bf16[1,64,2048]{2,1,0:T(8,128)(2,1)S(1)} %get-tuple-element.94), channel_id=1, source_target_pairs={{0,1},{1,0},{2,3},{3,2},{4,5},{5,4},{6,7},{7,6},{8,9},{9,8},{10,11... | collective-permute-start | bytes 786440 | tf_op jit(solution)/shard_map/ppermute | solution.py:529
  64.2 14.8 %collective-permute-start.13 = (bf16[1,64,2048]{2,1,0:T(8,128)(2,1)S(1)}, bf16[1,64,2048]{2,1,0:T(8,128)(2,1)S(1)}, u32[]{:S(2)}, u32[]{:S(2)}) collective-permute-start(bf16[1,64,2048]{2,1,0:T(8,128)(2,1)S(1)} %get-tuple-element.95), channel_id=1, source_target_pairs={{0,2},{1,3},{2,0},{3,1},{4,6},{5,7},{6,4},{7,5},{8,10},{9,11},{10,... | collective-permute-start | bytes 786440 | tf_op jit(solution)/shard_map/ppermute | solution.py:529
  65.4 15.4 %collective-permute-start.14 = (bf16[1,64,2048]{2,1,0:T(8,128)(2,1)S(1)}, bf16[1,64,2048]{2,1,0:T(8,128)(2,1)S(1)}, u32[]{:S(2)}, u32[]{:S(2)}) collective-permute-start(bf16[1,64,2048]{2,1,0:T(8,128)(2,1)S(1)} %get-tuple-element.96), channel_id=1, source_target_pairs={{0,3},{1,2},{2,1},{3,0},{4,7},{5,6},{6,5},{7,4},{8,11},{9,10},{10,... | collective-permute-start | bytes 786440 | tf_op jit(solution)/shard_map/ppermute | solution.py:529
  74.3 16.1 %collective-permute-start.22 = (bf16[2,64,2048]{2,1,0:T(8,128)(2,1)S(1)}, bf16[2,64,2048]{2,1,0:T(8,128)(2,1)S(1)}, u32[]{:S(2)}, u32[]{:S(2)}) collective-permute-start(bf16[2,64,2048]{2,1,0:T(8,128)(2,1)S(1)} %get-tuple-element.105), channel_id=1, source_target_pairs={{0,1},{1,0},{2,3},{3,2},{4,5},{5,4},{6,7},{7,6},{8,9},{9,8},{10,11... | collective-permute-start | bytes 1572872 | tf_op jit(solution)/shard_map/ppermute | solution.py:529
  77.5 26.4 %collective-permute-start.23 = (bf16[2,64,2048]{2,1,0:T(8,128)(2,1)S(1)}, bf16[2,64,2048]{2,1,0:T(8,128)(2,1)S(1)}, u32[]{:S(2)}, u32[]{:S(2)}) collective-permute-start(bf16[2,64,2048]{2,1,0:T(8,128)(2,1)S(1)} %get-tuple-element.106), channel_id=1, source_target_pairs={{0,2},{1,3},{2,0},{3,1},{4,6},{5,7},{6,4},{7,5},{8,10},{9,11},{10,... | collective-permute-start | bytes 1572872 | tf_op jit(solution)/shard_map/ppermute | solution.py:529
  78.1 25.8 %collective-permute-start.24 = (bf16[2,64,2048]{2,1,0:T(8,128)(2,1)S(1)}, bf16[2,64,2048]{2,1,0:T(8,128)(2,1)S(1)}, u32[]{:S(2)}, u32[]{:S(2)}) collective-permute-start(bf16[2,64,2048]{2,1,0:T(8,128)(2,1)S(1)} %get-tuple-element.107), channel_id=1, source_target_pairs={{0,3},{1,2},{2,1},{3,0},{4,7},{5,6},{6,5},{7,4},{8,11},{9,10},{10,... | collective-permute-start | bytes 1572872 | tf_op jit(solution)/shard_map/ppermute | solution.py:529
  79.1 30.8 %collective-permute-start.21 = (bf16[128,2048]{1,0:T(8,128)(2,1)S(1)}, bf16[128,2048]{1,0:T(8,128)(2,1)S(1)}, u32[]{:S(2)}, u32[]{:S(2)}) collective-permute-start(bf16[128,2048]{1,0:T(8,128)(2,1)S(1)} %copy-done.3), channel_id=1, source_target_pairs={{0,4},{1,5},{2,6},{3,7},{4,0},{5,1},{6,2},{7,3},{8,12},{9,13},{10,... | collective-permute-start | bytes 1572872 | tf_op jit(solution)/shard_map/ppermute | solution.py:529
  80.7 32.0 %collective-permute-start.20 = (bf16[144,2048]{1,0:T(8,128)(2,1)S(1)}, bf16[144,2048]{1,0:T(8,128)(2,1)S(1)}, u32[]{:S(2)}, u32[]{:S(2)}) collective-permute-start(bf16[144,2048]{1,0:T(8,128)(2,1)S(1)} %get-tuple-element.73.refs_0_.refs_2_.meta_ref), channel_id=1, source_target_pairs={{0,4},{1,5},{2,6},{3,7},{4,0},{5,1},{6,2},{7,3},{8,12},{9,13},{10,... | collective-permute-start | bytes 1769480 | tf_op jit(solution)/shard_map/ppermute | solution.py:529
  90.3 23.8 %collective-permute-start.17 = (bf16[64,2048]{1,0:T(8,128)(2,1)S(1)}, bf16[64,2048]{1,0:T(8,128)(2,1)S(1)}, u32[]{:S(2)}, u32[]{:S(2)}) collective-permute-start(bf16[64,2048]{1,0:T(8,128)(2,1)S(1)} %get-tuple-element.102), channel_id=1, source_target_pairs={{0,1},{1,0},{2,3},{3,2},{4,5},{5,4},{6,7},{7,6},{8,9},{9,8},{10,11... | collective-permute-start | bytes 786440 | tf_op jit(solution)/shard_map/ppermute | solution.py:529
  103.9 11.6 %collective-permute-start.18 = (bf16[64,2048]{1,0:T(8,128)(2,1)S(1)}, bf16[64,2048]{1,0:T(8,128)(2,1)S(1)}, u32[]{:S(2)}, u32[]{:S(2)}) collective-permute-start(bf16[64,2048]{1,0:T(8,128)(2,1)S(1)} %get-tuple-element.103), channel_id=1, source_target_pairs={{0,2},{1,3},{2,0},{3,1},{4,6},{5,7},{6,4},{7,5},{8,10},{9,11},{10,... | collective-permute-start | bytes 786440 | tf_op jit(solution)/shard_map/ppermute | solution.py:529
  103.9 11.6 %collective-permute-start.19 = (bf16[64,2048]{1,0:T(8,128)(2,1)S(1)}, bf16[64,2048]{1,0:T(8,128)(2,1)S(1)}, u32[]{:S(2)}, u32[]{:S(2)}) collective-permute-start(bf16[64,2048]{1,0:T(8,128)(2,1)S(1)} %get-tuple-element.104), channel_id=1, source_target_pairs={{0,3},{1,2},{2,1},{3,0},{4,7},{5,6},{6,5},{7,4},{8,11},{9,10},{10,... | collective-permute-start | bytes 786440 | tf_op jit(solution)/shard_map/ppermute | solution.py:529
  109.8 10.4 %collective-permute-start.26 = (bf16[64,2048]{1,0:T(8,128)(2,1)S(1)}, bf16[64,2048]{1,0:T(8,128)(2,1)S(1)}, u32[]{:S(2)}, u32[]{:S(2)}) collective-permute-start(bf16[64,2048]{1,0:T(8,128)(2,1)S(1)} %get-tuple-element.110), channel_id=1, source_target_pairs={{0,1},{1,0},{2,3},{3,2},{4,5},{5,4},{6,7},{7,6},{8,9},{9,8},{10,11... | collective-permute-start | bytes 786440 | tf_op jit(solution)/shard_map/ppermute | solution.py:529
  112.7 9.2 %collective-permute-start.27 = (bf16[64,2048]{1,0:T(8,128)(2,1)S(1)}, bf16[64,2048]{1,0:T(8,128)(2,1)S(1)}, u32[]{:S(2)}, u32[]{:S(2)}) collective-permute-start(bf16[64,2048]{1,0:T(8,128)(2,1)S(1)} %get-tuple-element.111), channel_id=1, source_target_pairs={{0,2},{1,3},{2,0},{3,1},{4,6},{5,7},{6,4},{7,5},{8,10},{9,11},{10,... | collective-permute-start | bytes 786440 | tf_op jit(solution)/shard_map/ppermute | solution.py:529
  114.1 31.8 %collective-permute-start.30 = (bf16[2,64,2048]{2,1,0:T(8,128)(2,1)S(1)}, bf16[2,64,2048]{2,1,0:T(8,128)(2,1)S(1)}, u32[]{:S(2)}, u32[]{:S(2)}) collective-permute-start(bf16[2,64,2048]{2,1,0:T(8,128)(2,1)S(1)} %get-tuple-element.113), channel_id=1, source_target_pairs={{0,1},{1,0},{2,3},{3,2},{4,5},{5,4},{6,7},{7,6},{8,9},{9,8},{10,11... | collective-permute-start | bytes 1572872 | tf_op jit(solution)/shard_map/ppermute | solution.py:529
  116.5 29.3 %collective-permute-start.25 = (bf16[128,2048]{1,0:T(8,128)(2,1)S(1)}, bf16[128,2048]{1,0:T(8,128)(2,1)S(1)}, u32[]{:S(2)}, u32[]{:S(2)}) collective-permute-start(bf16[128,2048]{1,0:T(8,128)(2,1)S(1)} %expand.5.refs_4_), channel_id=1, source_target_pairs={{0,8},{1,9},{2,10},{3,11},{4,12},{5,13},{6,14},{7,15},{8,0},{9,1},... | collective-permute-start | bytes 1572872 | tf_op jit(solution)/shard_map/ppermute | solution.py:529
  116.6 30.2 %collective-permute-start.31 = (bf16[2,64,2048]{2,1,0:T(8,128)(2,1)S(1)}, bf16[2,64,2048]{2,1,0:T(8,128)(2,1)S(1)}, u32[]{:S(2)}, u32[]{:S(2)}) collective-permute-start(bf16[2,64,2048]{2,1,0:T(8,128)(2,1)S(1)} %get-tuple-element.114), channel_id=1, source_target_pairs={{0,2},{1,3},{2,0},{3,1},{4,6},{5,7},{6,4},{7,5},{8,10},{9,11},{10,... | collective-permute-start | bytes 1572872 | tf_op jit(solution)/shard_map/ppermute | solution.py:529
  120.2 26.6 %collective-permute-start.32 = (bf16[2,64,2048]{2,1,0:T(8,128)(2,1)S(1)}, bf16[2,64,2048]{2,1,0:T(8,128)(2,1)S(1)}, u32[]{:S(2)}, u32[]{:S(2)}) collective-permute-start(bf16[2,64,2048]{2,1,0:T(8,128)(2,1)S(1)} %get-tuple-element.115), channel_id=1, source_target_pairs={{0,3},{1,2},{2,1},{3,0},{4,7},{5,6},{6,5},{7,4},{8,11},{9,10},{10,... | collective-permute-start | bytes 1572872 | tf_op jit(solution)/shard_map/ppermute | solution.py:529
  122.0 22.0 %collective-permute-start.28 = (bf16[64,2048]{1,0:T(8,128)(2,1)S(1)}, bf16[64,2048]{1,0:T(8,128)(2,1)S(1)}, u32[]{:S(2)}, u32[]{:S(2)}) collective-permute-start(bf16[64,2048]{1,0:T(8,128)(2,1)S(1)} %get-tuple-element.112), channel_id=1, source_target_pairs={{0,3},{1,2},{2,1},{3,0},{4,7},{5,6},{6,5},{7,4},{8,11},{9,10},{10,... | collective-permute-start | bytes 786440 | tf_op jit(solution)/shard_map/ppermute | solution.py:529
  145.8 31.0 %collective-permute-start.29 = (bf16[128,2048]{1,0:T(8,128)(2,1)}, bf16[128,2048]{1,0:T(8,128)(2,1)}, u32[]{:S(2)}, u32[]{:S(2)}) collective-permute-start(bf16[128,2048]{1,0:T(8,128)(2,1)} %expand.6.refs_1_), channel_id=1, source_target_pairs={{0,12},{1,13},{2,14},{3,15},{4,8},{5,9},{6,10},{7,11},{8,4},{9,5},... | collective-permute-start | bytes 1572872 | tf_op jit(solution)/shard_map/ppermute | solution.py:529
  145.9 6.4 %copy-start = (f32[128,2048]{1,0:T(8,128)}, f32[128,2048]{1,0:T(8,128)S(1)}, u32[]{:S(2)}) copy-start(f32[128,2048]{1,0:T(8,128)S(1)} %total.2.refs_8_.own_ref) | copy-start | bytes 3145732
  152.3 11.5 %collective-permute-start.33 = (bf16[64,2048]{1,0:T(8,128)(2,1)S(1)}, bf16[64,2048]{1,0:T(8,128)(2,1)S(1)}, u32[]{:S(2)}, u32[]{:S(2)}) collective-permute-start(bf16[64,2048]{1,0:T(8,128)(2,1)S(1)} %get-tuple-element.117), channel_id=1, source_target_pairs={{0,1},{1,0},{2,3},{3,2},{4,5},{5,4},{6,7},{7,6},{8,9},{9,8},{10,11... | collective-permute-start | bytes 786440 | tf_op jit(solution)/shard_map/ppermute | solution.py:529
  153.3 10.5 %collective-permute-start.34 = (bf16[64,2048]{1,0:T(8,128)(2,1)S(1)}, bf16[64,2048]{1,0:T(8,128)(2,1)S(1)}, u32[]{:S(2)}, u32[]{:S(2)}) collective-permute-start(bf16[64,2048]{1,0:T(8,128)(2,1)S(1)} %get-tuple-element.118), channel_id=1, source_target_pairs={{0,2},{1,3},{2,0},{3,1},{4,6},{5,7},{6,4},{7,5},{8,10},{9,11},{10,... | collective-permute-start | bytes 786440 | tf_op jit(solution)/shard_map/ppermute | solution.py:529
  155.2 8.5 %collective-permute-start.35 = (bf16[64,2048]{1,0:T(8,128)(2,1)S(1)}, bf16[64,2048]{1,0:T(8,128)(2,1)S(1)}, u32[]{:S(2)}, u32[]{:S(2)}) collective-permute-start(bf16[64,2048]{1,0:T(8,128)(2,1)S(1)} %get-tuple-element.119), channel_id=1, source_target_pairs={{0,3},{1,2},{2,1},{3,0},{4,7},{5,6},{6,5},{7,4},{8,11},{9,10},{10,... | collective-permute-start | bytes 786440 | tf_op jit(solution)/shard_map/ppermute | solution.py:529
  163.7 9.3 %collective-permute-start.37 = (bf16[1024,2304]{1,0:T(8,128)(2,1)S(1)}, bf16[1024,2304]{1,0:T(8,128)(2,1)S(1)}, u32[]{:S(2)}, u32[]{:S(2)}) collective-permute-start(bf16[1024,2304]{1,0:T(8,128)(2,1)S(1)} %lend.1.refs_4_), channel_id=1, source_target_pairs={{0,16},{16,0},{1,17},{17,1},{2,18},{18,2},{3,19},{19,3},{4,20},{20... | collective-permute-start | bytes 14155784 | tf_op jit(solution)/shard_map/ppermute | solution.py:616
  164.8 15.0 %collective-permute-start.36 = (bf16[128,2048]{1,0:T(8,128)(2,1)S(1)}, bf16[128,2048]{1,0:T(8,128)(2,1)S(1)}, u32[]{:S(2)}, u32[]{:S(2)}) collective-permute-start(bf16[128,2048]{1,0:T(8,128)(2,1)S(1)} %expand.7.refs_16_), channel_id=1, source_target_pairs={{0,4},{1,5},{2,6},{3,7},{4,0},{5,1},{6,2},{7,3},{8,12},{9,13},{10,... | collective-permute-start | bytes 1572872 | tf_op jit(solution)/shard_map/ppermute | solution.py:529
  173.0 6.8 %copy-start.1 = (f32[128,2048]{1,0:T(8,128)S(1)}, f32[128,2048]{1,0:T(8,128)}, u32[]{:S(2)}) copy-start(f32[128,2048]{1,0:T(8,128)} %copy-done) | copy-start | bytes 3145732
